TPU v7x, 32 devices: a whole 2x2x4 slice. The times are simulated.
32 devices in a mesh: blk: 8 (over z, y), gz: 4 (over x, core).
Axes of the slice: x: 2, y: 2, z: 4, core: 2. Of those that a mesh axis runs over, the one named last changes fastest.
Arguments:
- adjoint: float32 [4, 64, 19, 16, 256], P('gz', 'blk'), may hold values from -6 to 6
- velocity: float32 [4, 64, 3, 16, 256], P('gz', 'blk'), may hold values from -0.32 to 0.32
- porosity: float32 [4, 64, 16, 256], P('gz', 'blk'), may hold values from 0 to 1
- block_x: int32 [4, 64], P('gz'), may hold values from 0 to 7, as said below
- neighbours: int32 [4, 64, 6], P('gz'), may hold values from -1 to 63, as said below
- owner_map: int32 [8], replicated, may hold values from 1 to 24, 64 in all
Outputs:
- adjoint_out: float32 [4, 64, 19, 16, 256], P('gz', 'blk')
- smoothed: float32 [4, 8, 48, 16, 128], P('gz', 'blk')
Inputs may be any that keep to these rules, and one draw needn't show every extreme that they name: `block_x`: in every layer, block row k holds 8 blocks, one on each device of blk at that device's slot k (slot = device * 8 + k); the columns of one row of one layer are all different. `neighbours`: the entries name the blocks beside a slot in the same row (-x, +x), in the rows k - 1 and k + 1 (-y, +y) and at the same row and column in the layer below and above (-z, +z), as slots of that layer; -1 beyond the window's faces. Design slab j of every layer holds the 2 * owner_map[j] cell rows after those of slabs 0 to j - 1; the entries sum to 64.
All inputs are finite; a program needn't handle non-finite values.
Results may differ from a plain program's by a relative error of at most 0.0001.
Values sent between devices are 32-bit elements; how exact they have to be, the bound alone decides.
No kernel may reach another device: no remote copies, remote signals or barrier semaphores. Data moves between devices by JAX's collectives and lax.ppermute only.
A program may use at most 128 MiB of HBM per device.

v0:
```python
import jax
import jax.numpy as jnp
import numpy as np
from jax import lax
from jax.sharding import PartitionSpec as P

STEPS = 2


VELOCITIES = np.array(
    [
        [0, 0, 0],
        [1, 0, 0],
        [-1, 0, 0],
        [0, 1, 0],
        [0, -1, 0],
        [0, 0, 1],
        [0, 0, -1],
        [1, 1, 0],
        [-1, -1, 0],
        [1, -1, 0],
        [-1, 1, 0],
        [1, 0, 1],
        [-1, 0, -1],
        [1, 0, -1],
        [-1, 0, 1],
        [0, 1, 1],
        [0, -1, -1],
        [0, 1, -1],
        [0, -1, 1],
    ],
    dtype=np.float32,
)
WEIGHTS = np.array([1.0 / 3.0] + [1.0 / 18.0] * 6 + [1.0 / 36.0] * 12, dtype=np.float32)
EAST_POPS = [1, 7, 9, 11, 13]
WEST_POPS = [2, 8, 10, 12, 14]
NORTH_POPS = [3, 7, 10, 15, 17]
SOUTH_POPS = [4, 8, 9, 16, 18]
UPPER_POPS = [5, 11, 14, 15, 18]
LOWER_POPS = [6, 12, 13, 16, 17]
RELAX_RATE = 1.25
DRAG_RATE = 0.3
FILTER_TAPS = [1.0 / 3.0, 2.0 / 3.0, 1.0, 2.0 / 3.0, 1.0 / 3.0]


def padded_2(block, sides, width):
    for axis, dim in sides:
        count = lax.axis_size(axis)
        forward = [(i, i + 1) for i in range(count - 1)]
        backward = [(target, source) for source, target in forward]
        low = lax.ppermute(
            lax.slice_in_dim(block, block.shape[dim] - width, None, axis=dim), axis, forward
        )
        high = lax.ppermute(lax.slice_in_dim(block, 0, width, axis=dim), axis, backward)
        block = jnp.concatenate([low, block, high], axis=dim)
    return block


def pop_table(values, rank_count, pop_axis):
    shape = [1] * rank_count
    shape[pop_axis] = values.shape[0]
    return jnp.asarray(values).reshape(shape)


def collide(state, velocity, porosity, pop_axis):
    rank_count = state.ndim
    components = [lax.index_in_dim(velocity, c, pop_axis, keepdims=True) for c in range(3)]
    lattice = [pop_table(VELOCITIES[:, c], rank_count, pop_axis) for c in range(3)]
    weights = pop_table(WEIGHTS, rank_count, pop_axis)
    speed_sq = (
        components[0] * components[0]
        + components[1] * components[1]
        + components[2] * components[2]
    )
    along = lattice[0] * components[0] + lattice[1] * components[1] + lattice[2] * components[2]
    weighted = weights * state
    scalar = jnp.sum(
        weighted * (1.0 + 3.0 * along + 4.5 * along * along - 1.5 * speed_sq),
        axis=pop_axis,
        keepdims=True,
    )
    weight_total = jnp.sum(weighted, axis=pop_axis, keepdims=True)
    grown = weighted * (3.0 + 9.0 * along)
    vector_part = [
        jnp.sum(grown * lattice[c], axis=pop_axis, keepdims=True)
        - 3.0 * components[c] * weight_total
        for c in range(3)
    ]
    momentum = [jnp.sum(lattice[c] * state, axis=pop_axis, keepdims=True) for c in range(3)]
    sens_step = (
        components[0] * momentum[0] + components[1] * momentum[1] + components[2] * momentum[2]
    )
    relative = [lattice[c] - components[c] for c in range(3)]
    project_vector = (
        relative[0] * vector_part[0] + relative[1] * vector_part[1] + relative[2] * vector_part[2]
    )
    project_momentum = (
        relative[0] * momentum[0] + relative[1] * momentum[1] + relative[2] * momentum[2]
    )
    collided = (
        (1.0 - RELAX_RATE) * state
        + RELAX_RATE * (scalar + project_vector)
        - DRAG_RATE * porosity * project_momentum
    )
    return (collided, sens_step)


def smooth_slices(padded, axis_pos, length):
    result = FILTER_TAPS[0] * lax.slice_in_dim(padded, 0, length, axis=axis_pos)
    for offset in range(1, 5):
        result = result + FILTER_TAPS[offset] * lax.slice_in_dim(
            padded, offset, offset + length, axis=axis_pos
        )
    return result


def pick_rows(source, slot_index):
    found_rows = jnp.take(source, jnp.maximum(slot_index, 0), axis=0)
    present = (slot_index >= 0).reshape(slot_index.shape + (1,) * (source.ndim - 1))
    return jnp.where(present, found_rows, jnp.zeros_like(found_rows))


def section_x(collided, gathered, own_table, column_pos, edge):
    blocks = collided.shape[0]
    from_east = pick_rows(gathered[:, 0], own_table[:, 1]).reshape(blocks, 5, edge, edge)
    from_west = pick_rows(gathered[:, 1], own_table[:, 0]).reshape(blocks, 5, edge, edge)
    east_group = jnp.where(
        column_pos == edge - 1,
        jnp.repeat(from_east, edge, axis=-1),
        jnp.roll(collided[:, EAST_POPS], -1, axis=-1),
    )
    west_group = jnp.where(
        column_pos == 0,
        jnp.repeat(from_west, edge, axis=-1),
        jnp.roll(collided[:, WEST_POPS], 1, axis=-1),
    )
    return collided.at[:, EAST_POPS].set(east_group).at[:, WEST_POPS].set(west_group)


def section_y(moved, north_in, south_in, row_pos, edge):
    north_group = jnp.where(
        row_pos == edge - 1,
        jnp.tile(north_in, (1, 1, 1, edge)),
        jnp.roll(moved[:, NORTH_POPS], -edge, axis=-1),
    )
    south_group = jnp.where(
        row_pos == 0,
        jnp.tile(south_in, (1, 1, 1, edge)),
        jnp.roll(moved[:, SOUTH_POPS], edge, axis=-1),
    )
    return moved.at[:, NORTH_POPS].set(north_group).at[:, SOUTH_POPS].set(south_group)


def section_z(moved, from_above, from_below, depth_pos, edge):
    upper_group = jnp.where(
        depth_pos == edge - 1, from_above[:, :, None, :], jnp.roll(moved[:, UPPER_POPS], -1, axis=2)
    )
    lower_group = jnp.where(
        depth_pos == 0, from_below[:, :, None, :], jnp.roll(moved[:, LOWER_POPS], 1, axis=2)
    )
    return moved.at[:, UPPER_POPS].set(upper_group).at[:, LOWER_POPS].set(lower_group)


def local(adjoint, velocity, porosity, block_x, neighbours, owner_map):
    blocks = adjoint.shape[1]
    edge = adjoint.shape[3]
    plane = adjoint.shape[4]
    devices = lax.axis_size("blk")
    my_index = lax.axis_index("blk")
    adjoint_state = adjoint[0]
    flow = velocity[0]
    design = porosity[0][:, None]
    table_all = neighbours[0]
    own_table = lax.dynamic_slice_in_dim(table_all, my_index * blocks, blocks, 0)
    column_pos = lax.broadcasted_iota(jnp.int32, (1, 1, 1, plane), 3) % edge
    row_pos = lax.broadcasted_iota(jnp.int32, (1, 1, 1, plane), 3) // edge
    depth_pos = lax.broadcasted_iota(jnp.int32, (1, 1, edge, 1), 2)
    sens_total = jnp.zeros((blocks, edge, plane), jnp.float32)
    for iteration in range(STEPS):
        collided, sens_step = collide(adjoint_state, flow, design, 1)
        sens_total = sens_total + sens_step[:, 0]
        east_group = collided[:, EAST_POPS]
        west_group = collided[:, WEST_POPS]
        x_out = jnp.stack(
            [
                east_group[..., 0::edge].reshape(blocks, 5, edge * edge),
                west_group[..., edge - 1 :: edge].reshape(blocks, 5, edge * edge),
            ],
            axis=1,
        )
        x_all = lax.all_gather(x_out, "blk", axis=0, tiled=True)
        moved = section_x(collided, x_all, own_table, column_pos, edge)
        north_group = moved[:, NORTH_POPS]
        south_group = moved[:, SOUTH_POPS]
        y_after = jnp.stack(
            [
                north_group[..., :edge].reshape(blocks, 5, edge * edge),
                south_group[..., plane - edge :].reshape(blocks, 5, edge * edge),
            ],
            axis=1,
        )
        y_all = lax.all_gather(y_after, "blk", axis=0, tiled=True)
        north_in = pick_rows(y_all[:, 0], own_table[:, 3]).reshape(blocks, 5, edge, edge)
        south_in = pick_rows(y_all[:, 1], own_table[:, 2]).reshape(blocks, 5, edge, edge)
        moved = section_y(moved, north_in, south_in, row_pos, edge)
        upper_group = moved[:, UPPER_POPS]
        lower_group = moved[:, LOWER_POPS]
        z_out = jnp.stack([upper_group[:, :, 0], lower_group[:, :, edge - 1]], axis=1)
        layer_ends = padded_2(z_out, (("gz", 1),), 1)
        below_all, above_all = (
            lax.all_gather(layer_ends[:, 0], "blk", axis=0, tiled=True),
            lax.all_gather(layer_ends[:, 3], "blk", axis=0, tiled=True),
        )
        adjoint_state = section_z(
            moved,
            pick_rows(above_all, own_table[:, 5]),
            pick_rows(below_all, own_table[:, 4]),
            depth_pos,
            edge,
        )
    units = blocks * edge // 2
    rows_cap = 2 * (3 * units // devices)
    lead = 0
    span = rows_cap + 2 * lead
    height = blocks * edge
    band_rows = 2 * owner_map
    band_start = jnp.cumsum(band_rows) - band_rows
    offsets = jnp.arange(span, dtype=jnp.int32)
    wanted = band_start[:, None] - lead + offsets[None, :]
    present = (offsets[None, :] < band_rows[:, None] + 2 * lead) & (wanted >= 0) & (wanted < height)
    row_major = (
        sens_total.reshape(blocks, edge, edge, edge)
        .transpose(0, 2, 1, 3)
        .reshape(height, edge * edge)
    )
    outgoing = jnp.take(row_major, jnp.clip(wanted, 0, height - 1), axis=0)
    outgoing = jnp.where(present[..., None], outgoing, jnp.zeros_like(outgoing))
    incoming = lax.all_to_all(outgoing, "blk", split_axis=0, concat_axis=0, tiled=True)
    own_start = band_start[my_index]
    own_rows = band_rows[my_index]
    local_rows = own_start - lead + offsets
    block_row = jnp.clip(local_rows, 0, height - 1) // edge
    columns = block_x[0].reshape(devices, blocks)
    hits = columns[:, :, None] == jnp.arange(devices, dtype=jnp.int32)[None, None, :]
    holder = jnp.sum(
        jnp.where(hits, jnp.arange(devices, dtype=jnp.int32)[:, None, None], 0), axis=0
    )
    sender = jnp.take(holder, block_row, axis=0)
    arranged = jnp.take_along_axis(jnp.transpose(incoming, (1, 0, 2)), sender[:, :, None], axis=1)
    field = (
        arranged.reshape(span, devices, edge, edge)
        .transpose(0, 2, 1, 3)
        .reshape(span, edge, devices * edge)
    )
    rim_rows = jnp.concatenate(
        [field[:2], lax.dynamic_slice_in_dim(field, own_rows - 2, 2, 0)], axis=0
    )
    beside = padded_2(rim_rows, (("blk", 0),), 2)
    padded_rows = jnp.concatenate([beside[:2], field, jnp.zeros_like(field[:2])], axis=0)
    padded_rows = lax.dynamic_update_slice_in_dim(padded_rows, beside[6:], own_rows + 2, 0)
    along_rows = smooth_slices(padded_rows, 0, rows_cap)
    widened = jnp.pad(along_rows, ((0, 0), (0, 0), (2, 2)))
    along_cols = smooth_slices(widened, 2, devices * edge)
    deepened = padded_2(along_cols, (("gz", 1),), 2)
    along_depth = smooth_slices(deepened, 1, edge)
    keep_rows = jnp.arange(rows_cap, dtype=jnp.int32) < own_rows
    smoothed = jnp.where(keep_rows[:, None, None], along_depth, jnp.zeros_like(along_depth))
    return (adjoint_state[None], smoothed[None, None])


def solution(mesh):
    placed = (
        P("gz", "blk", None, None, None),
        P("gz", "blk", None, None, None),
        P("gz", "blk", None, None),
        P("gz", None),
        P("gz", None, None),
        P(),
    )
    return jax.shard_map(
        local,
        mesh=mesh,
        in_specs=placed,
        out_specs=(P("gz", "blk", None, None, None), P("gz", "blk", None, None, None)),
        check_vma=False,
    )
```

profile of v0, /device:TPU:1, one launch (start us, length us, event | category | flops | bytes accessed | tf_op | source)
XLA Modules:
  0.0 613.6 jit_solution(14853633623648210313)
XLA Ops:
  8.6 5.1 multiply_reduce_fusion.9
  14.5 2.3 fusion.7
  18.3 2.9 slice.241
  22.7 4.4 slice.240
  28.8 2.2 slice.364
  38.8 28.4 %all_gather.24 = f32[64,2,5,256]{3,2,0,1:T(8,128)S(1)} all-gather(f32[8,2,5,256]{3,2,0,1:T(8,128)S(1)} %pad_maximum_fusion.2), channel_id=1, replica_groups=mesh['blk'=8,'gz'=4] {'blk'}, dimensions={0}, use_global_device_ids=true | all-gather | bytes 737280 | tf_op jit(solution)/shard_map/all_gather | solution.py:191
  68.2 2.2 gather_fusion.16
  72.0 2.2 gather_fusion.15
  79.1 4.0 broadcast_in_dim.415
  83.1 5.0 reshape.493
  88.1 4.0 broadcast_in_dim.410
  92.1 5.0 reshape.491
  97.2 2.4 fusion.26
  101.4 2.3 fusion.27
  117.4 29.2 %all_gather.25 = f32[64,2,5,256]{3,2,0,1:T(8,128)S(1)} all-gather(f32[8,2,5,256]{3,2,0,1:T(8,128)S(1)} %pad_maximum_fusion.3), channel_id=1, replica_groups=mesh['blk'=8,'gz'=4] {'blk'}, dimensions={0}, use_global_device_ids=true | all-gather | bytes 737280 | tf_op jit(solution)/shard_map/all_gather | solution.py:202
  147.7 2.2 gather_fusion.18
  151.4 2.2 gather_fusion.17
  158.5 3.7 tile.44
  162.2 5.0 tile.45
  167.2 3.7 tile.41
  170.9 5.0 tile.42
  175.9 2.4 fusion.28
  180.2 2.3 fusion.29
  185.7 13.6 %collective-permute-start.1 = (f32[8,1,5,256]{3,0,2,1:T(8,128)}, f32[8,1,5,256]{3,0,2,1:T(8,128)}, u32[]{:S(2)}, u32[]{:S(2)}) collective-permute-start(f32[8,1,5,256]{3,0,2,1:T(8,128)} %bitcast.301), channel_id=1, source_target_pairs={{0,1},{1,2},{2,3},{4,5},{5,6},{6,7},{8,9},{9,10},{10,11},{12,13},{... | collective-permute-start | bytes 122888 | tf_op jit(solution)/shard_map/ppermute | solution.py:51
  228.9 24.8 %all-gather.1 = f32[64,1,5,256]{3,0,2,1:T(8,128)S(1)} all-gather(f32[8,1,5,256]{3,0,2,1:T(8,128)} %collective-permute-done.1), channel_id=3, replica_groups=mesh['blk'=8,'gz'=4] {'blk'}, dimensions={0}, use_global_device_ids=true | all-gather | bytes 368640 | tf_op jit(solution)/shard_map/all_gather | solution.py:211
  254.6 2.3 gather_fusion.20
  258.6 25.5 %all-gather = f32[64,1,5,256]{3,0,2,1:T(8,128)S(1)} all-gather(f32[8,1,5,256]{3,0,2,1:T(8,128)} %collective-permute-done), channel_id=2, replica_groups=mesh['blk'=8,'gz'=4] {'blk'}, dimensions={0}, use_global_device_ids=true | all-gather | bytes 368640 | tf_op jit(solution)/shard_map/all_gather | solution.py:212
  285.1 2.3 gather_fusion.19
  290.2 2.1 scatter_fusion.4
  296.5 4.4 multiply_reduce_fusion.5
  301.8 3.8 fusion.16
  305.5 2.6 gather_fusion.7
  308.3 3.0 slice.268
  312.8 4.4 slice.267
  318.9 2.2 slice.380
  326.1 28.2 %all_gather.28 = f32[64,2,5,256]{3,2,0,1:T(8,128)S(1)} all-gather(f32[8,2,5,256]{3,2,0,1:T(8,128)S(1)} %pad_maximum_fusion.4), channel_id=1, replica_groups=mesh['blk'=8,'gz'=4] {'blk'}, dimensions={0}, use_global_device_ids=true | all-gather | bytes 737280 | tf_op jit(solution)/shard_map/all_gather | solution.py:191
  363.5 4.0 broadcast_in_dim.449
  367.5 5.0 reshape.497
  372.5 4.0 broadcast_in_dim.446
  376.4 5.0 reshape.495
  381.5 2.4 fusion.32
  385.7 2.2 fusion.33
  399.6 26.1 %all_gather.29 = f32[64,2,5,256]{3,2,0,1:T(8,128)S(1)} all-gather(f32[8,2,5,256]{3,2,0,1:T(8,128)S(1)} %pad_maximum_fusion.5), channel_id=1, replica_groups=mesh['blk'=8,'gz'=4] {'blk'}, dimensions={0}, use_global_device_ids=true | all-gather | bytes 737280 | tf_op jit(solution)/shard_map/all_gather | solution.py:202
  430.8 2.7 tile.50
  433.5 5.0 tile.51
  438.5 2.7 tile.47
  441.2 5.0 tile.48
  446.2 2.5 fusion.34
  450.6 2.3 fusion.35
  456.8 26.6 %collective-permute-start.3 = (f32[8,1,5,256]{3,0,2,1:T(8,128)}, f32[8,1,5,256]{3,0,2,1:T(8,128)}, u32[]{:S(2)}, u32[]{:S(2)}) collective-permute-start(f32[8,1,5,256]{3,0,2,1:T(8,128)} %bitcast.299), channel_id=1, source_target_pairs={{0,1},{1,2},{2,3},{4,5},{5,6},{6,7},{8,9},{9,10},{10,11},{12,13},{... | collective-permute-start | bytes 122888 | tf_op jit(solution)/shard_map/ppermute | solution.py:51
  483.4 2.2 gather_fusion.13
  490.0 5.8 all-to-all-start
  499.1 25.5 %all-gather.3 = f32[64,1,5,256]{3,0,2,1:T(8,128)S(1)} all-gather(f32[8,1,5,256]{3,0,2,1:T(8,128)} %collective-permute-done.3), channel_id=5, replica_groups=mesh['blk'=8,'gz'=4] {'blk'}, dimensions={0}, use_global_device_ids=true | all-gather | bytes 368640 | tf_op jit(solution)/shard_map/all_gather | solution.py:211
  525.6 2.3 gather_fusion.26
  529.5 25.2 %all-gather.2 = f32[64,1,5,256]{3,0,2,1:T(8,128)S(1)} all-gather(f32[8,1,5,256]{3,0,2,1:T(8,128)} %collective-permute-done.2), channel_id=4, replica_groups=mesh['blk'=8,'gz'=4] {'blk'}, dimensions={0}, use_global_device_ids=true | all-gather | bytes 368640 | tf_op jit(solution)/shard_map/all_gather | solution.py:212
  555.7 2.3 gather_fusion.25
  560.1 2.6 gather_fusion.14
  562.7 2.7 gather.119
  565.4 3.3 select_bitcast_fusion
  568.8 3.7 copy.174
  572.5 2.6 constant_dynamic-slice_fusion
  576.7 3.3 collective-permute-start.4
  580.1 2.3 copy.176
  588.5 16.6 %collective-permute-start.6 = (f32[48,2,128]{2,1,0:T(2,128)}, f32[48,2,128]{2,1,0:T(2,128)S(1)}, u32[]{:S(2)}, u32[]{:S(2)}) collective-permute-start(f32[48,2,128]{2,1,0:T(2,128)} %get-tuple-element.59), channel_id=1, source_target_pairs={{0,1},{1,2},{2,3},{4,5},{5,6},{6,7},{8,9},{9,10},{10,11},{12,13},{... | collective-permute-start | bytes 147464 | tf_op jit(solution)/shard_map/ppermute | solution.py:51
  (375 shorter events, 165.6 us)
Async XLA Ops:
  2.8 71.4 %copy-start.57 = (pred[8]{0:T(512)(128)(4,1)}, pred[8]{0:T(512)(128)(4,1)S(1)}, u32[]{:S(2)}) copy-start(pred[8]{0:T(512)(128)(4,1)S(1)} %get-tuple-element.28) | copy-start | bytes 28
  6.4 10.4 %copy-start.46 = (s32[1024]{0:T(1024)}, s32[1024]{0:T(1024)S(1)}, u32[]{:S(2)}) copy-start(s32[1024]{0:T(1024)S(1)} %pad_clamp_fusion.12) | copy-start | bytes 12292
  7.3 6.5 %copy-start.30 = (f32[8,16,256]{2,1,0:T(8,128)}, f32[8,16,256]{2,1,0:T(8,128)S(1)}, u32[]{:S(2)}) copy-start(f32[8,16,256]{2,1,0:T(8,128)S(1)} %multiply_bitcast_fusion) | copy-start | bytes 393220
  7.3 6.4 %copy-start.6 = (f32[1,8,3,16,256]{4,3,2,1,0:T(8,128)S(1)}, f32[1,8,3,16,256]{4,3,2,1,0:T(8,128)}, u32[]{:S(2)}) copy-start(f32[1,8,3,16,256]{4,3,2,1,0:T(8,128)} %param.52) | copy-start | bytes 1179652
  8.5 5.9 copy-start.4
  8.6 5.9 copy-start.37
  8.6 5.9 copy-start.39
  8.6 5.9 copy-start.41
  17.4 13.5 %copy-start.88 = (s32[8]{0:T(128)S(1)}, s32[8]{0:T(128)}, u32[]{:S(2)}) copy-start(s32[8]{0:T(128)} %get-tuple-element.72) | copy-start | bytes 100
  21.2 9.7 %copy-start.51 = (s32[1024]{0:T(1024)}, s32[1024]{0:T(1024)S(1)}, u32[]{:S(2)}) copy-start(s32[1024]{0:T(1024)S(1)} %pad_clamp_fusion.13) | copy-start | bytes 12292
  30.9 43.3 %copy-start.50 = (s32[1024]{0:T(1024)}, s32[1024]{0:T(1024)S(1)}, u32[]{:S(2)}) copy-start(s32[1024]{0:T(1024)S(1)} %pad_clamp_fusion.10) | copy-start | bytes 12292
  31.6 42.7 %copy-start.48 = (s32[1024]{0:T(1024)}, s32[1024]{0:T(1024)S(1)}, u32[]{:S(2)}) copy-start(s32[1024]{0:T(1024)S(1)} %pad_clamp_fusion.11) | copy-start | bytes 12292
  32.2 73.3 %copy-start.44 = (s32[1024]{0:T(1024)}, s32[1024]{0:T(1024)S(1)}, u32[]{:S(2)}) copy-start(s32[1024]{0:T(1024)S(1)} %pad_clamp_fusion.9) | copy-start | bytes 12292
  92.1 7.4 %copy-start.68 = (s32[5]{0:T(128)S(1)}, s32[5]{0:T(128)}, u32[]{:S(2)}) copy-start(s32[5]{0:T(128)} %constant.230) | copy-start | bytes 64
  108.0 39.6 %copy-start.47 = (s32[1024]{0:T(1024)}, s32[1024]{0:T(1024)S(1)}, u32[]{:S(2)}) copy-start(s32[1024]{0:T(1024)S(1)} %pad_clamp_fusion.6) | copy-start | bytes 12292
  108.1 43.4 %copy-start.45 = (s32[1024]{0:T(1024)}, s32[1024]{0:T(1024)S(1)}, u32[]{:S(2)}) copy-start(s32[1024]{0:T(1024)S(1)} %pad_clamp_fusion.7) | copy-start | bytes 12292
  108.7 38.9 %copy-start.52 = (s32[1024]{0:T(1024)}, s32[1024]{0:T(1024)S(1)}, u32[]{:S(2)}) copy-start(s32[1024]{0:T(1024)S(1)} %pad_clamp_fusion.8) | copy-start | bytes 12292
  109.4 74.9 %copy-start.43 = (s32[1024]{0:T(1024)}, s32[1024]{0:T(1024)S(1)}, u32[]{:S(2)}) copy-start(s32[1024]{0:T(1024)S(1)} %pad_clamp_fusion.3) | copy-start | bytes 12292
  170.9 7.4 %copy-start.63 = (s32[5]{0:T(128)S(1)}, s32[5]{0:T(128)}, u32[]{:S(2)}) copy-start(s32[5]{0:T(128)} %constant.234) | copy-start | bytes 64
  180.2 19.1 %copy-start.59 = (s32[5]{0:T(128)S(1)}, s32[5]{0:T(128)}, u32[]{:S(2)}) copy-start(s32[5]{0:T(128)} %constant.238) | copy-start | bytes 64
  182.5 29.4 %copy-start.84 = (s32[8]{0:T(128)S(1)}, s32[8]{0:T(128)}, u32[]{:S(2)}) copy-start(s32[8]{0:T(128)} %get-tuple-element.29) | copy-start | bytes 100
  184.3 28.0 %copy-start.85 = (s32[8]{0:T(128)S(1)}, s32[8]{0:T(128)}, u32[]{:S(2)}) copy-start(s32[8]{0:T(128)} %get-tuple-element.34) | copy-start | bytes 100
  184.9 14.3 %copy-start.15 = (f32[5,8,16,256]{3,2,1,0:T(8,128)}, f32[5,8,16,256]{3,2,1,0:T(8,128)S(1)}, u32[]{:S(2)}) copy-start(f32[5,8,16,256]{3,2,1,0:T(8,128)S(1)} %gather_fusion.5) | copy-start | bytes 1966084
  185.0 14.3 %copy-start.32 = (f32[8,5,1,256]{3,2,0,1:T(1,128)}, f32[8,5,1,256]{3,2,0,1:T(1,128)S(1)}, u32[]{:S(2)}) copy-start(f32[8,5,1,256]{3,2,0,1:T(1,128)S(1)} %slice.377) | copy-start | bytes 122884
  185.7 43.2 %collective-permute-start.1 = (f32[8,1,5,256]{3,0,2,1:T(8,128)}, f32[8,1,5,256]{3,0,2,1:T(8,128)}, u32[]{:S(2)}, u32[]{:S(2)}) collective-permute-start(f32[8,1,5,256]{3,0,2,1:T(8,128)} %bitcast.301), channel_id=1, source_target_pairs={{0,1},{1,2},{2,3},{4,5},{5,6},{6,7},{8,9},{9,10},{10,11},{12,13},{... | collective-permute-start | bytes 122888 | tf_op jit(solution)/shard_map/ppermute | solution.py:51
  199.3 16.7 %copy-start.49 = (s32[1024]{0:T(1024)}, s32[1024]{0:T(1024)S(1)}, u32[]{:S(2)}) copy-start(s32[1024]{0:T(1024)S(1)} %pad_clamp_fusion.5) | copy-start | bytes 12292
  201.2 57.4 %collective-permute-start = (f32[8,1,5,256]{3,0,2,1:T(8,128)}, f32[8,1,5,256]{3,0,2,1:T(8,128)}, u32[]{:S(2)}, u32[]{:S(2)}) collective-permute-start(f32[8,1,5,256]{3,0,2,1:T(8,128)} %bitcast.302), channel_id=1, source_target_pairs={{1,0},{2,1},{3,2},{5,4},{6,5},{7,6},{9,8},{10,9},{11,10},{13,12},{... | collective-permute-start | bytes 122888 | tf_op jit(solution)/shard_map/ppermute | solution.py:54
  224.8 63.6 %copy-start.19 = (f32[8,5,15,256]{3,2,0,1:T(8,128)S(1)}, f32[8,5,15,256]{3,2,0,1:T(8,128)}, u32[]{:S(2)}) copy-start(f32[8,5,15,256]{3,2,0,1:T(8,128)} %slice.376) | copy-start | bytes 1843204
  290.2 6.2 %copy-start.8 = (f32[8,16,256]{2,1,0:T(8,128)S(1)}, f32[8,16,256]{2,1,0:T(8,128)}, u32[]{:S(2)}) copy-start(f32[8,16,256]{2,1,0:T(8,128)} %copy-done.7) | copy-start | bytes 393220
  290.2 6.2 %copy-start.10 = (f32[8,16,256]{2,1,0:T(8,128)S(1)}, f32[8,16,256]{2,1,0:T(8,128)}, u32[]{:S(2)}) copy-start(f32[8,16,256]{2,1,0:T(8,128)} %copy-done.9) | copy-start | bytes 393220
  290.2 6.2 %copy-start.12 = (f32[8,16,256]{2,1,0:T(8,128)S(1)}, f32[8,16,256]{2,1,0:T(8,128)}, u32[]{:S(2)}) copy-start(f32[8,16,256]{2,1,0:T(8,128)} %copy-done.11) | copy-start | bytes 393220
  290.2 6.2 %copy-start.23 = (f32[8,16,256]{2,1,0:T(8,128)S(1)}, f32[8,16,256]{2,1,0:T(8,128)}, u32[]{:S(2)}) copy-start(f32[8,16,256]{2,1,0:T(8,128)} %copy-done.22) | copy-start | bytes 393220
  376.4 7.4 %copy-start.69 = (s32[5]{0:T(128)S(1)}, s32[5]{0:T(128)}, u32[]{:S(2)}) copy-start(s32[5]{0:T(128)} %constant.230) | copy-start | bytes 64
  398.1 30.4 %copy-start.56 = (pred[8]{0:T(512)(128)(4,1)S(1)}, pred[8]{0:T(512)(128)(4,1)}, u32[]{:S(2)}) copy-start(pred[8]{0:T(512)(128)(4,1)} %get-tuple-element.25) | copy-start | bytes 28
  398.1 30.4 %copy-start.71 = (pred[8]{0:T(512)(128)(4,1)S(1)}, pred[8]{0:T(512)(128)(4,1)}, u32[]{:S(2)}) copy-start(pred[8]{0:T(512)(128)(4,1)} %get-tuple-element.76) | copy-start | bytes 28
  399.2 31.1 %copy-start.14 = (f32[8,5,16,16]{3,2,0,1:T(8,128)}, f32[8,5,16,16]{3,2,0,1:T(8,128)S(1)}, u32[]{:S(2)}) copy-start(f32[8,5,16,16]{3,2,0,1:T(8,128)S(1)} %slice.386) | copy-start | bytes 122884
  399.2 31.1 %copy-start.55 = (pred[8]{0:T(512)(128)(4,1)S(1)}, pred[8]{0:T(512)(128)(4,1)}, u32[]{:S(2)}) copy-start(pred[8]{0:T(512)(128)(4,1)} %get-tuple-element.26) | copy-start | bytes 28
  399.2 31.1 %copy-start.70 = (pred[8]{0:T(512)(128)(4,1)S(1)}, pred[8]{0:T(512)(128)(4,1)}, u32[]{:S(2)}) copy-start(pred[8]{0:T(512)(128)(4,1)} %get-tuple-element.77) | copy-start | bytes 28
  441.2 7.5 %copy-start.64 = (s32[5]{0:T(128)S(1)}, s32[5]{0:T(128)}, u32[]{:S(2)}) copy-start(s32[5]{0:T(128)} %constant.234) | copy-start | bytes 64
  454.7 30.9 %copy-start.73 = (pred[8,48]{1,0:T(8,128)(4,1)S(1)}, pred[8,48]{1,0:T(8,128)(4,1)}, u32[]{:S(2)}) copy-start(pred[8,48]{1,0:T(8,128)(4,1)} %get-tuple-element.66) | copy-start | bytes 1156
  454.7 30.9 %copy-start.74 = (pred[8,48]{1,0:T(8,128)(4,1)S(1)}, pred[8,48]{1,0:T(8,128)(4,1)}, u32[]{:S(2)}) copy-start(pred[8,48]{1,0:T(8,128)(4,1)} %get-tuple-element.67) | copy-start | bytes 1156
  455.4 30.2 %copy-start.16 = (f32[5,8,16,256]{3,2,1,0:T(8,128)}, f32[5,8,16,256]{3,2,1,0:T(8,128)S(1)}, u32[]{:S(2)}) copy-start(f32[5,8,16,256]{3,2,1,0:T(8,128)S(1)} %gather_fusion.11) | copy-start | bytes 1966084
  456.8 42.3 %collective-permute-start.3 = (f32[8,1,5,256]{3,0,2,1:T(8,128)}, f32[8,1,5,256]{3,0,2,1:T(8,128)}, u32[]{:S(2)}, u32[]{:S(2)}) collective-permute-start(f32[8,1,5,256]{3,0,2,1:T(8,128)} %bitcast.299), channel_id=1, source_target_pairs={{0,1},{1,2},{2,3},{4,5},{5,6},{6,7},{8,9},{9,10},{10,11},{12,13},{... | collective-permute-start | bytes 122888 | tf_op jit(solution)/shard_map/ppermute | solution.py:51
  487.6 40.4 %copy-start.54 = (pred[8]{0:T(512)(128)(4,1)S(1)}, pred[8]{0:T(512)(128)(4,1)}, u32[]{:S(2)}) copy-start(pred[8]{0:T(512)(128)(4,1)} %get-tuple-element.23) | copy-start | bytes 28
  490.0 68.0 %copy-start.17 = (f32[5,8,16,256]{3,2,1,0:T(8,128)S(1)}, f32[5,8,16,256]{3,2,1,0:T(8,128)}, u32[]{:S(2)}) copy-start(f32[5,8,16,256]{3,2,1,0:T(8,128)} %copy-done.16) | copy-start | bytes 1966084
  490.0 69.9 %all-to-all-start = ((f32[8,48,256]{2,1,0:T(8,128)}), f32[8,48,256]{2,1,0:T(8,128)S(1)}, u32[]{:S(2)}, u32[]{:S(2)}) async-start(f32[8,48,256]{2,1,0:T(8,128)} %select_select_fusion), calls=%async_computation | async-start | bytes 786432 | tf_op jit(solution)/shard_map/all_to_all | solution.py:238
  497.2 32.3 %collective-permute-start.2 = (f32[8,1,5,256]{3,0,2,1:T(8,128)}, f32[8,1,5,256]{3,0,2,1:T(8,128)}, u32[]{:S(2)}, u32[]{:S(2)}) collective-permute-start(f32[8,1,5,256]{3,0,2,1:T(8,128)} %bitcast.300), channel_id=1, source_target_pairs={{1,0},{2,1},{3,2},{5,4},{6,5},{7,6},{9,8},{10,9},{11,10},{13,12},{... | collective-permute-start | bytes 122888 | tf_op jit(solution)/shard_map/ppermute | solution.py:54
  572.5 7.5 %copy-start.36 = (f32[8,5,256]{2,1,0:T(8,128)S(1)}, f32[8,5,256]{2,1,0:T(8,128)}, u32[]{:S(2)}) copy-start(f32[8,5,256]{2,1,0:T(8,128)} %gather_fusion.25) | copy-start | bytes 122884
  572.5 7.5 %copy-start.53 = (pred[8]{0:T(512)(128)(4,1)S(1)}, pred[8]{0:T(512)(128)(4,1)}, u32[]{:S(2)}) copy-start(pred[8]{0:T(512)(128)(4,1)} %get-tuple-element.24) | copy-start | bytes 28
  572.5 7.5 %copy-start.72 = (pred[8]{0:T(512)(128)(4,1)S(1)}, pred[8]{0:T(512)(128)(4,1)}, u32[]{:S(2)}) copy-start(pred[8]{0:T(512)(128)(4,1)} %get-tuple-element.75) | copy-start | bytes 28
  572.5 9.9 %slice-start = ((f32[48,16,8,16]{3,1,2,0:T(8,128)}), f32[2,16,8,16]{3,1,2,0:T(8,128)S(1)}, s32[]{:S(2)}) async-start(f32[48,16,8,16]{3,1,2,0:T(8,128)} %select_bitcast_fusion), calls=%async_computation.1 | async-start | bytes 262144 | tf_op jit(solution)/shard_map/slice | solution.py:256
  572.5 11.5 %copy-start.90 = (f32[52]{0:T(128)S(1)}, f32[52]{0:T(128)}, u32[]{:S(2)}) copy-start(f32[52]{0:T(128)} %pad.11.clone) | copy-start | bytes 628
  576.7 7.3 %collective-permute-start.4 = (f32[2,16,128]{2,1,0:T(8,128)S(1)}, f32[2,16,128]{2,1,0:T(8,128)S(1)}, u32[]{:S(2)}, u32[]{:S(2)}) collective-permute-start(f32[2,16,128]{2,1,0:T(8,128)S(1)} %copy.175), channel_id=1, source_target_pairs={{0,4},{4,8},{8,12},{12,16},{16,20},{20,24},{24,28},{1,5},{5,9},{9,... | collective-permute-start | bytes 49160 | tf_op jit(solution)/shard_map/ppermute | solution.py:51
  582.4 24.7 %copy-start.18 = (f32[8,5,15,256]{3,2,0,1:T(8,128)S(1)}, f32[8,5,15,256]{3,2,0,1:T(8,128)}, u32[]{:S(2)}) copy-start(f32[8,5,15,256]{3,2,0,1:T(8,128)} %slice.392) | copy-start | bytes 1843204
  582.4 24.7 %copy-start.34 = (f32[8,5,1,256]{3,2,0,1:T(1,128)S(1)}, f32[8,5,1,256]{3,2,0,1:T(1,128)}, u32[]{:S(2)}) copy-start(f32[8,5,1,256]{3,2,0,1:T(1,128)} %slice.391) | copy-start | bytes 122884
  582.4 24.7 %copy-start.75 = (pred[16]{0:T(512)(128)(4,1)S(1)}, pred[16]{0:T(512)(128)(4,1)}, u32[]{:S(2)}) copy-start(pred[16]{0:T(512)(128)(4,1)} %iota_compare_fusion.4) | copy-start | bytes 52
  582.6 4.6 collective-permute-start.5
  585.1 23.0 %copy-start.60 = (s32[5]{0:T(128)S(1)}, s32[5]{0:T(128)}, u32[]{:S(2)}) copy-start(s32[5]{0:T(128)} %constant.238) | copy-start | bytes 64
  587.3 22.7 %copy-start.58 = (s32[5]{0:T(128)S(1)}, s32[5]{0:T(128)}, u32[]{:S(2)}) copy-start(s32[5]{0:T(128)} %constant.240) | copy-start | bytes 64
  587.8 19.3 %copy-start.20 = (f32[48,16,128]{2,1,0:T(8,128)}, f32[48,16,128]{2,1,0:T(8,128)S(1)}, u32[]{:S(2)}) copy-start(f32[48,16,128]{2,1,0:T(8,128)S(1)} %fusion.52) | copy-start | bytes 1179652
  588.5 23.4 %collective-permute-start.6 = (f32[48,2,128]{2,1,0:T(2,128)}, f32[48,2,128]{2,1,0:T(2,128)S(1)}, u32[]{:S(2)}, u32[]{:S(2)}) collective-permute-start(f32[48,2,128]{2,1,0:T(2,128)} %get-tuple-element.59), channel_id=1, source_target_pairs={{0,1},{1,2},{2,3},{4,5},{5,6},{6,7},{8,9},{9,10},{10,11},{12,13},{... | collective-permute-start | bytes 147464 | tf_op jit(solution)/shard_map/ppermute | solution.py:51
  605.1 6.8 %copy-start.89 = (pred[48]{0:T(512)(128)(4,1)S(1)}, pred[48]{0:T(512)(128)(4,1)}, u32[]{:S(2)}) copy-start(pred[48]{0:T(512)(128)(4,1)} %iota_compare_fusion.2) | copy-start | bytes 148
  605.1 6.7 %collective-permute-start.7 = (f32[48,2,128]{2,1,0:T(2,128)S(1)}, f32[48,2,128]{2,1,0:T(2,128)S(1)}, u32[]{:S(2)}, u32[]{:S(2)}) collective-permute-start(f32[48,2,128]{2,1,0:T(2,128)S(1)} %get-tuple-element.60), channel_id=1, source_target_pairs={{1,0},{2,1},{3,2},{5,4},{6,5},{7,6},{9,8},{10,9},{11,10},{13,12},{... | collective-permute-start | bytes 147464 | tf_op jit(solution)/shard_map/ppermute | solution.py:54
  607.1 6.3 %copy-start.1 = (s32[1,64,6]{1,0,2:T(1,128)S(1)}, s32[1,64,6]{1,0,2:T(1,128)}, u32[]{:S(2)}) copy-start(s32[1,64,6]{1,0,2:T(1,128)} %param.55) | copy-start | bytes 4612
  (37 other events, 143.8 us)
where the time goes:
time: 623 us; the launch traced here: 614 us
  local copies, waits for them, and re-layouts  234 us (38%)
  blocking collectives  213 us (34%)
  other arithmetic  86.6 us (14%)
  starting transfers between devices  73.1 us (12%)
    ppermute x4, starting transfers between devices, padded_2(): lax.ppermute(lax.slice_in_dim(block, block.shape[dim] - width, None, axis...  60.1 us
    all_gather x2, blocking collectives, local(): x_all = lax.all_gather(x_out, 'blk', axis=0, tiled=True)  56.6 us
    all_gather x2, blocking collectives, local(): y_all = lax.all_gather(y_after, 'blk', axis=0, tiled=True)  55.3 us
    all_gather x2, blocking collectives, local(): lax.all_gather(layer_ends[:, 3], 'blk', axis=0, tiled=True)  50.7 us
    all_gather x2, blocking collectives, local(): lax.all_gather(layer_ends[:, 0], 'blk', axis=0, tiled=True)  50.3 us
    gather x12, local copies, waits for them, and re-layouts, pick_rows(): found_rows = jnp.take(source, jnp.maximum(slot_index, 0), axis=0)  25.1 us
    another operation x6, local copies, waits for them, and re-layouts, section_y(): jnp.tile(north_in, (1, 1, 1, edge))  18.2 us
    another operation x6, local copies, waits for them, and re-layouts, section_y(): jnp.tile(south_in, (1, 1, 1, edge))  18.2 us
  transfers between devices with their start and end apart: 9, of which 1 were waited for; matrix products, arithmetic and copies ran while one was open for 9% of the time, Pallas kernels for 0%

commit v1 on v0

v1 whole, which is shorter than its diff:
```python
import functools

import jax
import jax.numpy as jnp
import numpy as np
from jax import lax
from jax.experimental import pallas as pl
from jax.experimental.pallas import tpu as pltpu
from jax.sharding import PartitionSpec as P

STEPS = 2
VELOCITIES = [
    (0, 0, 0),
    (1, 0, 0),
    (-1, 0, 0),
    (0, 1, 0),
    (0, -1, 0),
    (0, 0, 1),
    (0, 0, -1),
    (1, 1, 0),
    (-1, -1, 0),
    (1, -1, 0),
    (-1, 1, 0),
    (1, 0, 1),
    (-1, 0, -1),
    (1, 0, -1),
    (-1, 0, 1),
    (0, 1, 1),
    (0, -1, -1),
    (0, 1, -1),
    (0, -1, 1),
]
POPS = 19
EAST_POPS = [1, 7, 9, 11, 13]
WEST_POPS = [2, 8, 10, 12, 14]
NORTH_POPS = [3, 7, 10, 15, 17]
SOUTH_POPS = [4, 8, 9, 16, 18]
UPPER_POPS = [5, 11, 14, 15, 18]
LOWER_POPS = [6, 12, 13, 16, 17]
RELAX_RATE = 1.25
DRAG_RATE = 0.3
TAP_EDGE, TAP_NEAR = 1.0 / 3.0, 2.0 / 3.0

FACE_ROWS = 48


def dev_of(slot, blocks):
    return lax.div(jnp.maximum(slot, 0), jnp.int32(blocks))


def shift(value, amount, axis=1):
    amount = amount % value.shape[axis]
    return value if amount == 0 else pltpu.roll(value, amount, axis)


def lanes(shape):
    return lax.broadcasted_iota(jnp.int32, shape, len(shape) - 1)


def collide_cells(f, u, porosity):
    total, gap = {}, {}
    for i in range(1, POPS, 2):
        total[i], gap[i] = f[i] + f[i + 1], f[i] - f[i + 1]
    ux, uy, uz = u
    mx = gap[1] + gap[7] + gap[9] + gap[11] + gap[13]
    my = gap[3] + gap[7] - gap[9] + gap[15] + gap[17]
    mz = gap[5] + gap[11] - gap[13] + gap[15] - gap[17]
    xy_sum, xz_sum, yz_sum = total[7] + total[9], total[11] + total[13], total[15] + total[17]
    xx = 2.0 * total[1] + xy_sum + xz_sum
    yy = 2.0 * total[3] + xy_sum + yz_sum
    zz = 2.0 * total[5] + xz_sum + yz_sum
    xy, xz, yz = total[7] - total[9], total[11] - total[13], total[15] - total[17]
    mass = 12.0 * f[0] + 2.0 * (total[1] + total[3] + total[5]) + (xy_sum + xz_sum + yz_sum)
    speed_sq = ux * ux + uy * uy + uz * uz
    qx = xx * ux + xy * uy + xz * uz
    qy = xy * ux + yy * uy + yz * uz
    qz = xz * ux + yz * uy + zz * uz
    sens = ux * mx + uy * my + uz * mz
    drag = DRAG_RATE * porosity
    scale = RELAX_RATE / 36.0
    quad = ux * qx + uy * qy + uz * qz
    base = scale * (mass + 1.5 * (speed_sq * mass) - 4.5 * quad) + drag * sens
    gx = (3.0 * scale) * (mx + gap[1] + 3.0 * qx - ux * mass) - drag * mx
    gy = (3.0 * scale) * (my + gap[3] + 3.0 * qy - uy * mass) - drag * my
    gz = (3.0 * scale) * (mz + gap[5] + 3.0 * qz - uz * mass) - drag * mz
    along = {1: gx, 3: gy, 5: gz, 7: gx + gy, 9: gx - gy, 11: gx + gz, 13: gx - gz, 15: gy + gz, 17: gy - gz}
    keep = 1.0 - RELAX_RATE
    post = [base + keep * f[0]]
    for i in range(1, POPS, 2):
        post.append(base + along[i] + keep * f[i])
        post.append(base - along[i] + keep * f[i + 1])
    return post, sens


def collide_block(read, velocity_ref, porosity_ref, post_ref, edge, plane):
    parts = {}
    for low in range(0, edge, 8):
        for left in range(0, plane, 128):
            zs, cells = pl.ds(low, 8), pl.ds(left, 128)
            post, sens = collide_cells(
                [read(p, zs, cells) for p in range(POPS)],
                [velocity_ref[c, zs, cells] for c in range(3)],
                porosity_ref[zs, cells],
            )
            for p in range(POPS):
                post_ref[p, zs, cells] = post[p]
            parts[low, left] = sens
    return parts


def pack_faces(block, blocks, post_ref, faces_ref, edge, plane):
    slot = lanes((edge, plane)) % edge
    x_tile = jnp.zeros((edge, plane), jnp.float32)
    for s, p in enumerate(EAST_POPS):
        x_tile = jnp.where(slot == s, shift(post_ref[p], s), x_tile)
    for s, p in enumerate(WEST_POPS):
        x_tile = jnp.where(slot == 5 + s, shift(post_ref[p], 5 + s - (edge - 1)), x_tile)
    faces_ref[block, 0:16, :] = x_tile
    for i in range(5):
        faces_ref[block, 32 + i : 33 + i, :] = post_ref[UPPER_POPS[i], 0:1, :]
        faces_ref[block, 40 + i : 41 + i, :] = post_ref[LOWER_POPS[i], edge - 1 : edge, :]
    faces_ref[block, 37:38, :] = x_tile[0:1]
    faces_ref[block, 45:46, :] = x_tile[edge - 1 : edge]
    group = lanes((edge, 128)) // edge
    north = jnp.zeros((edge, 128), jnp.float32)
    south = jnp.zeros((edge, 128), jnp.float32)
    for q in range(5):
        north = jnp.where(group == q, shift(post_ref[NORTH_POPS[q], :, 0:128], q * edge), north)
        south = jnp.where(
            group == q, shift(post_ref[SOUTH_POPS[q], :, plane - 128 : plane], (q + 1) * edge - 128), south
        )

    @pl.when(block > 0)
    def _():
        faces_ref[block - 1, 16:32, 0:128] = north
        faces_ref[block - 1, 38:39, 0:128] = north[0:1]
        faces_ref[block - 1, 46:47, 0:128] = north[edge - 1 : edge]

    @pl.when(block < blocks - 1)
    def _():
        faces_ref[block + 1, 16:32, 128:256] = south
        faces_ref[block + 1, 38:39, 128:256] = south[0:1]
        faces_ref[block + 1, 46:47, 128:256] = south[edge - 1 : edge]


def stream_pop(p, source, halo_ref, edge, plane):
    cx, cy, cz = VELOCITIES[p]
    lane = lanes((edge, plane))
    value = shift(source, -(cx + edge * cy))
    if cx != 0:
        face = edge - 1 if cx > 0 else 0
        s = EAST_POPS.index(p) if cx > 0 else 5 + WEST_POPS.index(p)
        arrived = shift(halo_ref[0, 0:16, :], face - s - edge * cy)
        value = jnp.where(lane % edge == face, arrived, value)
    if cy != 0:
        face = edge - 1 if cy > 0 else 0
        start = NORTH_POPS.index(p) * edge if cy > 0 else 128 + SOUTH_POPS.index(p) * edge
        arrived = shift(halo_ref[0, 16:32, :], face * edge - start)
        value = jnp.where(lane // edge == face, arrived, value)
    if cz != 0:
        face = edge - 1 if cz > 0 else 0
        row = 32 + UPPER_POPS.index(p) if cz > 0 else 40 + LOWER_POPS.index(p)
        arrived = halo_ref[0, row : row + 1, :]
        depth = lax.broadcasted_iota(jnp.int32, (edge, plane), 0)
        value = jnp.where(depth == face, arrived, shift(value, -cz, 0))
    return value


def first_kernel(blocks, state_ref, velocity_ref, porosity_ref, post_ref, sens_ref, faces_ref):
    block = pl.program_id(0)
    edge, plane = porosity_ref.shape[1:]
    parts = collide_block(
        lambda p, zs, cells: state_ref[0, p, zs, cells],
        velocity_ref.at[0],
        porosity_ref.at[0],
        post_ref.at[0],
        edge,
        plane,
    )
    for (low, left), sens in parts.items():
        sens_ref[0, pl.ds(low, 8), pl.ds(left, 128)] = sens
    pack_faces(block, blocks, post_ref.at[0], faces_ref, edge, plane)


def slab_start(owner_ref, slab, devices):
    start = jnp.int32(0)
    for j in range(devices):
        start = start + jnp.where(j < slab, 2 * owner_ref[j], 0)
    return start


def second_kernel(
    blocks,
    devices,
    chunks,
    owner_ref,
    before_ref,
    halo_ref,
    velocity_ref,
    porosity_ref,
    sens_ref,
    post_ref,
    faces_ref,
    rows_ref,
    state_ref,
    field_ref,
):
    block = pl.program_id(0)
    edge, plane = porosity_ref.shape[1:]
    for p in range(POPS):
        state_ref[p] = stream_pop(p, before_ref[0, p], halo_ref, edge, plane)
    parts = collide_block(
        lambda p, zs, cells: state_ref[p, zs, cells],
        velocity_ref.at[0],
        porosity_ref.at[0],
        post_ref.at[0],
        edge,
        plane,
    )
    for (low, left), sens in parts.items():
        field_ref[block * (plane // 128) + left // 128, pl.ds(low, 8), :] = (
            sens_ref[0, pl.ds(low, 8), pl.ds(left, 128)] + sens
        )
    pack_faces(block, blocks, post_ref.at[0], faces_ref, edge, plane)

    @pl.when(block == blocks - 1)
    def _():
        held = blocks * (plane // 128)
        start = jnp.int32(0)
        for j in range(devices):
            first = lax.div(start + 6, jnp.int32(8)) - 1
            for i in range(chunks):
                rows_ref[j, i] = field_ref[jnp.clip(first + i, 0, held - 1)]
            start = start + 2 * owner_ref[j]


def last_kernel(before_ref, halo_ref, out_ref):
    edge, plane = out_ref.shape[2:]
    for p in range(POPS):
        out_ref[0, p] = stream_pop(p, before_ref[0, p], halo_ref, edge, plane)


def route_kernel(blocks, devices, table_ref, row_ref, faces_ref, above_ref, below_ref, halo_ref):
    row = row_ref[0]
    edge, plane = 16, faces_ref.shape[2]
    slot = lanes((edge, plane)) % edge
    lane = lanes((edge, 128))
    line = lanes((1, plane))
    dev = functools.partial(dev_of, blocks=blocks)

    def beside(slot_id, face):
        return jnp.where(slot_id < 0, -1, table_ref[jnp.maximum(slot_id, 0), face])

    def one(d, carry):
        here = d * blocks + row
        west, east, south, north, below, above = [table_ref[here, face] for face in range(6)]
        zero = jnp.float32(0.0)
        halo_ref[d, 0:16, :] = jnp.where(
            slot < 5,
            jnp.where(east >= 0, faces_ref[dev(east), 0:16, :], zero),
            jnp.where(west >= 0, faces_ref[dev(west), 0:16, :], zero),
        )

        def y_face(where_from, left, east_q, west_q):
            far_east, far_west = beside(where_from, 1), beside(where_from, 0)

            def tile(slot_id):
                return jnp.where(slot_id >= 0, faces_ref[dev(slot_id), 16:32, left : left + 128], zero)

            own = tile(where_from)
            e, w = east_q * edge, west_q * edge
            moved = jnp.where((lane >= e) & (lane < e + edge), shift(own, -1), own)
            moved = jnp.where(lane == e + edge - 1, shift(tile(far_east), edge - 1), moved)
            moved = jnp.where((lane >= w) & (lane < w + edge), shift(own, 1), moved)
            return jnp.where(lane == w, shift(tile(far_west), 1 - edge), moved)

        halo_ref[d, 16:32, 0:128] = y_face(north, 0, 1, 2)
        halo_ref[d, 16:32, 128:256] = y_face(south, 128, 2, 1)

        def z_face(ref, where_from, face, pops, row0):
            def rows(slot_id, r):
                return jnp.where(slot_id >= 0, ref[dev(slot_id), r : r + 1, :], zero)

            from_x = {1: rows(beside(east, face), 5), -1: rows(beside(west, face), 5)}
            from_y = {1: rows(beside(north, face), 6), -1: rows(beside(south, face), 6)}
            for i, p in enumerate(pops):
                cx, cy, _ = VELOCITIES[p]
                value = shift(rows(where_from, i), -(cx + edge * cy))
                if cx != 0:
                    at = edge - 1 if cx > 0 else 0
                    s = EAST_POPS.index(p) if cx > 0 else 5 + WEST_POPS.index(p)
                    value = jnp.where(line % edge == at, shift(from_x[cx], at - s), value)
                if cy != 0:
                    at = edge - 1 if cy > 0 else 0
                    start = NORTH_POPS.index(p) * edge if cy > 0 else 128 + SOUTH_POPS.index(p) * edge
                    value = jnp.where(line // edge == at, shift(from_y[cy], at * edge - start), value)
                halo_ref[d, row0 + i : row0 + i + 1, :] = value

        z_face(above_ref, above, 5, UPPER_POPS, 32)
        z_face(below_ref, below, 4, LOWER_POPS, 40)
        return carry

    lax.fori_loop(0, devices, one, 0)


def slab_kernel(
    blocks, devices, chunks, owner_ref, column_ref, slab_ref, rows_ref, out_ref, low_ref, high_ref, field_ref
):
    slab = slab_ref[0]
    count, edge, width = out_ref.shape
    start = slab_start(owner_ref, slab, devices)
    first = lax.div(start + 6, jnp.int32(8)) - 1
    lane = lanes((edge, width))
    group = lane // edge
    per_block = 256 // 128
    held = blocks * per_block

    def chunk(i, carry):
        at = first + i
        inside = (at >= 0) & (at < held)
        block_row = lax.div(jnp.clip(at, 0, held - 1), jnp.int32(per_block))
        tiles = [jnp.zeros((edge, width), jnp.float32) for _ in range(8)]
        for e in range(devices):
            column = column_ref[0, e * blocks + block_row]
            value = rows_ref[e, i]
            turned = pltpu.roll(value, lax.rem(column, jnp.int32(8)) * edge, 1)
            hit = (group == column) & inside
            for r in range(8):
                part = shift(turned, -r * edge)
                if width > 128:
                    part = jnp.concatenate([part] * (width // 128), axis=1)
                tiles[r] = jnp.where(hit, part, tiles[r])
        for r in range(8):
            field_ref[i * 8 + r] = tiles[r]
        return carry

    lax.fori_loop(0, chunks, chunk, 0)
    offset = start - 2 - 8 * first

    def row(r, carry):
        at = offset + r
        mixed = TAP_EDGE * (field_ref[at] + field_ref[at + 4]) + (
            TAP_NEAR * (field_ref[at + 1] + field_ref[at + 3]) + field_ref[at + 2]
        )
        value = mixed
        for step, tap in ((1, TAP_NEAR), (2, TAP_EDGE)):
            left = jnp.where(lane >= step, shift(mixed, step), 0.0)
            right = jnp.where(lane < width - step, shift(mixed, -step), 0.0)
            value = value + tap * (left + right)
        out_ref[r] = value
        for z in range(2):
            low_ref[z, pl.ds(r, 1), :] = value[z : z + 1]
            high_ref[z, pl.ds(r, 1), :] = value[edge - 2 + z : edge - 1 + z]
        return carry

    lax.fori_loop(0, count, row, 0)


def depth_kernel(owner_ref, slab_ref, rows_ref, below_ref, above_ref, out_ref):
    count, edge, width = out_ref.shape
    own_rows = 2 * owner_ref[slab_ref[0]]
    depth = lax.broadcasted_iota(jnp.int32, (edge, width), 0)

    def row(r, carry):
        value = rows_ref[r]
        b0, b1 = [below_ref[z, pl.ds(r, 1), :] for z in range(2)]
        a0, a1 = [above_ref[z, pl.ds(r, 1), :] for z in range(2)]
        down = jnp.where(depth == 0, b1, shift(value, 1, 0))
        up = jnp.where(depth == edge - 1, a0, shift(value, -1, 0))
        down_2 = jnp.where(depth == 0, b0, jnp.where(depth == 1, b1, shift(value, 2, 0)))
        up_2 = jnp.where(depth == edge - 1, a1, jnp.where(depth == edge - 2, a0, shift(value, -2, 0)))
        total = value + TAP_NEAR * (down + up) + TAP_EDGE * (down_2 + up_2)
        out_ref[r] = jnp.where(r < own_rows, total, 0.0)
        return carry

    lax.fori_loop(0, count, row, 0)


SMEM = pl.BlockSpec(memory_space=pltpu.SMEM)
VMEM = pl.BlockSpec(memory_space=pltpu.VMEM)


def by_block(shape):
    rest = len(shape) - 1
    return pl.BlockSpec((1,) + tuple(shape[1:]), lambda b: (b,) + (0,) * rest)


def whole(shape):
    return pl.BlockSpec(tuple(shape), lambda b: (0,) * len(shape))


def f32(*shape):
    return jax.ShapeDtypeStruct(shape, jnp.float32)


def local(adjoint, velocity, porosity, block_x, neighbours, owner_map):
    blocks, _, edge, plane = adjoint.shape[1:]
    devices, layers = lax.axis_size("blk"), lax.axis_size("gz")
    my_index = lax.axis_index("blk").astype(jnp.int32)
    row_id = jnp.minimum(my_index, blocks - 1).reshape(1)
    slab_id = my_index.reshape(1)
    state, flow, design, table = adjoint[0], velocity[0], porosity[0], neighbours[0]
    rows_cap = 2 * (3 * (blocks * edge // 2) // devices)
    chunks = -(-(rows_cap + 10) // 8)
    width = devices * edge
    upward = [(g, g + 1) for g in range(layers - 1)]
    downward = [(g + 1, g) for g in range(layers - 1)]
    faces_shape = (devices, FACE_ROWS, plane)
    params = pltpu.CompilerParams(vmem_limit_bytes=32 * 1024 * 1024)

    def to_halo(faces):
        gathered = lax.all_to_all(faces, "blk", 0, 0, tiled=True)
        above = lax.ppermute(gathered[:, 32:40], "gz", downward)
        below = lax.ppermute(gathered[:, 40:48], "gz", upward)
        halo = pl.pallas_call(
            functools.partial(route_kernel, blocks, devices),
            out_shape=f32(*faces_shape),
            in_specs=[SMEM, SMEM, VMEM, VMEM, VMEM],
            out_specs=VMEM,
            compiler_params=params,
            name="route",
        )(table, row_id, gathered, above, below)
        return lax.all_to_all(halo, "blk", 0, 0, tiled=True)

    post, sens, faces = pl.pallas_call(
        functools.partial(first_kernel, blocks),
        grid=(blocks,),
        out_shape=(f32(*state.shape), f32(*design.shape), f32(*faces_shape)),
        in_specs=[by_block(state.shape), by_block(flow.shape), by_block(design.shape)],
        out_specs=(by_block(state.shape), by_block(design.shape), whole(faces_shape)),
        compiler_params=params,
        name="collide_first",
    )(state, flow, design)
    halo = to_halo(faces)
    rows_shape = (devices, chunks, edge, 128)
    post, faces, rows = pl.pallas_call(
        functools.partial(second_kernel, blocks, devices, chunks),
        grid=(blocks,),
        out_shape=(f32(*state.shape), f32(*faces_shape), f32(*rows_shape)),
        in_specs=[
            SMEM,
            by_block(state.shape),
            by_block(faces_shape),
            by_block(flow.shape),
            by_block(design.shape),
            by_block(design.shape),
        ],
        out_specs=(by_block(state.shape), whole(faces_shape), whole(rows_shape)),
        scratch_shapes=[
            pltpu.VMEM((POPS, edge, plane), jnp.float32),
            pltpu.VMEM((blocks * plane // 128, edge, 128), jnp.float32),
        ],
        compiler_params=params,
        name="stream_collide",
    )(owner_map, post, halo, flow, design, sens)
    halo = to_halo(faces)
    rows = lax.all_to_all(rows, "blk", 0, 0, tiled=True)
    ends = (2, rows_cap, width)
    slab, low, high = pl.pallas_call(
        functools.partial(slab_kernel, blocks, devices, chunks),
        out_shape=(f32(rows_cap, edge, width), f32(*ends), f32(*ends)),
        in_specs=[SMEM, SMEM, SMEM, VMEM],
        out_specs=(VMEM, VMEM, VMEM),
        scratch_shapes=[pltpu.VMEM((chunks * 8, edge, width), jnp.float32)],
        compiler_params=params,
        name="slab_rows",
    )(owner_map, block_x, slab_id, rows)
    below = lax.ppermute(high, "gz", upward)
    above = lax.ppermute(low, "gz", downward)
    smoothed = pl.pallas_call(
        depth_kernel,
        out_shape=f32(rows_cap, edge, width),
        in_specs=[SMEM, SMEM, VMEM, VMEM, VMEM],
        out_specs=VMEM,
        compiler_params=params,
        name="slab_depth",
    )(owner_map, slab_id, slab, below, above)
    moved = pl.pallas_call(
        last_kernel,
        grid=(blocks,),
        out_shape=f32(*state.shape),
        in_specs=[by_block(state.shape), by_block(faces_shape)],
        out_specs=by_block(state.shape),
        compiler_params=params,
        name="stream_last",
    )(post, halo)
    return (moved[None], smoothed[None, None])


def solution(mesh):
    placed = (
        P("gz", "blk", None, None, None),
        P("gz", "blk", None, None, None),
        P("gz", "blk", None, None),
        P("gz", None),
        P("gz", None, None),
        P(),
    )
    return jax.shard_map(
        local,
        mesh=mesh,
        in_specs=placed,
        out_specs=(P("gz", "blk", None, None, None), P("gz", "blk", None, None, None)),
        check_vma=False,
    )
```

time: 623 us -> 114 us (0.18); the launches traced: 614 us -> 113 us
  local copies, waits for them, and re-layouts: 234 us -> 7.63 us
  blocking collectives: 213 us -> 44.3 us
  other arithmetic: 86.6 us -> 0 us
  starting transfers between devices: 73.1 us -> 25.1 us
  Pallas kernels: 0 us -> 22.6 us
  waiting for transfers between devices: 2.05 us -> 12.7 us
    all_gather x8 -> x0, blocking collectives: 213 us -> none  [the longest x2 56.6 us: local(): x_all = lax.all_gather(x_out, 'blk', axis=0, tiled=True)]
    another operation x28 -> x0, local copies, waits for them, and re-layouts: 53.2 us -> none  [the longest x6 18.2 us: section_y(): jnp.tile(north_in, (1, 1, 1, edge))]
    ppermute x8 -> x6, starting transfers between devices: 67.3 us -> 16.3 us  [the longest x2 7.62 us: to_halo(): below = lax.ppermute(gathered[:, 40:48], 'gz', upward)]
    gather x29 -> x0, local copies, waits for them, and re-layouts: 46.8 us -> none  [the longest x12 25.1 us: pick_rows(): found_rows = jnp.take(source, jnp.maximum(slot_index, 0), axis=0)]
    all_to_all x0 -> x3, blocking collectives: none -> 44.3 us  [the longest x2 30.9 us: to_halo(): gathered = lax.all_to_all(faces, 'blk', 0, 0, tiled=True)]
    select_n x31 -> x0, other arithmetic: 38.4 us -> none  [the longest x12 8.26 us: pick_rows(): return jnp.where(present, found_rows, jnp.zeros_like(found_rows))]
    slice x27 -> x2, local copies, waits for them, and re-layouts: 32.6 us -> 0.02 us  [to_halo(): below = lax.ppermute(gathered[:, 40:48], 'gz', upward)]
    reshape x10 -> x0, local copies, waits for them, and re-layouts: 29.8 us -> none  [the longest x2 10 us: section_x(): jnp.repeat(from_east, edge, axis=-1)]
  transfers between devices with their start and end apart: 9 -> 8, of which waited for: 1 -> 4; matrix products, arithmetic and copies ran while one was open for 9% -> 0% of each run, Pallas kernels for 0% -> 9%
where the time goes in v1:
time: 114 us; the launch traced here: 113 us
  blocking collectives  44.3 us (39%)
  starting transfers between devices  25.1 us (22%)
  Pallas kernels  22.6 us (20%)
  waiting for transfers between devices  12.7 us (11%)
  local copies, waits for them, and re-layouts  7.63 us (7%)
    all_to_all x2, blocking collectives, to_halo(): gathered = lax.all_to_all(faces, 'blk', 0, 0, tiled=True)  30.9 us
    all_to_all x1, blocking collectives, to_halo(): return lax.all_to_all(halo, 'blk', 0, 0, tiled=True)  13.4 us
    ppermute x2, starting transfers between devices, to_halo(): below = lax.ppermute(gathered[:, 40:48], 'gz', upward)  7.62 us
    unnamed x25, local copies, waits for them, and re-layouts  7.61 us
    ppermute x2, waiting for transfers between devices, to_halo(): above = lax.ppermute(gathered[:, 32:40], 'gz', downward)  7 us
    pallas_call x1, Pallas kernels, local(): pl.pallas_call(functools.partial(slab_kernel, blocks, devices, chunks), o...  6.72 us
    all_to_all x1, starting transfers between devices, to_halo(): return lax.all_to_all(halo, 'blk', 0, 0, tiled=True)  4.88 us
    pallas_call x2, Pallas kernels, to_halo(): pl.pallas_call(functools.partial(route_kernel, blocks, devices), out_shap...  4.39 us
  transfers between devices with their start and end apart: 8, of which 4 were waited for; matrix products, arithmetic and copies ran while one was open for 0% of the time, Pallas kernels for 9%

profile of v1, /device:TPU:1, one launch (start us, length us, event | category | flops | bytes accessed | tf_op | source)
XLA Modules:
  0.0 113.1 jit_solution(5548987674142216090)
XLA Ops:
  0.6 0.0 copy-start.11
  0.6 0.0 copy-start
  0.7 1.7 %copy-done = f32[1,8,19,16,256]{4,3,2,1,0:T(8,128)S(1)} copy-done((f32[1,8,19,16,256]{4,3,2,1,0:T(8,128)S(1)}, f32[1,8,19,16,256]{4,3,2,1,0:T(8,128)}, u32[]{:S(2)}) %copy-start) | copy-done | bytes 2490392
  2.4 0.0 copy-start.4
  2.4 1.0 copy-done.4
  3.3 0.0 copy-start.7
  3.3 0.9 copy-done.7
  4.3 0.0 copy-start.5
  4.3 0.0 copy-start.8
  4.3 0.0 copy-start.9
  4.3 1.6 %collide_first.1 = (f32[8,19,16,256]{3,2,1,0:T(8,128)S(1)}, f32[8,16,256]{2,1,0:T(8,128)S(1)}, f32[8,48,256]{2,1,0:T(8,128)S(1)}) custom-call(f32[8,19,16,256]{3,2,1,0:T(8,128)S(1)} %bitcast.8, f32[8,3,16,256]{3,2,1,0:T(8,128)S(1)} %bitcast.9, f32[8,16,256]{2,1,0:T(8,128)S(1)} %bitcast.11), custom_call_target="tpu_custom_call" | custom-call | tf_op jit(solution)/shard_map/collide_first/pallas_call | solution.py:425
  5.9 0.0 copy-start.1
  5.9 1.4 %copy-done.1 = f32[8,19,16,256]{3,2,1,0:T(8,128)} copy-done((f32[8,19,16,256]{3,2,1,0:T(8,128)}, f32[8,19,16,256]{3,2,1,0:T(8,128)S(1)}, u32[]{:S(2)}) %copy-start.1) | copy-done | bytes 2490392
  7.4 16.5 %all_to_all.25.faces_ref = f32[8,48,256]{2,1,0:T(8,128)S(1)} all-to-all(f32[8,48,256]{2,1,0:T(8,128)S(1)} %get-tuple-element.12), channel_id=1, replica_groups=mesh['blk'=8,'gz'=4] {'blk'}, dimensions={0} | all-to-all | bytes 786432 | tf_op jit(solution)/shard_map/all_to_all | solution.py:412
  23.9 5.7 %collective-permute-start.1 = (f32[8,8,256]{2,1,0:T(8,128)S(1)}, f32[8,8,256]{2,1,0:T(8,128)S(1)}, u32[]{:S(2)}, u32[]{:S(2)}) collective-permute-start(f32[8,8,256]{2,1,0:T(8,128)S(1)} %get-tuple-element.22), channel_id=1, source_target_pairs={{0,1},{1,2},{2,3},{4,5},{5,6},{6,7},{8,9},{9,10},{10,11},{12,13},{... | collective-permute-start | bytes 196616 | tf_op jit(solution)/shard_map/ppermute | solution.py:414
  29.6 1.9 %collective-permute-start = (f32[8,8,256]{2,1,0:T(8,128)S(1)}, f32[8,8,256]{2,1,0:T(8,128)S(1)}, u32[]{:S(2)}, u32[]{:S(2)}) collective-permute-start(f32[8,8,256]{2,1,0:T(8,128)S(1)} %get-tuple-element.23), channel_id=1, source_target_pairs={{1,0},{2,1},{3,2},{5,4},{6,5},{7,6},{9,8},{10,9},{11,10},{13,12},{... | collective-permute-start | bytes 196616 | tf_op jit(solution)/shard_map/ppermute | solution.py:413
  31.5 0.0 copy-done.11
  31.5 0.1 copy.8
  31.6 0.0 collective-permute-done.1.below_ref
  31.6 3.5 %collective-permute-done.above_ref = f32[8,8,256]{2,1,0:T(8,128)S(1)} collective-permute-done((f32[8,8,256]{2,1,0:T(8,128)S(1)}, f32[8,8,256]{2,1,0:T(8,128)S(1)}, u32[]{:S(2)}, u32[]{:S(2)}) %collective-permute-start) | collective-permute-done | bytes 65568 | tf_op jit(solution)/shard_map/ppermute | solution.py:413
  35.2 2.2 %route.2 = f32[8,48,256]{2,1,0:T(8,128)S(1)} custom-call(s32[64,6]{1,0:T(8,128)S(1)} %bitcast.13, s32[1]{0:T(128)} %bitcast.4.row_ref, f32[8,48,256]{2,1,0:T(8,128)S(1)} %all_to_all.25.faces_ref, f32[8,8,256]{2,1,0:T(8,128)S(1)} %collective-permute-done.above_ref, f32[8,8,256]{2,1,0:T(8,128)S(1)} %collective-permute-done.1.below_ref), custom_call_target="tpu_custom_call" | custom-call | tf_op jit(solution)/shard_map/route/pallas_call | solution.py:415
  37.4 13.4 %all_to_all.26.halo_ref = f32[8,48,256]{2,1,0:T(8,128)S(1)} all-to-all(f32[8,48,256]{2,1,0:T(8,128)S(1)} %route.2), channel_id=1, replica_groups=mesh['blk'=8,'gz'=4] {'blk'}, dimensions={0} | all-to-all | bytes 786432 | tf_op jit(solution)/shard_map/all_to_all | solution.py:423
  50.8 0.0 copy-done.5
  50.8 0.0 copy-done.8
  50.8 0.0 copy-done.9
  50.8 0.0 copy-start.2
  50.8 1.7 %copy-done.2 = f32[8,19,16,256]{3,2,1,0:T(8,128)S(1)} copy-done((f32[8,19,16,256]{3,2,1,0:T(8,128)S(1)}, f32[8,19,16,256]{3,2,1,0:T(8,128)}, u32[]{:S(2)}) %copy-start.2) | copy-done | bytes 2490392
  52.5 4.0 %stream_collide.1 = (f32[8,19,16,256]{3,2,1,0:T(8,128)S(1)}, f32[8,48,256]{2,1,0:T(8,128)S(1)}, f32[8,8,16,128]{3,2,1,0:T(8,128)S(1)}) custom-call(s32[8]{0:T(128)S(1)} %copy-done.9, f32[8,19,16,256]{3,2,1,0:T(8,128)S(1)} %copy-done.2, f32[8,48,256]{2,1,0:T(8,128)S(1)} %all_to_all.26.halo_ref, f32[8,3,16,256]{3,2,1,0:T(8,128)S(1)} %bitcast.10, ...), custom_call_target="tpu_custom_call" | custom-call | tf_op jit(solution)/shard_map/stream_collide/pallas_call | solution.py:436
  56.6 0.0 copy-start.6
  56.6 0.0 copy-start.10
  56.6 14.4 %all_to_all.27.faces_ref = f32[8,48,256]{2,1,0:T(8,128)S(1)} all-to-all(f32[8,48,256]{2,1,0:T(8,128)S(1)} %get-tuple-element.15), channel_id=1, replica_groups=mesh['blk'=8,'gz'=4] {'blk'}, dimensions={0} | all-to-all | bytes 786432 | tf_op jit(solution)/shard_map/all_to_all | solution.py:412
  71.0 0.0 copy-done.6
  71.0 4.0 %all-to-all-start.4 = ((f32[8,8,16,128]{3,2,1,0:T(8,128)}), f32[8,8,16,128]{3,2,1,0:T(8,128)S(1)}, u32[]{:S(2)}, u32[]{:S(2)}) async-start(f32[8,8,16,128]{3,2,1,0:T(8,128)} %copy-done.6), calls=%async_computation.4 | async-start | bytes 1048576 | tf_op jit(solution)/shard_map/all_to_all | solution.py:457
  75.0 1.9 %collective-permute-start.3 = (f32[8,8,256]{2,1,0:T(8,128)S(1)}, f32[8,8,256]{2,1,0:T(8,128)S(1)}, u32[]{:S(2)}, u32[]{:S(2)}) collective-permute-start(f32[8,8,256]{2,1,0:T(8,128)S(1)} %get-tuple-element.20), channel_id=1, source_target_pairs={{0,1},{1,2},{2,3},{4,5},{5,6},{6,7},{8,9},{9,10},{10,11},{12,13},{... | collective-permute-start | bytes 196616 | tf_op jit(solution)/shard_map/ppermute | solution.py:414
  76.9 2.4 %collective-permute-start.2 = (f32[8,8,256]{2,1,0:T(8,128)S(1)}, f32[8,8,256]{2,1,0:T(8,128)S(1)}, u32[]{:S(2)}, u32[]{:S(2)}) collective-permute-start(f32[8,8,256]{2,1,0:T(8,128)S(1)} %get-tuple-element.21), channel_id=1, source_target_pairs={{1,0},{2,1},{3,2},{5,4},{6,5},{7,6},{9,8},{10,9},{11,10},{13,12},{... | collective-permute-start | bytes 196616 | tf_op jit(solution)/shard_map/ppermute | solution.py:413
  79.3 0.0 collective-permute-done.3.below_ref
  79.3 3.5 %collective-permute-done.2.above_ref = f32[8,8,256]{2,1,0:T(8,128)S(1)} collective-permute-done((f32[8,8,256]{2,1,0:T(8,128)S(1)}, f32[8,8,256]{2,1,0:T(8,128)S(1)}, u32[]{:S(2)}, u32[]{:S(2)}) %collective-permute-start.2) | collective-permute-done | bytes 65568 | tf_op jit(solution)/shard_map/ppermute | solution.py:413
  82.8 2.2 %route.3 = f32[8,48,256]{2,1,0:T(8,128)S(1)} custom-call(s32[64,6]{1,0:T(8,128)S(1)} %bitcast.14, s32[1]{0:T(128)} %bitcast.4.row_ref, f32[8,48,256]{2,1,0:T(8,128)S(1)} %all_to_all.27.faces_ref, f32[8,8,256]{2,1,0:T(8,128)S(1)} %collective-permute-done.2.above_ref, f32[8,8,256]{2,1,0:T(8,128)S(1)} %collective-permute-done.3.below_ref), custom_call_target="tpu_custom_call" | custom-call | tf_op jit(solution)/shard_map/route/pallas_call | solution.py:415
  85.0 0.0 copy-start.3
  85.0 0.7 copy-done.3
  85.7 2.7 %all-to-all-done.4.rows_ref = f32[8,8,16,128]{3,2,1,0:T(8,128)S(1)} async-done(((f32[8,8,16,128]{3,2,1,0:T(8,128)}), f32[8,8,16,128]{3,2,1,0:T(8,128)S(1)}, u32[]{:S(2)}, u32[]{:S(2)}) %all-to-all-start.4) | async-done | bytes 524320 | tf_op jit(solution)/shard_map/all_to_all | solution.py:457
  88.4 4.9 %all-to-all-start.3 = ((f32[8,48,256]{2,1,0:T(8,128)}), f32[8,48,256]{2,1,0:T(8,128)S(1)}, u32[]{:S(2)}, u32[]{:S(2)}) async-start(f32[8,48,256]{2,1,0:T(8,128)} %copy-done.3), calls=%async_computation.3 | async-start | bytes 786432 | tf_op jit(solution)/shard_map/all_to_all | solution.py:423
  93.3 0.0 copy-done.10
  93.3 6.7 %slab_rows.1 = (f32[48,16,128]{2,1,0:T(8,128)S(1)}, f32[2,48,128]{2,1,0:T(8,128)S(1)}, f32[2,48,128]{2,1,0:T(8,128)S(1)}) custom-call(s32[8]{0:T(128)S(1)} %copy-done.9, s32[1,64]{1,0:T(1,128)S(1)} %copy-done.10, s32[1]{0:T(128)} %bitcast.6.slab_ref, f32[8,8,16,128]{3,2,1,0:T(8,128)S(1)} %all-to-all-done.4.rows_ref), custom_call_target="tpu_custom_call" | custom-call | tf_op jit(solution)/shard_map/slab_rows/pallas_call | solution.py:459
  100.0 1.9 %collective-permute-start.4 = (f32[2,48,128]{2,1,0:T(8,128)S(1)}, f32[2,48,128]{2,1,0:T(8,128)S(1)}, u32[]{:S(2)}, u32[]{:S(2)}) collective-permute-start(f32[2,48,128]{2,1,0:T(8,128)S(1)} %get-tuple-element.18), channel_id=1, source_target_pairs={{0,1},{1,2},{2,3},{4,5},{5,6},{6,7},{8,9},{9,10},{10,11},{12,13},{... | collective-permute-start | bytes 147464 | tf_op jit(solution)/shard_map/ppermute | solution.py:468
  101.9 2.4 %collective-permute-start.5 = (f32[2,48,128]{2,1,0:T(8,128)S(1)}, f32[2,48,128]{2,1,0:T(8,128)S(1)}, u32[]{:S(2)}, u32[]{:S(2)}) collective-permute-start(f32[2,48,128]{2,1,0:T(8,128)S(1)} %get-tuple-element.19), channel_id=1, source_target_pairs={{1,0},{2,1},{3,2},{5,4},{6,5},{7,6},{9,8},{10,9},{11,10},{13,12},{... | collective-permute-start | bytes 147464 | tf_op jit(solution)/shard_map/ppermute | solution.py:469
  104.3 0.0 collective-permute-done.4.below_ref
  104.4 3.0 %collective-permute-done.5.above_ref = f32[2,48,128]{2,1,0:T(8,128)S(1)} collective-permute-done((f32[2,48,128]{2,1,0:T(8,128)S(1)}, f32[2,48,128]{2,1,0:T(8,128)S(1)}, u32[]{:S(2)}, u32[]{:S(2)}) %collective-permute-start.5) | collective-permute-done | bytes 49184 | tf_op jit(solution)/shard_map/ppermute | solution.py:469
  107.3 1.8 %slab_depth.1 = f32[48,16,128]{2,1,0:T(8,128)} custom-call(s32[8]{0:T(128)S(1)} %copy-done.9, s32[1]{0:T(128)} %bitcast.6.slab_ref, f32[48,16,128]{2,1,0:T(8,128)S(1)} %get-tuple-element.17.rows_ref, f32[2,48,128]{2,1,0:T(8,128)S(1)} %collective-permute-done.4.below_ref, f32[2,48,128]{2,1,0:T(8,128)S(1)} %collective-permute-done.5.above_ref), custom_call_target="tpu_custom_call" | custom-call | tf_op jit(solution)/shard_map/slab_depth/pallas_call | solution.py:470
  109.1 0.0 all-to-all-done.3.halo_ref
  109.1 4.0 %stream_last.1 = f32[8,19,16,256]{3,2,1,0:T(8,128)} custom-call(f32[8,19,16,256]{3,2,1,0:T(8,128)S(1)} %get-tuple-element.14.before_ref, f32[8,48,256]{2,1,0:T(8,128)S(1)} %all-to-all-done.3.halo_ref), custom_call_target="tpu_custom_call" | custom-call | tf_op jit(solution)/shard_map/stream_last/pallas_call | solution.py:478
  (2 shorter events, 0.0 us)
Async XLA Ops:
  0.6 30.9 %copy-start.11 = (s32[1,64,6]{1,0,2:T(1,128)S(1)}, s32[1,64,6]{1,0,2:T(1,128)}, u32[]{:S(2)}) copy-start(s32[1,64,6]{1,0,2:T(1,128)} %param.10) | copy-start | bytes 4612
  0.6 1.7 %copy-start = (f32[1,8,19,16,256]{4,3,2,1,0:T(8,128)S(1)}, f32[1,8,19,16,256]{4,3,2,1,0:T(8,128)}, u32[]{:S(2)}) copy-start(f32[1,8,19,16,256]{4,3,2,1,0:T(8,128)} %param.6) | copy-start | bytes 7471108
  2.4 1.0 copy-start.4
  3.3 0.9 copy-start.7
  4.3 46.5 %copy-start.5 = (f32[1,8,3,16,256]{4,3,2,1,0:T(8,128)S(1)}, f32[1,8,3,16,256]{4,3,2,1,0:T(8,128)}, u32[]{:S(2)}) copy-start(f32[1,8,3,16,256]{4,3,2,1,0:T(8,128)} %param.7) | copy-start | bytes 1179652
  4.3 46.5 %copy-start.8 = (f32[1,8,16,256]{3,2,1,0:T(8,128)S(1)}, f32[1,8,16,256]{3,2,1,0:T(8,128)}, u32[]{:S(2)}) copy-start(f32[1,8,16,256]{3,2,1,0:T(8,128)} %param.8) | copy-start | bytes 393220
  4.3 46.5 %copy-start.9 = (s32[8]{0:T(128)S(1)}, s32[8]{0:T(128)}, u32[]{:S(2)}) copy-start(s32[8]{0:T(128)} %owner_ref.5) | copy-start | bytes 100
  5.9 1.5 %copy-start.1 = (f32[8,19,16,256]{3,2,1,0:T(8,128)}, f32[8,19,16,256]{3,2,1,0:T(8,128)S(1)}, u32[]{:S(2)}) copy-start(f32[8,19,16,256]{3,2,1,0:T(8,128)S(1)} %get-tuple-element.11.before_ref) | copy-start | bytes 7471108
  23.9 7.8 %collective-permute-start.1 = (f32[8,8,256]{2,1,0:T(8,128)S(1)}, f32[8,8,256]{2,1,0:T(8,128)S(1)}, u32[]{:S(2)}, u32[]{:S(2)}) collective-permute-start(f32[8,8,256]{2,1,0:T(8,128)S(1)} %get-tuple-element.22), channel_id=1, source_target_pairs={{0,1},{1,2},{2,3},{4,5},{5,6},{6,7},{8,9},{9,10},{10,11},{12,13},{... | collective-permute-start | bytes 196616 | tf_op jit(solution)/shard_map/ppermute | solution.py:414
  29.6 5.6 %collective-permute-start = (f32[8,8,256]{2,1,0:T(8,128)S(1)}, f32[8,8,256]{2,1,0:T(8,128)S(1)}, u32[]{:S(2)}, u32[]{:S(2)}) collective-permute-start(f32[8,8,256]{2,1,0:T(8,128)S(1)} %get-tuple-element.23), channel_id=1, source_target_pairs={{1,0},{2,1},{3,2},{5,4},{6,5},{7,6},{9,8},{10,9},{11,10},{13,12},{... | collective-permute-start | bytes 196616 | tf_op jit(solution)/shard_map/ppermute | solution.py:413
  50.8 1.7 %copy-start.2 = (f32[8,19,16,256]{3,2,1,0:T(8,128)S(1)}, f32[8,19,16,256]{3,2,1,0:T(8,128)}, u32[]{:S(2)}) copy-start(f32[8,19,16,256]{3,2,1,0:T(8,128)} %copy-done.1) | copy-start | bytes 7471108
  56.6 14.4 %copy-start.6 = (f32[8,8,16,128]{3,2,1,0:T(8,128)}, f32[8,8,16,128]{3,2,1,0:T(8,128)S(1)}, u32[]{:S(2)}) copy-start(f32[8,8,16,128]{3,2,1,0:T(8,128)S(1)} %get-tuple-element.16) | copy-start | bytes 1572868
  56.6 36.7 %copy-start.10 = (s32[1,64]{1,0:T(1,128)S(1)}, s32[1,64]{1,0:T(1,128)}, u32[]{:S(2)}) copy-start(s32[1,64]{1,0:T(1,128)} %column_ref.1) | copy-start | bytes 772
  71.0 17.4 %all-to-all-start.4 = ((f32[8,8,16,128]{3,2,1,0:T(8,128)}), f32[8,8,16,128]{3,2,1,0:T(8,128)S(1)}, u32[]{:S(2)}, u32[]{:S(2)}) async-start(f32[8,8,16,128]{3,2,1,0:T(8,128)} %copy-done.6), calls=%async_computation.4 | async-start | bytes 1048576 | tf_op jit(solution)/shard_map/all_to_all | solution.py:457
  75.0 4.3 %collective-permute-start.3 = (f32[8,8,256]{2,1,0:T(8,128)S(1)}, f32[8,8,256]{2,1,0:T(8,128)S(1)}, u32[]{:S(2)}, u32[]{:S(2)}) collective-permute-start(f32[8,8,256]{2,1,0:T(8,128)S(1)} %get-tuple-element.20), channel_id=1, source_target_pairs={{0,1},{1,2},{2,3},{4,5},{5,6},{6,7},{8,9},{9,10},{10,11},{12,13},{... | collective-permute-start | bytes 196616 | tf_op jit(solution)/shard_map/ppermute | solution.py:414
  76.9 5.9 %collective-permute-start.2 = (f32[8,8,256]{2,1,0:T(8,128)S(1)}, f32[8,8,256]{2,1,0:T(8,128)S(1)}, u32[]{:S(2)}, u32[]{:S(2)}) collective-permute-start(f32[8,8,256]{2,1,0:T(8,128)S(1)} %get-tuple-element.21), channel_id=1, source_target_pairs={{1,0},{2,1},{3,2},{5,4},{6,5},{7,6},{9,8},{10,9},{11,10},{13,12},{... | collective-permute-start | bytes 196616 | tf_op jit(solution)/shard_map/ppermute | solution.py:413
  85.0 0.7 copy-start.3
  88.4 20.7 %all-to-all-start.3 = ((f32[8,48,256]{2,1,0:T(8,128)}), f32[8,48,256]{2,1,0:T(8,128)S(1)}, u32[]{:S(2)}, u32[]{:S(2)}) async-start(f32[8,48,256]{2,1,0:T(8,128)} %copy-done.3), calls=%async_computation.3 | async-start | bytes 786432 | tf_op jit(solution)/shard_map/all_to_all | solution.py:423
  100.0 4.3 %collective-permute-start.4 = (f32[2,48,128]{2,1,0:T(8,128)S(1)}, f32[2,48,128]{2,1,0:T(8,128)S(1)}, u32[]{:S(2)}, u32[]{:S(2)}) collective-permute-start(f32[2,48,128]{2,1,0:T(8,128)S(1)} %get-tuple-element.18), channel_id=1, source_target_pairs={{0,1},{1,2},{2,3},{4,5},{5,6},{6,7},{8,9},{9,10},{10,11},{12,13},{... | collective-permute-start | bytes 147464 | tf_op jit(solution)/shard_map/ppermute | solution.py:468
  101.9 5.4 %collective-permute-start.5 = (f32[2,48,128]{2,1,0:T(8,128)S(1)}, f32[2,48,128]{2,1,0:T(8,128)S(1)}, u32[]{:S(2)}, u32[]{:S(2)}) collective-permute-start(f32[2,48,128]{2,1,0:T(8,128)S(1)} %get-tuple-element.19), channel_id=1, source_target_pairs={{1,0},{2,1},{3,2},{5,4},{6,5},{7,6},{9,8},{10,9},{11,10},{13,12},{... | collective-permute-start | bytes 147464 | tf_op jit(solution)/shard_map/ppermute | solution.py:469

commit v2 on v1

v2 whole, which is shorter than its diff:
```python
import functools

import jax
import jax.numpy as jnp
import numpy as np
from jax import lax
from jax.experimental import pallas as pl
from jax.experimental.pallas import tpu as pltpu
from jax.sharding import PartitionSpec as P

STEPS = 2
VELOCITIES = [
    (0, 0, 0),
    (1, 0, 0),
    (-1, 0, 0),
    (0, 1, 0),
    (0, -1, 0),
    (0, 0, 1),
    (0, 0, -1),
    (1, 1, 0),
    (-1, -1, 0),
    (1, -1, 0),
    (-1, 1, 0),
    (1, 0, 1),
    (-1, 0, -1),
    (1, 0, -1),
    (-1, 0, 1),
    (0, 1, 1),
    (0, -1, -1),
    (0, 1, -1),
    (0, -1, 1),
]
POPS = 19
EAST_POPS = [1, 7, 9, 11, 13]
WEST_POPS = [2, 8, 10, 12, 14]
NORTH_POPS = [7, 10, 15, 17]
SOUTH_POPS = [8, 9, 16, 18]
UPPER_POPS = [5, 11, 14, 15, 18]
LOWER_POPS = [6, 12, 13, 16, 17]
RELAX_RATE = 1.25
DRAG_RATE = 0.3
TAP_EDGE, TAP_NEAR = 1.0 / 3.0, 2.0 / 3.0

FACE_ROWS = 40
FIRST, SECOND = 24, 32
SOUTH = 64


def dev_of(slot, blocks):
    return lax.div(jnp.maximum(slot, 0), jnp.int32(blocks))


def shift(value, amount, axis=1):
    amount = amount % value.shape[axis]
    return value if amount == 0 else pltpu.roll(value, amount, axis)


def lanes(shape):
    return lax.broadcasted_iota(jnp.int32, shape, len(shape) - 1)


def collide_cells(f, u, porosity):
    total, gap = {}, {}
    for i in range(1, POPS, 2):
        total[i], gap[i] = f[i] + f[i + 1], f[i] - f[i + 1]
    ux, uy, uz = u
    mx = gap[1] + gap[7] + gap[9] + gap[11] + gap[13]
    my = gap[3] + gap[7] - gap[9] + gap[15] + gap[17]
    mz = gap[5] + gap[11] - gap[13] + gap[15] - gap[17]
    xy_sum, xz_sum, yz_sum = total[7] + total[9], total[11] + total[13], total[15] + total[17]
    xx = 2.0 * total[1] + xy_sum + xz_sum
    yy = 2.0 * total[3] + xy_sum + yz_sum
    zz = 2.0 * total[5] + xz_sum + yz_sum
    xy, xz, yz = total[7] - total[9], total[11] - total[13], total[15] - total[17]
    mass = 12.0 * f[0] + 2.0 * (total[1] + total[3] + total[5]) + (xy_sum + xz_sum + yz_sum)
    speed_sq = ux * ux + uy * uy + uz * uz
    qx = xx * ux + xy * uy + xz * uz
    qy = xy * ux + yy * uy + yz * uz
    qz = xz * ux + yz * uy + zz * uz
    sens = ux * mx + uy * my + uz * mz
    drag = DRAG_RATE * porosity
    scale = RELAX_RATE / 36.0
    quad = ux * qx + uy * qy + uz * qz
    base = scale * (mass + 1.5 * (speed_sq * mass) - 4.5 * quad) + drag * sens
    gx = (3.0 * scale) * (mx + gap[1] + 3.0 * qx - ux * mass) - drag * mx
    gy = (3.0 * scale) * (my + gap[3] + 3.0 * qy - uy * mass) - drag * my
    gz = (3.0 * scale) * (mz + gap[5] + 3.0 * qz - uz * mass) - drag * mz
    along = {1: gx, 3: gy, 5: gz, 7: gx + gy, 9: gx - gy, 11: gx + gz, 13: gx - gz, 15: gy + gz, 17: gy - gz}
    keep = 1.0 - RELAX_RATE
    post = [base + keep * f[0]]
    for i in range(1, POPS, 2):
        post.append(base + along[i] + keep * f[i])
        post.append(base - along[i] + keep * f[i + 1])
    return post, sens


def collide_block(read, velocity_ref, porosity_ref, post_ref, edge, plane):
    parts = {}
    for low in range(0, edge, 8):
        for left in range(0, plane, 128):
            zs, cells = pl.ds(low, 8), pl.ds(left, 128)
            post, sens = collide_cells(
                [read(p, zs, cells) for p in range(POPS)],
                [velocity_ref[c, zs, cells] for c in range(3)],
                porosity_ref[zs, cells],
            )
            for p in range(POPS):
                post_ref[p, zs, cells] = post[p]
            parts[low, left] = sens
    return parts


def pack_faces(block, blocks, swapped, post_ref, faces_ref, edge, plane):
    def put_ends(target, row, cells, low, high):
        faces_ref[target, FIRST + row : FIRST + row + 1, cells] = jnp.where(swapped, high, low)
        faces_ref[target, SECOND + row : SECOND + row + 1, cells] = jnp.where(swapped, low, high)

    every = slice(0, plane)
    slot = lanes((edge, plane)) % edge
    x_tile = jnp.zeros((edge, plane), jnp.float32)
    for s, p in enumerate(EAST_POPS):
        x_tile = jnp.where(slot == s, shift(post_ref[p], s), x_tile)
    for s, p in enumerate(WEST_POPS):
        x_tile = jnp.where(slot == 5 + s, shift(post_ref[p], 5 + s - (edge - 1)), x_tile)
    faces_ref[block, 0:16, :] = x_tile
    for i in range(5):
        put_ends(block, i, every, post_ref[UPPER_POPS[i], 0:1, :], post_ref[LOWER_POPS[i], edge - 1 : edge, :])
    put_ends(block, 5, every, x_tile[0:1], x_tile[edge - 1 : edge])
    group = lanes((edge, 128)) // edge
    north = jnp.zeros((edge, 128), jnp.float32)
    south = jnp.zeros((edge, 128), jnp.float32)
    for q in range(4):
        north = jnp.where(group == q, shift(post_ref[NORTH_POPS[q], :, 0:128], q * edge), north)
        south = jnp.where(
            group == 4 + q, shift(post_ref[SOUTH_POPS[q], :, plane - 128 : plane], (q + 5) * edge), south
        )

    def put_y(target, tile, start, pop, left, first, row):
        for half in range(2):
            rows = tile[half * 8 : half * 8 + 8]
            at = half * 128
            faces_ref[target, 16:24, at + start : at + start + 64] = rows[:, start : start + 64]
            line = post_ref[pop, half * 8 : half * 8 + 8, left : left + 128]
            line = jnp.where(group[0:8] == first, line, 0.0)
            line = pltpu.roll(line, (128 - first * edge) % 128, 1, stride=edge, stride_axis=0)
            faces_ref[target, row + 7 : row + 8, at : at + 128] = jnp.sum(line, axis=0, keepdims=True)
        put_ends(target, 6, slice(start, start + 64), tile[0:1, start : start + 64], tile[edge - 1 : edge, start : start + 64])

    @pl.when(block > 0)
    def _():
        put_y(block - 1, north, 0, 3, 0, 0, FIRST)

    @pl.when(block < blocks - 1)
    def _():
        put_y(block + 1, south, SOUTH, 4, plane - 128, 7, SECOND)


def first_partner_above():
    return lax.rem(lax.axis_index("gz").astype(jnp.int32), jnp.int32(2)) == 0


def stream_pop(p, source, halo_ref, edge, plane):
    cx, cy, cz = VELOCITIES[p]
    lane = lanes((edge, plane))
    value = shift(source, -(cx + edge * cy))
    if cx != 0:
        face = edge - 1 if cx > 0 else 0
        s = EAST_POPS.index(p) if cx > 0 else 5 + WEST_POPS.index(p)
        arrived = shift(halo_ref[0:16, :], face - s - edge * cy)
        value = jnp.where(lane % edge == face, arrived, value)
    if cy != 0:
        face = 7 if cy > 0 else 0
        if p in (3, 4):
            row = (FIRST if cy > 0 else SECOND) + 7
            lined = lax.broadcasted_iota(jnp.int32, (8, 128), 0) == lane[0:8, 0:128] // edge
            arrived = [jnp.where(lined, halo_ref[row : row + 1, at : at + 128], 0.0) for at in (0, 128)]
            for step in (4, 2, 1):
                arrived = [part + shift(part, step * edge) for part in arrived]
        else:
            start = NORTH_POPS.index(p) * edge if cy > 0 else SOUTH + SOUTH_POPS.index(p) * edge
            arrived = [shift(halo_ref[16:24, at : at + 128], face * edge - start) for at in (0, 128)]
        arrived = jnp.concatenate(arrived, axis=0)
        halves = [value[:, side : side + 128] for side in range(0, plane, 128)]
        at = -1 if cy > 0 else 0
        halves[at] = jnp.where(lane[:, 0:128] // edge == face, arrived, halves[at])
        value = jnp.concatenate(halves, axis=1)
    if cz != 0:
        face = edge - 1 if cz > 0 else 0
        row = FIRST + UPPER_POPS.index(p) if cz > 0 else SECOND + LOWER_POPS.index(p)
        arrived = halo_ref[row : row + 1, :]
        depth = lax.broadcasted_iota(jnp.int32, (edge, plane), 0)
        value = jnp.where(depth == face, arrived, shift(value, -cz, 0))
    return value


def first_kernel(
    blocks,
    state_hbm,
    velocity_hbm,
    porosity_hbm,
    post_hbm,
    faces_ref,
    state_ref,
    velocity_ref,
    porosity_ref,
    post_ref,
    sems,
):
    edge, plane = porosity_ref.shape[1:]
    swapped = first_partner_above()

    def copies(b):
        return (
            pltpu.make_async_copy(state_hbm.at[b], state_ref.at[b], sems.at[0, b]),
            pltpu.make_async_copy(velocity_hbm.at[b], velocity_ref.at[b], sems.at[1, b]),
            pltpu.make_async_copy(porosity_hbm.at[b], porosity_ref.at[b], sems.at[2, b]),
        )

    def result(b):
        return pltpu.make_async_copy(post_ref.at[b], post_hbm.at[b], sems.at[3, b])

    for b in range(blocks):
        for copy in copies(b):
            copy.start()

    def one(b, carry):
        for copy in copies(b):
            copy.wait()
        parts = collide_block(
            lambda p, zs, cells: state_ref[b, p, zs, cells],
            velocity_ref.at[b],
            porosity_ref.at[b],
            post_ref.at[b],
            edge,
            plane,
        )
        for (low, left), sens in parts.items():
            post_ref[b, POPS, pl.ds(low, 8), pl.ds(left, 128)] = sens
        result(b).start()
        pack_faces(b, blocks, swapped, post_ref.at[b], faces_ref, edge, plane)
        return carry

    lax.fori_loop(0, blocks, one, 0)
    for b in range(blocks):
        result(b).wait()


def slab_start(owner_ref, slab, devices):
    start = jnp.int32(0)
    for j in range(devices):
        start = start + jnp.where(j < slab, 2 * owner_ref[j], 0)
    return start


def second_kernel(
    blocks,
    devices,
    chunks,
    owner_ref,
    before_hbm,
    velocity_hbm,
    porosity_hbm,
    halo_ref,
    post_hbm,
    faces_ref,
    before_ref,
    velocity_ref,
    porosity_ref,
    post_ref,
    state_ref,
    field_ref,
    sems,
):
    edge, plane = porosity_ref.shape[1:]
    swapped = first_partner_above()

    def copies(b):
        return (
            pltpu.make_async_copy(before_hbm.at[b], before_ref.at[b], sems.at[0, b]),
            pltpu.make_async_copy(velocity_hbm.at[b], velocity_ref.at[b], sems.at[1, b]),
            pltpu.make_async_copy(porosity_hbm.at[b], porosity_ref.at[b], sems.at[2, b]),
        )

    def result(b):
        return pltpu.make_async_copy(post_ref.at[b], post_hbm.at[b], sems.at[3, b])

    for b in range(blocks):
        for copy in copies(b):
            copy.start()

    def one(b, carry):
        for copy in copies(b):
            copy.wait()
        for p in range(POPS):
            state_ref[p] = stream_pop(p, before_ref[b, p], halo_ref.at[b], edge, plane)
        parts = collide_block(
            lambda p, zs, cells: state_ref[p, zs, cells],
            velocity_ref.at[b],
            porosity_ref.at[b],
            post_ref.at[b],
            edge,
            plane,
        )
        result(b).start()
        for (low, left), sens in parts.items():
            field_ref[b * (plane // 128) + left // 128, pl.ds(low, 8), :] = (
                before_ref[b, POPS, pl.ds(low, 8), pl.ds(left, 128)] + sens
            )
        pack_faces(b, blocks, swapped, post_ref.at[b], faces_ref, edge, plane)
        return carry

    lax.fori_loop(0, blocks, one, 0)
    held = blocks * (plane // 128)
    start = jnp.int32(0)
    lane = lanes((edge, 128))
    for j in range(devices):
        first = lax.div(start + 6, jnp.int32(8)) - 1
        behind = (start - 2 - 8 * first) * edge
        turned = [
            pltpu.roll(field_ref[jnp.clip(first + i, 0, held - 1)], lax.rem(128 - behind, jnp.int32(128)), 1)
            for i in range(chunks + 1)
        ]
        for i in range(chunks):
            value = jnp.where(lane < 128 - behind, turned[i], turned[i + 1])
            at = FACE_ROWS + 8 * i
            faces_ref[j, at : at + 8, 0:128] = value[0:8]
            faces_ref[j, at : at + 8, 128:256] = value[8:16]
        start = start + 2 * owner_ref[j]
    for b in range(blocks):
        result(b).wait()


def last_kernel(blocks, before_hbm, halo_ref, out_hbm, before_ref, out_ref, sems):
    edge, plane = before_ref.shape[2:]

    def copy(b):
        return pltpu.make_async_copy(before_hbm.at[b], before_ref.at[b], sems.at[0, b])

    def result(b):
        return pltpu.make_async_copy(out_ref.at[b], out_hbm.at[b], sems.at[1, b])

    for b in range(blocks):
        copy(b).start()

    def one(b, carry):
        copy(b).wait()
        for p in range(POPS):
            out_ref[b, p] = stream_pop(p, before_ref[b, p], halo_ref.at[b], edge, plane)
        result(b).start()
        return carry

    lax.fori_loop(0, blocks, one, 0)
    for b in range(blocks):
        result(b).wait()


def route_kernel(blocks, devices, table_ref, faces_ref, first_ref, second_ref, halo_ref):
    row = jnp.minimum(lax.axis_index("blk").astype(jnp.int32), blocks - 1)
    swapped = first_partner_above()
    edge, plane = 16, faces_ref.shape[2]
    slot = lanes((edge, plane)) % edge
    line = lanes((1, plane))
    lane = lanes((8, plane)) % 128
    from_north = lane < SOUTH
    in_east = (lane < edge) | ((lane >= SOUTH + edge) & (lane < SOUTH + 2 * edge))
    in_west = ((lane >= edge) & (lane < 2 * edge)) | ((lane >= SOUTH) & (lane < SOUTH + edge))
    dev = functools.partial(dev_of, blocks=blocks)

    def beside(slot_id, face):
        return jnp.where(slot_id < 0, -1, table_ref[jnp.maximum(slot_id, 0), face])

    def one(d, carry):
        here = d * blocks + row
        west, east, south, north, below, above = [table_ref[here, face] for face in range(6)]
        zero = jnp.float32(0.0)
        halo_ref[d, 0:16, :] = jnp.where(
            slot < 5,
            jnp.where(east >= 0, faces_ref[dev(east), 0:16, :], zero),
            jnp.where(west >= 0, faces_ref[dev(west), 0:16, :], zero),
        )

        def y_tile(north_slot, south_slot):
            n = jnp.where(north_slot >= 0, faces_ref[dev(north_slot), 16:24, :], zero)
            s = jnp.where(south_slot >= 0, faces_ref[dev(south_slot), 16:24, :], zero)
            return jnp.where(from_north, n, s)

        own = y_tile(north, south)
        far_east = y_tile(beside(north, 1), beside(south, 1))
        far_west = y_tile(beside(north, 0), beside(south, 0))
        east_part = jnp.where(lane % edge == edge - 1, shift(far_east, edge - 1), shift(own, -1))
        west_part = jnp.where(lane % edge == 0, shift(far_west, 1 - edge), shift(own, 1))
        halo_ref[d, 16:24, :] = jnp.where(in_east, east_part, jnp.where(in_west, west_part, own))
        for slot_id, r in ((north, FIRST + 7), (south, SECOND + 7)):
            halo_ref[d, r : r + 1, :] = jnp.where(slot_id >= 0, faces_ref[dev(slot_id), r : r + 1, :], zero)

        def z_face(from_first, where_from, face, pops, row0):
            def rows(slot_id, r):
                first, second = [ref[dev(slot_id), r : r + 1, :] for ref in (first_ref, second_ref)]
                return jnp.where(slot_id >= 0, jnp.where(from_first, first, second), zero)

            from_x = {1: rows(beside(east, face), 5), -1: rows(beside(west, face), 5)}
            from_y = {1: rows(beside(north, face), 6), -1: rows(beside(south, face), 6)}
            for i, p in enumerate(pops):
                cx, cy, _ = VELOCITIES[p]
                value = shift(rows(where_from, i), -(cx + edge * cy))
                if cx != 0:
                    at = edge - 1 if cx > 0 else 0
                    s = EAST_POPS.index(p) if cx > 0 else 5 + WEST_POPS.index(p)
                    value = jnp.where(line % edge == at, shift(from_x[cx], at - s), value)
                if cy != 0:
                    at = edge - 1 if cy > 0 else 0
                    start = NORTH_POPS.index(p) * edge if cy > 0 else SOUTH + SOUTH_POPS.index(p) * edge
                    value = jnp.where(line // edge == at, shift(from_y[cy], at * edge - start), value)
                halo_ref[d, row0 + i : row0 + i + 1, :] = value

        z_face(swapped, above, 5, UPPER_POPS, FIRST)
        z_face(jnp.logical_not(swapped), below, 4, LOWER_POPS, SECOND)
        return carry

    lax.fori_loop(0, devices, one, 0, unroll=4)


def slab_kernel(
    blocks, devices, chunks, owner_ref, column_ref, rows_ref, out_ref, first_ref, second_ref, field_ref
):
    slab = lax.axis_index("blk").astype(jnp.int32)
    swapped = first_partner_above()
    count, edge, width = out_ref.shape
    start = slab_start(owner_ref, slab, devices)
    group = lanes((edge, width)) // edge
    lane = lanes((edge, width))
    height = blocks * edge

    def chunk(i, carry):
        top = start - 2 + 8 * i
        tiles = [jnp.zeros((edge, width), jnp.float32) for _ in range(8)]
        at = pl.multiple_of(FACE_ROWS + 8 * i, 8)
        values = [
            jnp.concatenate([rows_ref[e, pl.ds(at, 8), 0:128], rows_ref[e, pl.ds(at, 8), 128:256]], axis=0)
            for e in range(devices)
        ]
        for r in range(0, 8, 2):
            inside = (top + r >= 0) & (top + r < height)
            block_row = lax.div(jnp.clip(top + r, 0, height - 1), jnp.int32(edge))
            for e in range(devices):
                column = column_ref[0, e * blocks + block_row]
                hit = group == jnp.where(inside, column, -1)
                for k in range(r, r + 2):
                    part = pltpu.roll(values[e], lax.rem(column + (8 - k), jnp.int32(8)) * edge, 1)
                    if width > 128:
                        part = jnp.concatenate([part] * (width // 128), axis=1)
                    tiles[k] = jnp.where(hit, part, tiles[k])
        for r in range(8):
            field_ref[i * 8 + r] = tiles[r]
        return carry

    lax.fori_loop(0, chunks, chunk, 0)

    def row(r):
        at = r
        mixed = TAP_EDGE * (field_ref[at] + field_ref[at + 4]) + (
            TAP_NEAR * (field_ref[at + 1] + field_ref[at + 3]) + field_ref[at + 2]
        )
        value = mixed
        for step, tap in ((1, TAP_NEAR), (2, TAP_EDGE)):
            left = jnp.where(lane >= step, shift(mixed, step), 0.0)
            right = jnp.where(lane < width - step, shift(mixed, -step), 0.0)
            value = value + tap * (left + right)
        out_ref[r] = value
        low, high = value[0:2], value[edge - 2 : edge]
        first_ref[r] = jnp.where(swapped, high, low)
        second_ref[r] = jnp.where(swapped, low, high)

    by_rows(count, row)


def by_rows(count, body):
    step = 8 if count % 8 == 0 else 4 if count % 4 == 0 else 2

    def several(i, carry):
        for k in range(step):
            body(i * step + k)
        return carry

    lax.fori_loop(0, count // step, several, 0)


def depth_kernel(devices, layers, owner_ref, rows_ref, first_ref, second_ref, out_ref):
    count, edge, width = out_ref.shape
    slab, layer = lax.axis_index("blk").astype(jnp.int32), lax.axis_index("gz").astype(jnp.int32)
    own_rows = jnp.int32(0)
    for j in range(devices):
        own_rows = jnp.where(slab == j, 2 * owner_ref[j], own_rows)
    swapped = first_partner_above()
    depth = lax.broadcasted_iota(jnp.int32, (edge, width), 0)

    def row(r):
        value = rows_ref[r]
        first, second = first_ref[r], second_ref[r]
        below = jnp.where(layer > 0, jnp.where(swapped, second, first), 0.0)
        above = jnp.where(layer < layers - 1, jnp.where(swapped, first, second), 0.0)
        b0, b1, a0, a1 = below[0:1], below[1:2], above[0:1], above[1:2]
        down = jnp.where(depth == 0, b1, shift(value, 1, 0))
        up = jnp.where(depth == edge - 1, a0, shift(value, -1, 0))
        down_2 = jnp.where(depth == 0, b0, jnp.where(depth == 1, b1, shift(value, 2, 0)))
        up_2 = jnp.where(depth == edge - 1, a1, jnp.where(depth == edge - 2, a0, shift(value, -2, 0)))
        total = value + TAP_NEAR * (down + up) + TAP_EDGE * (down_2 + up_2)
        out_ref[r] = jnp.where(r < own_rows, total, 0.0)

    by_rows(count, row)


SMEM = pl.BlockSpec(memory_space=pltpu.SMEM)
VMEM = pl.BlockSpec(memory_space=pltpu.VMEM)


ANY = pl.BlockSpec(memory_space=pl.ANY)


def f32(*shape):
    return jax.ShapeDtypeStruct(shape, jnp.float32)


def hbm(*shape):
    return pltpu.HBM(shape, jnp.float32)


def vmem(*shape):
    return pltpu.VMEM(shape, jnp.float32)


def local(adjoint, velocity, porosity, block_x, neighbours, owner_map):
    blocks, _, edge, plane = adjoint.shape[1:]
    devices, layers = lax.axis_size("blk"), lax.axis_size("gz")
    table = neighbours[0]
    state, flow, design = [pltpu.with_memory_space_constraint(x[0], pltpu.HBM) for x in (adjoint, velocity, porosity)]
    rows_cap = 2 * (3 * (blocks * edge // 2) // devices)
    chunks = -(-(rows_cap + 4) // 8)
    width = devices * edge
    first_pairs = [(g, g ^ 1) for g in range(layers)]
    second_pairs = [(g, (g + 1 if g % 2 else g - 1) % layers) for g in range(layers)]
    faces_shape = (devices, FACE_ROWS, plane)
    post_shape = (blocks, POPS + 1, edge, plane)
    params = pltpu.CompilerParams(vmem_limit_bytes=32 * 1024 * 1024)

    def to_halo(gathered):
        first = lax.ppermute(gathered[:, FIRST : FIRST + 8], "gz", first_pairs)
        second = lax.ppermute(gathered[:, SECOND : SECOND + 8], "gz", second_pairs)
        halo = pl.pallas_call(
            functools.partial(route_kernel, blocks, devices),
            out_shape=f32(*faces_shape),
            in_specs=[SMEM, VMEM, VMEM, VMEM],
            out_specs=VMEM,
            compiler_params=params,
            name="route",
        )(table, gathered, first, second)
        return lax.all_to_all(halo, "blk", 0, 0, tiled=True)

    inputs = [vmem(*state.shape), vmem(*flow.shape), vmem(*design.shape)]
    post, faces = pl.pallas_call(
        functools.partial(first_kernel, blocks),
        out_shape=(hbm(*post_shape), f32(*faces_shape)),
        in_specs=[ANY] * 3,
        out_specs=(ANY, VMEM),
        scratch_shapes=inputs + [vmem(*post_shape), pltpu.SemaphoreType.DMA((4, blocks))],
        compiler_params=params,
        name="collide_first",
    )(state, flow, design)
    halo = to_halo(lax.all_to_all(faces, "blk", 0, 0, tiled=True))
    post, faces = pl.pallas_call(
        functools.partial(second_kernel, blocks, devices, chunks),
        out_shape=(hbm(*state.shape), f32(devices, FACE_ROWS + 8 * chunks, plane)),
        in_specs=[SMEM] + [ANY] * 3 + [VMEM],
        out_specs=(ANY, VMEM),
        scratch_shapes=[vmem(*post_shape)]
        + inputs[1:]
        + [
            vmem(*state.shape),
            vmem(POPS, edge, plane),
            vmem(blocks * plane // 128, edge, 128),
            pltpu.SemaphoreType.DMA((4, blocks)),
        ],
        compiler_params=params,
        name="stream_collide",
    )(owner_map, pltpu.with_memory_space_constraint(post, pltpu.HBM), flow, design, halo)
    gathered = lax.all_to_all(faces, "blk", 0, 0, tiled=True)
    halo = to_halo(gathered)
    slab_shape, ends = (rows_cap, edge, width), (rows_cap, 2, width)
    slab, first, second = pl.pallas_call(
        functools.partial(slab_kernel, blocks, devices, chunks),
        out_shape=(f32(*slab_shape), f32(*ends), f32(*ends)),
        in_specs=[SMEM, SMEM, VMEM],
        out_specs=(VMEM,) * 3,
        scratch_shapes=[vmem(chunks * 8, edge, width)],
        compiler_params=params,
        name="slab_rows",
    )(owner_map, block_x, gathered)
    first = lax.ppermute(first, "gz", first_pairs)
    second = lax.ppermute(second, "gz", second_pairs)
    smoothed = pl.pallas_call(
        functools.partial(depth_kernel, devices, layers),
        out_shape=f32(*slab_shape),
        in_specs=[SMEM, VMEM, VMEM, VMEM],
        out_specs=VMEM,
        compiler_params=params,
        name="slab_depth",
    )(owner_map, slab, first, second)
    moved = pl.pallas_call(
        functools.partial(last_kernel, blocks),
        out_shape=hbm(*state.shape),
        in_specs=[ANY, VMEM],
        out_specs=ANY,
        scratch_shapes=[vmem(*state.shape), vmem(*state.shape), pltpu.SemaphoreType.DMA((2, blocks))],
        compiler_params=params,
        name="stream_last",
    )(pltpu.with_memory_space_constraint(post, pltpu.HBM), halo)
    return (moved[None], smoothed[None, None])


def solution(mesh):
    placed = (
        P("gz", "blk", None, None, None),
        P("gz", "blk", None, None, None),
        P("gz", "blk", None, None),
        P("gz", None),
        P("gz", None, None),
        P(),
    )
    return jax.shard_map(
        local,
        mesh=mesh,
        in_specs=placed,
        out_specs=(P("gz", "blk", None, None, None), P("gz", "blk", None, None, None)),
        check_vma=False,
    )
```

time: 114 us -> 97.8 us (0.86)
  starting transfers between devices: 25.1 us -> 11.9 us
  local copies, waits for them, and re-layouts: 7.63 us -> 0.13 us
  blocking collectives: 44.3 us -> 50.5 us
  waiting for transfers between devices: 12.7 us -> 8.46 us
  Pallas kernels: 22.6 us -> 24.3 us
    ppermute x6, starting transfers between devices: 16.3 us -> 8.42 us  [the longest x2 6.75 us: to_halo(): second = lax.ppermute(gathered[:, SECOND:SECOND + 8], 'gz', second_pairs)]
    all_to_all x2, blocking collectives: 30.9 us -> 38.8 us  [the longest x1 23.6 us: local(): gathered = lax.all_to_all(faces, 'blk', 0, 0, tiled=True)]
    unnamed x25 -> x7, local copies, waits for them, and re-layouts: 7.61 us -> 0.11 us
    all_to_all x1 -> x0, starting transfers between devices: 3.98 us -> none  [local(): rows = lax.all_to_all(rows, 'blk', 0, 0, tiled=True)]
    pallas_call x1, Pallas kernels: 6.72 us -> 3.27 us  [local(): pl.pallas_call(functools.partial(slab_kernel, blocks, devices, chunks), o...]
    pallas_call x1, Pallas kernels: 4.03 us -> 6.77 us  [local(): pl.pallas_call(functools.partial(second_kernel, blocks, devices, chunks),...]
    all_to_all x1 -> x0, waiting for transfers between devices: 2.66 us -> none  [local(): rows = lax.all_to_all(rows, 'blk', 0, 0, tiled=True)]
    pallas_call x3, Pallas kernels: 7.42 us -> 9.82 us  [the longest x1 4.42 us: local(): pl.pallas_call(functools.partial(first_kernel, blocks), out_shape=(hbm(*p...]
  transfers between devices with their start and end apart: 8 -> 7, of which waited for: 4 -> 4; matrix products, arithmetic and copies ran while one was open for 0% -> 0% of each run, Pallas kernels for 9% -> 5%
where the time goes in v2:
time: 97.8 us; the launch traced here: 96 us
  blocking collectives  50.5 us (52%)
  Pallas kernels  24.3 us (25%)
  starting transfers between devices  11.9 us (12%)
  waiting for transfers between devices  8.46 us (9%)
    all_to_all x1, blocking collectives, local(): gathered = lax.all_to_all(faces, 'blk', 0, 0, tiled=True)  23.6 us
    all_to_all x1, blocking collectives, local(): halo = to_halo(lax.all_to_all(faces, 'blk', 0, 0, tiled=True))  15.1 us
    all_to_all x1, blocking collectives, to_halo(): return lax.all_to_all(halo, 'blk', 0, 0, tiled=True)  11.8 us
    pallas_call x1, Pallas kernels, local(): pl.pallas_call(functools.partial(second_kernel, blocks, devices, chunks),...  6.77 us
    ppermute x2, starting transfers between devices, to_halo(): second = lax.ppermute(gathered[:, SECOND:SECOND + 8], 'gz', second_pairs)  6.75 us
    ppermute x2, waiting for transfers between devices, to_halo(): second = lax.ppermute(gathered[:, SECOND:SECOND + 8], 'gz', second_pairs)  5.42 us
    pallas_call x1, Pallas kernels, local(): pl.pallas_call(functools.partial(first_kernel, blocks), out_shape=(hbm(*p...  4.42 us
    pallas_call x2, Pallas kernels, to_halo(): pl.pallas_call(functools.partial(route_kernel, blocks, devices), out_shap...  4.39 us
  transfers between devices with their start and end apart: 7, of which 4 were waited for; matrix products, arithmetic and copies ran while one was open for 0% of the time, Pallas kernels for 5%

profile of v2, /device:TPU:1, one launch (start us, length us, event | category | flops | bytes accessed | tf_op | source)
XLA Modules:
  0.0 96.0 jit_solution(5273356623566939145)
XLA Ops:
  0.6 0.0 copy-start.2
  0.6 0.0 copy-start
  0.6 4.4 %collide_first.1 = (f32[8,20,16,256]{3,2,1,0:T(8,128)}, f32[8,40,256]{2,1,0:T(8,128)S(1)}) custom-call(f32[8,19,16,256]{3,2,1,0:T(8,128)} %bitcast.8, f32[8,3,16,256]{3,2,1,0:T(8,128)} %bitcast.10, f32[8,16,256]{2,1,0:T(8,128)} %bitcast.12), custom_call_target="tpu_custom_call" | custom-call | tf_op jit(solution)/shard_map/collide_first/pallas_call | solution.py:560
  5.1 15.1 %all_to_all.20.faces_ref = f32[8,40,256]{2,1,0:T(8,128)S(1)} all-to-all(f32[8,40,256]{2,1,0:T(8,128)S(1)} %get-tuple-element.10), channel_id=1, replica_groups=mesh['blk'=8,'gz'=4] {'blk'}, dimensions={0} | all-to-all | bytes 655360 | tf_op jit(solution)/shard_map/all_to_all | solution.py:569
  20.2 4.1 %collective-permute-start.1 = (f32[8,8,256]{2,1,0:T(8,128)S(1)}, f32[8,8,256]{2,1,0:T(8,128)S(1)}, u32[]{:S(2)}, u32[]{:S(2)}) collective-permute-start(f32[8,8,256]{2,1,0:T(8,128)S(1)} %get-tuple-element.18), channel_id=1, source_target_pairs={{0,3},{1,2},{2,1},{3,0},{4,7},{5,6},{6,5},{7,4},{8,11},{9,10},{10,... | collective-permute-start | bytes 196616 | tf_op jit(solution)/shard_map/ppermute | solution.py:548
  24.3 0.0 collective-permute-start
  24.3 0.0 copy-done.2
  24.3 0.1 copy.8
  24.4 2.8 %collective-permute-done.1.second_ref = f32[8,8,256]{2,1,0:T(8,128)S(1)} collective-permute-done((f32[8,8,256]{2,1,0:T(8,128)S(1)}, f32[8,8,256]{2,1,0:T(8,128)S(1)}, u32[]{:S(2)}, u32[]{:S(2)}) %collective-permute-start.1) | collective-permute-done | bytes 65568 | tf_op jit(solution)/shard_map/ppermute | solution.py:548
  27.1 0.0 collective-permute-done.first_ref
  27.2 1.8 %route.2 = f32[8,40,256]{2,1,0:T(8,128)S(1)} custom-call(s32[64,6]{1,0:T(8,128)S(1)} %bitcast.6, f32[8,40,256]{2,1,0:T(8,128)S(1)} %all_to_all.20.faces_ref, f32[8,8,256]{2,1,0:T(8,128)S(1)} %collective-permute-done.first_ref, f32[8,8,256]{2,1,0:T(8,128)S(1)} %collective-permute-done.1.second_ref), custom_call_target="tpu_custom_call" | custom-call | tf_op jit(solution)/shard_map/route/pallas_call | solution.py:549
  29.0 11.8 %all_to_all.21.halo_ref = f32[8,40,256]{2,1,0:T(8,128)S(1)} all-to-all(f32[8,40,256]{2,1,0:T(8,128)S(1)} %route.2), channel_id=1, replica_groups=mesh['blk'=8,'gz'=4] {'blk'}, dimensions={0} | all-to-all | bytes 655360 | tf_op jit(solution)/shard_map/all_to_all | solution.py:557
  40.8 0.0 copy-done
  40.8 6.8 %stream_collide.1 = (f32[8,19,16,256]{3,2,1,0:T(8,128)}, f32[8,96,256]{2,1,0:T(8,128)S(1)}) custom-call(s32[8]{0:T(128)S(1)} %copy-done, f32[8,20,16,256]{3,2,1,0:T(8,128)} %get-tuple-element.9.before_hbm, f32[8,3,16,256]{3,2,1,0:T(8,128)} %bitcast.11, f32[8,16,256]{2,1,0:T(8,128)} %bitcast.13, f32[8,40,256]{2,1,0:T(8,128)S(1)} %all_to_all.21.halo_ref), custom_call_target="tpu_custom_call" | custom-call | tf_op jit(solution)/shard_map/stream_collide/pallas_call | solution.py:570
  47.5 0.0 copy-start.1
  47.6 23.6 %all_to_all.22.faces_ref.rows_ref = f32[8,96,256]{2,1,0:T(8,128)S(1)} all-to-all(f32[8,96,256]{2,1,0:T(8,128)S(1)} %get-tuple-element.12), channel_id=1, replica_groups=mesh['blk'=8,'gz'=4] {'blk'}, dimensions={0} | all-to-all | bytes 1572864 | tf_op jit(solution)/shard_map/all_to_all | solution.py:586
  71.2 2.7 %collective-permute-start.3 = (f32[8,8,256]{2,1,0:T(8,128)S(1)}, f32[8,8,256]{2,1,0:T(8,128)S(1)}, u32[]{:S(2)}, u32[]{:S(2)}) collective-permute-start(f32[8,8,256]{2,1,0:T(8,128)S(1)} %get-tuple-element.16), channel_id=1, source_target_pairs={{0,3},{1,2},{2,1},{3,0},{4,7},{5,6},{6,5},{7,4},{8,11},{9,10},{10,... | collective-permute-start | bytes 196616 | tf_op jit(solution)/shard_map/ppermute | solution.py:548
  73.9 0.0 collective-permute-start.2
  73.9 2.7 %collective-permute-done.3.second_ref = f32[8,8,256]{2,1,0:T(8,128)S(1)} collective-permute-done((f32[8,8,256]{2,1,0:T(8,128)S(1)}, f32[8,8,256]{2,1,0:T(8,128)S(1)}, u32[]{:S(2)}, u32[]{:S(2)}) %collective-permute-start.3) | collective-permute-done | bytes 65568 | tf_op jit(solution)/shard_map/ppermute | solution.py:548
  76.6 0.0 collective-permute-done.2.first_ref
  76.6 2.6 %route.3 = f32[8,40,256]{2,1,0:T(8,128)} custom-call(s32[64,6]{1,0:T(8,128)S(1)} %bitcast.7, f32[8,96,256]{2,1,0:T(8,128)S(1)} %all_to_all.22.faces_ref.rows_ref, f32[8,8,256]{2,1,0:T(8,128)S(1)} %collective-permute-done.2.first_ref, f32[8,8,256]{2,1,0:T(8,128)S(1)} %collective-permute-done.3.second_ref), custom_call_target="tpu_custom_call" | custom-call | tf_op jit(solution)/shard_map/route/pallas_call | solution.py:549
  79.1 3.4 %all-to-all-start.3 = ((f32[8,40,256]{2,1,0:T(8,128)}), f32[8,40,256]{2,1,0:T(8,128)S(1)}, u32[]{:S(2)}, u32[]{:S(2)}) async-start(f32[8,40,256]{2,1,0:T(8,128)} %route.3), calls=%async_computation.3 | async-start | bytes 655360 | tf_op jit(solution)/shard_map/all_to_all | solution.py:557
  82.6 0.0 copy-done.1
  82.6 3.3 %slab_rows.1 = (f32[48,16,128]{2,1,0:T(8,128)S(1)}, f32[48,2,128]{2,1,0:T(2,128)S(1)}, f32[48,2,128]{2,1,0:T(2,128)S(1)}) custom-call(s32[8]{0:T(128)S(1)} %copy-done, s32[1,64]{1,0:T(1,128)S(1)} %copy-done.1, f32[8,96,256]{2,1,0:T(8,128)S(1)} %all_to_all.22.faces_ref.rows_ref), custom_call_target="tpu_custom_call" | custom-call | tf_op jit(solution)/shard_map/slab_rows/pallas_call | solution.py:589
  85.8 0.9 collective-permute-start.4
  86.7 0.8 collective-permute-start.5
  87.5 0.1 collective-permute-done.4.first_ref
  87.6 2.9 %collective-permute-done.5.second_ref = f32[48,2,128]{2,1,0:T(2,128)S(1)} collective-permute-done((f32[48,2,128]{2,1,0:T(2,128)S(1)}, f32[48,2,128]{2,1,0:T(2,128)S(1)}, u32[]{:S(2)}, u32[]{:S(2)}) %collective-permute-start.5) | collective-permute-done | bytes 49184 | tf_op jit(solution)/shard_map/ppermute | solution.py:599
  90.6 1.6 %slab_depth.1 = f32[48,16,128]{2,1,0:T(8,128)} custom-call(s32[8]{0:T(128)S(1)} %copy-done, f32[48,16,128]{2,1,0:T(8,128)S(1)} %get-tuple-element.13.rows_ref, f32[48,2,128]{2,1,0:T(2,128)S(1)} %collective-permute-done.4.first_ref, f32[48,2,128]{2,1,0:T(2,128)S(1)} %collective-permute-done.5.second_ref), custom_call_target="tpu_custom_call" | custom-call | tf_op jit(solution)/shard_map/slab_depth/pallas_call | solution.py:600
  92.2 0.0 all-to-all-done.3.halo_ref
  92.2 3.8 %stream_last.1 = f32[8,19,16,256]{3,2,1,0:T(8,128)} custom-call(f32[8,19,16,256]{3,2,1,0:T(8,128)} %get-tuple-element.11.before_hbm, f32[8,40,256]{2,1,0:T(8,128)S(1)} %all-to-all-done.3.halo_ref), custom_call_target="tpu_custom_call" | custom-call | tf_op jit(solution)/shard_map/stream_last/pallas_call | solution.py:608
  (2 shorter events, 0.0 us)
Async XLA Ops:
  0.6 23.7 %copy-start.2 = (s32[1,64,6]{1,0,2:T(1,128)S(1)}, s32[1,64,6]{1,0,2:T(1,128)}, u32[]{:S(2)}) copy-start(s32[1,64,6]{1,0,2:T(1,128)} %param.10) | copy-start | bytes 4612
  0.6 40.1 %copy-start = (s32[8]{0:T(128)S(1)}, s32[8]{0:T(128)}, u32[]{:S(2)}) copy-start(s32[8]{0:T(128)} %owner_ref.5) | copy-start | bytes 100
  20.2 6.9 %collective-permute-start.1 = (f32[8,8,256]{2,1,0:T(8,128)S(1)}, f32[8,8,256]{2,1,0:T(8,128)S(1)}, u32[]{:S(2)}, u32[]{:S(2)}) collective-permute-start(f32[8,8,256]{2,1,0:T(8,128)S(1)} %get-tuple-element.18), channel_id=1, source_target_pairs={{0,3},{1,2},{2,1},{3,0},{4,7},{5,6},{6,5},{7,4},{8,11},{9,10},{10,... | collective-permute-start | bytes 196616 | tf_op jit(solution)/shard_map/ppermute | solution.py:548
  24.3 2.9 %collective-permute-start = (f32[8,8,256]{2,1,0:T(8,128)S(1)}, f32[8,8,256]{2,1,0:T(8,128)S(1)}, u32[]{:S(2)}, u32[]{:S(2)}) collective-permute-start(f32[8,8,256]{2,1,0:T(8,128)S(1)} %get-tuple-element.19), channel_id=1, source_target_pairs={{0,1},{1,0},{2,3},{3,2},{4,5},{5,4},{6,7},{7,6},{8,9},{9,8},{10,11... | collective-permute-start | bytes 196616 | tf_op jit(solution)/shard_map/ppermute | solution.py:547
  47.5 35.0 %copy-start.1 = (s32[1,64]{1,0:T(1,128)S(1)}, s32[1,64]{1,0:T(1,128)}, u32[]{:S(2)}) copy-start(s32[1,64]{1,0:T(1,128)} %column_ref.1) | copy-start | bytes 772
  71.2 5.3 %collective-permute-start.3 = (f32[8,8,256]{2,1,0:T(8,128)S(1)}, f32[8,8,256]{2,1,0:T(8,128)S(1)}, u32[]{:S(2)}, u32[]{:S(2)}) collective-permute-start(f32[8,8,256]{2,1,0:T(8,128)S(1)} %get-tuple-element.16), channel_id=1, source_target_pairs={{0,3},{1,2},{2,1},{3,0},{4,7},{5,6},{6,5},{7,4},{8,11},{9,10},{10,... | collective-permute-start | bytes 196616 | tf_op jit(solution)/shard_map/ppermute | solution.py:548
  73.9 2.7 %collective-permute-start.2 = (f32[8,8,256]{2,1,0:T(8,128)S(1)}, f32[8,8,256]{2,1,0:T(8,128)S(1)}, u32[]{:S(2)}, u32[]{:S(2)}) collective-permute-start(f32[8,8,256]{2,1,0:T(8,128)S(1)} %get-tuple-element.17), channel_id=1, source_target_pairs={{0,1},{1,0},{2,3},{3,2},{4,5},{5,4},{6,7},{7,6},{8,9},{9,8},{10,11... | collective-permute-start | bytes 196616 | tf_op jit(solution)/shard_map/ppermute | solution.py:547
  79.1 13.1 %all-to-all-start.3 = ((f32[8,40,256]{2,1,0:T(8,128)}), f32[8,40,256]{2,1,0:T(8,128)S(1)}, u32[]{:S(2)}, u32[]{:S(2)}) async-start(f32[8,40,256]{2,1,0:T(8,128)} %route.3), calls=%async_computation.3 | async-start | bytes 655360 | tf_op jit(solution)/shard_map/all_to_all | solution.py:557
  85.8 1.8 %collective-permute-start.4 = (f32[48,2,128]{2,1,0:T(2,128)S(1)}, f32[48,2,128]{2,1,0:T(2,128)S(1)}, u32[]{:S(2)}, u32[]{:S(2)}) collective-permute-start(f32[48,2,128]{2,1,0:T(2,128)S(1)} %get-tuple-element.14), channel_id=1, source_target_pairs={{0,1},{1,0},{2,3},{3,2},{4,5},{5,4},{6,7},{7,6},{8,9},{9,8},{10,11... | collective-permute-start | bytes 147464 | tf_op jit(solution)/shard_map/ppermute | solution.py:598
  86.7 3.8 %collective-permute-start.5 = (f32[48,2,128]{2,1,0:T(2,128)S(1)}, f32[48,2,128]{2,1,0:T(2,128)S(1)}, u32[]{:S(2)}, u32[]{:S(2)}) collective-permute-start(f32[48,2,128]{2,1,0:T(2,128)S(1)} %get-tuple-element.15), channel_id=1, source_target_pairs={{0,3},{1,2},{2,1},{3,0},{4,7},{5,6},{6,5},{7,4},{8,11},{9,10},{10,... | collective-permute-start | bytes 147464 | tf_op jit(solution)/shard_map/ppermute | solution.py:599

commit v3 on v2

v3 whole, which is shorter than its diff:
```python
import functools

import jax
import jax.numpy as jnp
import numpy as np
from jax import lax
from jax.experimental import pallas as pl
from jax.experimental.pallas import tpu as pltpu
from jax.sharding import PartitionSpec as P

STEPS = 2
VELOCITIES = [
    (0, 0, 0),
    (1, 0, 0),
    (-1, 0, 0),
    (0, 1, 0),
    (0, -1, 0),
    (0, 0, 1),
    (0, 0, -1),
    (1, 1, 0),
    (-1, -1, 0),
    (1, -1, 0),
    (-1, 1, 0),
    (1, 0, 1),
    (-1, 0, -1),
    (1, 0, -1),
    (-1, 0, 1),
    (0, 1, 1),
    (0, -1, -1),
    (0, 1, -1),
    (0, -1, 1),
]
POPS = 19
EAST_POPS = [1, 7, 9, 11, 13]
WEST_POPS = [2, 8, 10, 12, 14]
NORTH_POPS = [7, 10, 15, 17]
SOUTH_POPS = [8, 9, 16, 18]
UPPER_POPS = [5, 11, 14, 15, 18]
LOWER_POPS = [6, 12, 13, 16, 17]
RELAX_RATE = 1.25
DRAG_RATE = 0.3
TAP_EDGE, TAP_NEAR = 1.0 / 3.0, 2.0 / 3.0

FACE_ROWS = 40
STREAM_GROUP = 5
FIRST, SECOND = 24, 32
SOUTH = 64


SOURCES = 16


def shift(value, amount, axis=1):
    amount = amount % value.shape[axis]
    return value if amount == 0 else pltpu.roll(value, amount, axis)


def lanes(shape):
    return lax.broadcasted_iota(jnp.int32, shape, len(shape) - 1)


def collide_cells(f, u, porosity):
    total, gap = {}, {}
    for i in range(1, POPS, 2):
        total[i], gap[i] = f[i] + f[i + 1], f[i] - f[i + 1]
    ux, uy, uz = u
    mx = gap[1] + gap[7] + gap[9] + gap[11] + gap[13]
    my = gap[3] + gap[7] - gap[9] + gap[15] + gap[17]
    mz = gap[5] + gap[11] - gap[13] + gap[15] - gap[17]
    xy_sum, xz_sum, yz_sum = total[7] + total[9], total[11] + total[13], total[15] + total[17]
    xx = 2.0 * total[1] + xy_sum + xz_sum
    yy = 2.0 * total[3] + xy_sum + yz_sum
    zz = 2.0 * total[5] + xz_sum + yz_sum
    xy, xz, yz = total[7] - total[9], total[11] - total[13], total[15] - total[17]
    mass = 12.0 * f[0] + 2.0 * (total[1] + total[3] + total[5]) + (xy_sum + xz_sum + yz_sum)
    speed_sq = ux * ux + uy * uy + uz * uz
    qx = xx * ux + xy * uy + xz * uz
    qy = xy * ux + yy * uy + yz * uz
    qz = xz * ux + yz * uy + zz * uz
    sens = ux * mx + uy * my + uz * mz
    drag = DRAG_RATE * porosity
    scale = RELAX_RATE / 36.0
    quad = ux * qx + uy * qy + uz * qz
    base = scale * (mass + 1.5 * (speed_sq * mass) - 4.5 * quad) + drag * sens
    gx = (3.0 * scale) * (mx + gap[1] + 3.0 * qx - ux * mass) - drag * mx
    gy = (3.0 * scale) * (my + gap[3] + 3.0 * qy - uy * mass) - drag * my
    gz = (3.0 * scale) * (mz + gap[5] + 3.0 * qz - uz * mass) - drag * mz
    along = {1: gx, 3: gy, 5: gz, 7: gx + gy, 9: gx - gy, 11: gx + gz, 13: gx - gz, 15: gy + gz, 17: gy - gz}
    keep = 1.0 - RELAX_RATE
    post = [base + keep * f[0]]
    for i in range(1, POPS, 2):
        post.append(base + along[i] + keep * f[i])
        post.append(base - along[i] + keep * f[i + 1])
    return post, sens


def collide_block(read, velocity_ref, porosity_ref, post_ref, edge, plane):
    parts = {}
    for low in range(0, edge, 8):
        for left in range(0, plane, 128):
            zs, cells = pl.ds(low, 8), pl.ds(left, 128)
            post, sens = collide_cells(
                [read(p, zs, cells) for p in range(POPS)],
                [velocity_ref[c, zs, cells] for c in range(3)],
                porosity_ref[zs, cells],
            )
            for p in range(POPS):
                post_ref[p, zs, cells] = post[p]
            parts[low, left] = sens
    return parts


def part(ref, p, low, left):
    return ref[p, low : low + 8, left : left + 128]


def pack_faces(block, blocks, swapped, post_ref, faces_ref, edge, plane):
    def put_ends(target, row, cells, low, high):
        faces_ref[target, FIRST + row : FIRST + row + 1, cells] = jnp.where(swapped, high, low)
        faces_ref[target, SECOND + row : SECOND + row + 1, cells] = jnp.where(swapped, low, high)

    lane = lanes((8, 128))
    slot, group = lane % edge, lane // edge
    for left in range(0, plane, 128):
        cells = slice(left, left + 128)
        tiles = []
        for low in range(0, edge, 8):
            tile = part(post_ref, EAST_POPS[0], low, left)
            for s, p in enumerate(EAST_POPS[1:], 1):
                tile = jnp.where(slot == s, shift(part(post_ref, p, low, left), s), tile)
            for s, p in enumerate(WEST_POPS, 5):
                tile = jnp.where(slot == s, shift(part(post_ref, p, low, left), s - (edge - 1)), tile)
            faces_ref[block, low : low + 8, cells] = tile
            tiles.append(tile)
        put_ends(block, 5, cells, tiles[0][0:1], tiles[-1][7:8])
        for i in range(5):
            put_ends(
                block,
                i,
                cells,
                post_ref[UPPER_POPS[i], 0:1, cells],
                post_ref[LOWER_POPS[i], edge - 1 : edge, cells],
            )

    def y_tiles(pops, left, first):
        tiles = []
        for low in range(0, edge, 8):
            tile = None
            for q, p in enumerate(pops):
                moved = shift(part(post_ref, p, low, left), q * edge if first == 0 else (q + 5) * edge)
                tile = moved if tile is None else jnp.where(group == first + q, moved, tile)
            tiles.append(tile)
        return tiles

    north = y_tiles(NORTH_POPS, 0, 0)
    south = y_tiles(SOUTH_POPS, plane - 128, 4)

    def put_y(target, tiles, start, pop, left, first, row):
        cells = slice(start, start + 64)
        for half in range(2):
            at = half * 128
            faces_ref[target, 16:24, at + start : at + start + 64] = tiles[half][:, cells]
            line = jnp.where(group == first, part(post_ref, pop, half * 8, left), 0.0)
            line = pltpu.roll(line, (128 - first * edge) % 128, 1, stride=edge, stride_axis=0)
            faces_ref[target, row + 7 : row + 8, at : at + 128] = jnp.sum(line, axis=0, keepdims=True)
        put_ends(target, 6, cells, tiles[0][0:1, cells], tiles[1][7:8, cells])

    if block > 0:
        put_y(block - 1, north, 0, 3, 0, 0, FIRST)
    if block < blocks - 1:
        put_y(block + 1, south, SOUTH, 4, plane - 128, 7, SECOND)


def first_partner_above():
    return lax.rem(lax.axis_index("gz").astype(jnp.int32), jnp.int32(2)) == 0


def stream_pop(p, source_ref, halo_ref, edge):
    cx, cy, cz = VELOCITIES[p]
    lane = lanes((8, 128))
    sides, depths = (0, 1), (0, 1)
    value = {(z, c): shift(part(source_ref, p, z * 8, c * 128), -(cx + edge * cy)) for z in depths for c in sides}
    at_face = lane % edge == (edge - 1 if cx > 0 else 0)
    if cx != 0:
        s = EAST_POPS.index(p) if cx > 0 else 5 + WEST_POPS.index(p)
        turn = (edge - 1 if cx > 0 else 0) - s - edge * cy
        arrived = {(z, c): shift(halo_ref[z * 8 : z * 8 + 8, c * 128 : c * 128 + 128], turn) for z in depths for c in sides}
    if cy == 0:
        if cx != 0:
            value = {at: jnp.where(at_face, arrived[at], value[at]) for at in value}
    else:
        far = 7 if cy > 0 else 0
        border = lane // edge == far
        outer = 1 if cy > 0 else 0
        if p in (3, 4):
            row = (FIRST if cy > 0 else SECOND) + 7
            lined = lax.broadcasted_iota(jnp.int32, (8, 128), 0) == lane // edge
            faces = [jnp.where(lined, halo_ref[row : row + 1, at : at + 128], 0.0) for at in (0, 128)]
            for step in (4, 2, 1):
                faces = [face + shift(face, step * edge) for face in faces]
        else:
            start = NORTH_POPS.index(p) * edge if cy > 0 else SOUTH + SOUTH_POPS.index(p) * edge
            faces = [shift(halo_ref[16:24, at : at + 128], far * edge - start) for at in (0, 128)]
        moved = {}
        for z in depths:
            inner = jnp.where(border, value[z, outer], value[z, 1 - outer])
            rim = value[z, outer]
            if cx != 0:
                inner = jnp.where(at_face, jnp.where(border, arrived[z, outer], arrived[z, 1 - outer]), inner)
                rim = jnp.where(at_face, arrived[z, outer], rim)
            moved[z, 1 - outer] = inner
            moved[z, outer] = jnp.where(border, faces[z], rim)
        value = moved
    if cz != 0:
        row = FIRST + UPPER_POPS.index(p) if cz > 0 else SECOND + LOWER_POPS.index(p)
        outer = 1 if cz > 0 else 0
        border = lax.broadcasted_iota(jnp.int32, (8, 128), 0) == (7 if cz > 0 else 0)
        moved = {}
        for c in sides:
            turned = [shift(value[z, c], -cz, 0) for z in depths]
            moved[1 - outer, c] = jnp.where(border, turned[outer], turned[1 - outer])
            moved[outer, c] = jnp.where(border, halo_ref[row : row + 1, c * 128 : c * 128 + 128], turned[outer])
        value = moved
    return value


def stream_block(source_ref, halo_ref, out_ref, edge):
    for start in range(0, POPS, STREAM_GROUP):
        pops = range(start, min(start + STREAM_GROUP, POPS))
        values = [stream_pop(p, source_ref, halo_ref, edge) for p in pops]
        for p, value in zip(pops, values):
            for (z, c), tile in value.items():
                out_ref[p, z * 8 : z * 8 + 8, c * 128 : c * 128 + 128] = tile


def source_rows(d, row, blocks, table_ref, sources_ref, edge):
    here = d * blocks + row
    west, east, south, north, below, above = [table_ref[face, 0, here] for face in range(6)]

    def beside(slot_id, face):
        return jnp.where(slot_id < 0, -1, table_ref[face, 0, jnp.maximum(slot_id, 0)])

    lane = lanes((1, 128))
    in_north = lane < SOUTH
    near = jnp.where(in_north, north, south)
    far_east = jnp.where(in_north, beside(north, 1), beside(south, 1))
    far_west = jnp.where(in_north, beside(north, 0), beside(south, 0))
    in_east, in_west = east_west_groups(lane, edge)
    rows = [
        jnp.where(lane % edge < 5, east, west),
        jnp.where(
            in_east & (lane % edge == edge - 1),
            far_east,
            jnp.where(in_west & (lane % edge == 0), far_west, near),
        ),
        north,
        south,
    ]
    for face, own in ((5, above), (4, below)):
        rows += [own, beside(east, face), beside(west, face), beside(north, face), beside(south, face)]
    for r, slot_id in enumerate(rows):
        device = lax.shift_right_arithmetic(slot_id, jnp.int32(blocks.bit_length() - 1))
        sources_ref[d, r : r + 1, :] = jnp.broadcast_to(device, (1, 128))


def east_west_groups(lane, edge):
    group = lane // edge
    return (group == 0) | (group == 5), (group == 1) | (group == 4)


def first_kernel(
    blocks,
    devices,
    table_hbm,
    state_hbm,
    velocity_hbm,
    porosity_hbm,
    post_ref,
    faces_ref,
    sources_ref,
    state_ref,
    velocity_ref,
    porosity_ref,
    table_ref,
    sems,
    sem,
):
    edge, plane = porosity_ref.shape[1:]
    swapped = first_partner_above()
    row = jnp.minimum(lax.axis_index("blk").astype(jnp.int32), blocks - 1)

    def copy(b):
        return pltpu.make_async_copy(state_hbm.at[b], state_ref.at[b], sems.at[b])

    others = [
        pltpu.make_async_copy(table_hbm, table_ref, sem.at[0]),
        pltpu.make_async_copy(velocity_hbm, velocity_ref, sem.at[1]),
        pltpu.make_async_copy(porosity_hbm, porosity_ref, sem.at[2]),
    ]
    copy(0).start()
    for other in others:
        other.start()
    for b in range(1, blocks):
        copy(b).start()
    for other in others:
        other.wait()
    per = -(-devices // blocks)

    def one(b, carry):
        copy(b).wait()
        parts = collide_block(
            lambda p, zs, cells: state_ref[b, p, zs, cells],
            velocity_ref.at[b],
            porosity_ref.at[b],
            post_ref.at[b],
            edge,
            plane,
        )
        for (low, left), sens in parts.items():
            post_ref[b, POPS, pl.ds(low, 8), pl.ds(left, 128)] = sens
        for k in range(per):
            source_rows(jnp.minimum(b * per + k, devices - 1), row, blocks, table_ref, sources_ref, edge)
        return carry

    lax.fori_loop(0, blocks, one, 0)
    for b in range(blocks):
        pack_faces(b, blocks, swapped, post_ref.at[b], faces_ref, edge, plane)


def slab_start(owner_ref, slab, devices):
    start = jnp.int32(0)
    for j in range(devices):
        start = start + jnp.where(j < slab, 2 * owner_ref[j], 0)
    return start


def second_kernel(
    blocks,
    devices,
    chunks,
    owner_hbm,
    before_ref,
    velocity_hbm,
    porosity_hbm,
    halo_ref,
    near_hbm,
    late_hbm,
    faces_ref,
    velocity_ref,
    porosity_ref,
    post_ref,
    state_ref,
    field_ref,
    turned_ref,
    owner_ref,
    sems,
    sem,
):
    edge, plane = porosity_ref.shape[1:]
    swapped = first_partner_above()
    others = [
        pltpu.make_async_copy(velocity_hbm, velocity_ref, sem.at[1]),
        pltpu.make_async_copy(porosity_hbm, porosity_ref, sem.at[2]),
        pltpu.make_async_copy(owner_hbm, owner_ref, sem.at[0]),
    ]
    for other in others:
        other.start()

    half = blocks // 2

    def result(b, out_hbm, first):
        return pltpu.make_async_copy(post_ref.at[b], out_hbm.at[b - first], sems.at[b])

    def stream(b, carry):
        stream_block(before_ref.at[b], halo_ref.at[b], state_ref.at[b], edge)
        return carry

    lax.fori_loop(0, blocks, stream, 0)
    for other in others:
        other.wait()

    def collide(b, carry):
        parts = collide_block(
            lambda p, zs, cells: state_ref[b, p, zs, cells],
            velocity_ref.at[b],
            porosity_ref.at[b],
            post_ref.at[b],
            edge,
            plane,
        )

        @pl.when(b < half)
        def _():
            result(b, near_hbm, 0).start()

        @pl.when(b >= half)
        def _():
            result(b, late_hbm, half).start()

        for (low, left), sens in parts.items():
            field_ref[b * (plane // 128) + left // 128, pl.ds(low, 8), :] = (
                before_ref[b, POPS, pl.ds(low, 8), pl.ds(left, 128)] + sens
            )
        return carry

    lax.fori_loop(0, blocks, collide, 0)

    for b in range(blocks):
        pack_faces(b, blocks, swapped, post_ref.at[b], faces_ref, edge, plane)
    held = blocks * (plane // 128)
    lane = lanes((8, 128))
    for m in range(4):
        for low in (0, 8):
            turned = [shift(field_ref[c, low : low + 8, :], -2 * m * edge) for c in range(held)]
            for c in range(held + 1):
                ahead = turned[min(c, held - 1)]
                if 0 < c < held and m > 0:
                    ahead = jnp.where(lane < 128 - 2 * m * edge, turned[c - 1], ahead)
                elif m == 0 or c == held:
                    ahead = turned[max(c - 1, 0)]
                turned_ref[m, c, low : low + 8, :] = ahead
    start = jnp.int32(0)
    for j in range(devices):
        first = lax.div(start + 6, jnp.int32(8))
        phase = lax.div(start + 6 - 8 * first, jnp.int32(2))
        for i in range(chunks):
            at = FACE_ROWS + 8 * i
            value = turned_ref[phase, jnp.minimum(first + i, held)]
            faces_ref[j, at : at + 8, 0:128] = value[0:8]
            faces_ref[j, at : at + 8, 128:256] = value[8:16]
        start = start + 2 * owner_ref[j]
    for b in range(blocks):
        (result(b, near_hbm, 0) if b < half else result(b, late_hbm, half)).wait()


def last_kernel(blocks, near_ref, late_hbm, halo_ref, out_hbm, late_ref, out_ref, sems):
    edge = late_ref.shape[2]
    half = blocks // 2

    def late(b):
        return pltpu.make_async_copy(late_hbm.at[b - half], late_ref.at[b - half], sems.at[blocks + b - half])

    def result(b):
        return pltpu.make_async_copy(out_ref.at[b], out_hbm.at[b], sems.at[b])

    for b in range(half, blocks):
        late(b).start()

    def one(b, before_ref):
        stream_block(before_ref, halo_ref.at[b], out_ref.at[b], edge)
        result(b).start()

    def near_one(b, carry):
        one(b, near_ref.at[b])
        return carry

    def late_one(b, carry):
        late(b).wait()
        one(b, late_ref.at[b - half])
        return carry

    lax.fori_loop(0, half, near_one, 0)
    lax.fori_loop(half, blocks, late_one, 0)
    for b in range(blocks):
        result(b).wait()


def route_kernel(devices, sources_ref, faces_ref, first_ref, second_ref, halo_ref, y_ref, above_ref, below_ref):
    edge = 16
    swapped = first_partner_above()
    lane = lanes((8, 128))
    level = lax.broadcasted_iota(jnp.int32, (8, 128), 0)
    x, group = lane % edge, lane // edge
    in_east, in_west = east_west_groups(lane, edge)
    sides = (0, 128)

    def z_tiles(own, pops, last):
        out = list(own)
        for i, p in enumerate(pops):
            cx, cy, _ = VELOCITIES[p]
            if cx != 0:
                face = edge - 1 if cx > 0 else 0
                s = EAST_POPS.index(p) if cx > 0 else 5 + WEST_POPS.index(p)
                for c in range(2):
                    arrived = jnp.broadcast_to(shift(own[c][5:6], face - s), (8, 128))
                    value = jnp.where(x == face, arrived, shift(own[c], -cx))
                    out[c] = jnp.where(level == i, value, out[c])
            if cy != 0:
                outer = 1 if cy > 0 else 0
                face = 7 if cy > 0 else 0
                start = NORTH_POPS.index(p) * edge if cy > 0 else SOUTH + SOUTH_POPS.index(p) * edge
                turned = [shift(side, -cy * edge) for side in own]
                arrived = jnp.broadcast_to(shift(own[0][6:7], face * edge - start), (8, 128))
                inner = jnp.where(group == face, turned[outer], turned[1 - outer])
                rim = jnp.where(group == face, arrived, turned[outer])
                out[1 - outer] = jnp.where(level == i, inner, out[1 - outer])
                out[outer] = jnp.where(level == i, rim, out[outer])
        return [jnp.where(level == 7, last[c], out[c]) for c in range(2)]

    def prepare(e, carry):
        first, second = [[ref[e, :, at : at + 128] for at in sides] for ref in (first_ref, second_ref)]
        above = [jnp.where(swapped, a, b) for a, b in zip(first, second)]
        below = [jnp.where(swapped, b, a) for a, b in zip(first, second)]
        for own, pops, row, ref in ((above, UPPER_POPS, FIRST, above_ref), (below, LOWER_POPS, SECOND, below_ref)):
            last = [faces_ref[e, row + 7 : row + 8, at : at + 128] for at in sides]
            for at, tile in zip(sides, z_tiles(own, pops, last)):
                ref[e, :, at : at + 128] = tile
        for at in sides:
            own = faces_ref[e, 16:24, at : at + 128]
            east = jnp.where(x == edge - 1, shift(own, edge - 1), shift(own, -1))
            west = jnp.where(x == 0, shift(own, 1 - edge), shift(own, 1))
            y_ref[e, :, at : at + 128] = jnp.where(in_east, east, jnp.where(in_west, west, own))
        return carry

    lax.fori_loop(0, devices, prepare, 0, unroll=2)

    def pick(index, tiles_of):
        total = None
        for e in range(devices):
            hit = index == e
            tiles = tiles_of(e)
            total = [jnp.where(hit, t, 0.0 if total is None else total[k]) for k, t in enumerate(tiles)]
        return total

    def one(d, carry):
        row = [jnp.broadcast_to(sources_ref[d, r : r + 1, :], (8, 128)) for r in range(14)]
        spots = [(low, at) for low in (0, 8) for at in sides]
        x_tiles = pick(row[0], lambda e: [faces_ref[e, low : low + 8, at : at + 128] for low, at in spots])
        for (low, at), tile in zip(spots, x_tiles):
            halo_ref[d, low : low + 8, at : at + 128] = tile
        y_tiles = pick(row[1], lambda e: [y_ref[e, :, at : at + 128] for at in sides])
        for at, tile in zip(sides, y_tiles):
            halo_ref[d, 16:24, at : at + 128] = tile
        for pops, last, base, ref, top in ((UPPER_POPS, 2, 4, above_ref, FIRST), (LOWER_POPS, 3, 9, below_ref, SECOND)):
            index = [jnp.where(level == 7, row[last], row[base])] * 2
            for i, p in enumerate(pops):
                cx, cy, _ = VELOCITIES[p]
                if cx != 0:
                    here = (level == i) & (x == (edge - 1 if cx > 0 else 0))
                    index = [jnp.where(here, row[base + (1 if cx > 0 else 2)], side) for side in index]
                if cy != 0:
                    outer, face = (1, 7) if cy > 0 else (0, 0)
                    here = (level == i) & (group == face)
                    index[outer] = jnp.where(here, row[base + (3 if cy > 0 else 4)], index[outer])
            for at, side in zip(sides, index):
                (tile,) = pick(side, lambda e: [ref[e, :, at : at + 128]])
                halo_ref[d, top : top + 8, at : at + 128] = tile
        return carry

    lax.fori_loop(0, devices, one, 0, unroll=2)


def slab_kernel(
    blocks, devices, chunks, owner_ref, column_ref, rows_ref, out_ref, first_ref, second_ref, field_ref
):
    slab = lax.axis_index("blk").astype(jnp.int32)
    swapped = first_partner_above()
    count, edge, width = out_ref.shape
    start = slab_start(owner_ref, slab, devices)
    group = lanes((edge, width)) // edge
    lane = lanes((edge, width))
    height = blocks * edge

    def chunk(i, carry):
        top = start - 2 + 8 * i
        tiles = [jnp.zeros((edge, width), jnp.float32) for _ in range(8)]
        at = pl.multiple_of(FACE_ROWS + 8 * i, 8)
        values = [
            jnp.concatenate([rows_ref[e, pl.ds(at, 8), 0:128], rows_ref[e, pl.ds(at, 8), 128:256]], axis=0)
            for e in range(devices)
        ]
        for r in range(0, 8, 2):
            inside = (top + r >= 0) & (top + r < height)
            block_row = lax.div(jnp.clip(top + r, 0, height - 1), jnp.int32(edge))
            for e in range(devices):
                column = column_ref[0, e * blocks + block_row]
                hit = group == jnp.where(inside, column, -1)
                for k in range(r, r + 2):
                    part = pltpu.roll(values[e], lax.rem(column + (8 - k), jnp.int32(8)) * edge, 1)
                    if width > 128:
                        part = jnp.concatenate([part] * (width // 128), axis=1)
                    tiles[k] = jnp.where(hit, part, tiles[k])
        for r in range(8):
            field_ref[i * 8 + r] = tiles[r]
        return carry

    lax.fori_loop(0, chunks, chunk, 0)

    def row(r):
        at = r
        mixed = TAP_EDGE * (field_ref[at] + field_ref[at + 4]) + (
            TAP_NEAR * (field_ref[at + 1] + field_ref[at + 3]) + field_ref[at + 2]
        )
        value = mixed
        for step, tap in ((1, TAP_NEAR), (2, TAP_EDGE)):
            left = jnp.where(lane >= step, shift(mixed, step), 0.0)
            right = jnp.where(lane < width - step, shift(mixed, -step), 0.0)
            value = value + tap * (left + right)
        out_ref[r] = value
        low, high = value[0:2], value[edge - 2 : edge]
        first_ref[r] = jnp.where(swapped, high, low)
        second_ref[r] = jnp.where(swapped, low, high)

    by_rows(count, row)


def by_rows(count, body):
    step = 8 if count % 8 == 0 else 4 if count % 4 == 0 else 2

    def several(i, carry):
        for k in range(step):
            body(i * step + k)
        return carry

    lax.fori_loop(0, count // step, several, 0)


def depth_kernel(devices, layers, owner_ref, rows_ref, first_ref, second_ref, out_ref):
    count, edge, width = out_ref.shape
    slab, layer = lax.axis_index("blk").astype(jnp.int32), lax.axis_index("gz").astype(jnp.int32)
    own_rows = jnp.int32(0)
    for j in range(devices):
        own_rows = jnp.where(slab == j, 2 * owner_ref[j], own_rows)
    swapped = first_partner_above()
    depth = lax.broadcasted_iota(jnp.int32, (edge, width), 0)

    def row(r):
        value = rows_ref[r]
        first, second = first_ref[r], second_ref[r]
        below = jnp.where(layer > 0, jnp.where(swapped, second, first), 0.0)
        above = jnp.where(layer < layers - 1, jnp.where(swapped, first, second), 0.0)
        b0, b1, a0, a1 = below[0:1], below[1:2], above[0:1], above[1:2]
        down = jnp.where(depth == 0, b1, shift(value, 1, 0))
        up = jnp.where(depth == edge - 1, a0, shift(value, -1, 0))
        down_2 = jnp.where(depth == 0, b0, jnp.where(depth == 1, b1, shift(value, 2, 0)))
        up_2 = jnp.where(depth == edge - 1, a1, jnp.where(depth == edge - 2, a0, shift(value, -2, 0)))
        total = value + TAP_NEAR * (down + up) + TAP_EDGE * (down_2 + up_2)
        out_ref[r] = jnp.where(r < own_rows, total, 0.0)

    by_rows(count, row)


SMEM = pl.BlockSpec(memory_space=pltpu.SMEM)
VMEM = pl.BlockSpec(memory_space=pltpu.VMEM)


ANY = pl.BlockSpec(memory_space=pl.ANY)


def f32(*shape):
    return jax.ShapeDtypeStruct(shape, jnp.float32)


def hbm(*shape):
    return pltpu.HBM(shape, jnp.float32)


def vmem(*shape):
    return pltpu.VMEM(shape, jnp.float32)


def local(adjoint, velocity, porosity, block_x, neighbours, owner_map):
    blocks, _, edge, plane = adjoint.shape[1:]
    devices, layers = lax.axis_size("blk"), lax.axis_size("gz")
    table = pltpu.with_memory_space_constraint(jnp.transpose(neighbours, (2, 0, 1)), pltpu.HBM)
    state, flow, design = [pltpu.with_memory_space_constraint(x[0], pltpu.HBM) for x in (adjoint, velocity, porosity)]
    rows_cap = 2 * (3 * (blocks * edge // 2) // devices)
    chunks = -(-(rows_cap + 4) // 8)
    width = devices * edge
    first_pairs = [(g, g ^ 1) for g in range(layers)]
    second_pairs = [(g, (g + 1 if g % 2 else g - 1) % layers) for g in range(layers)]
    near_shape, late_shape = [(count,) + state.shape[1:] for count in (blocks // 2, blocks - blocks // 2)]
    faces_shape = (devices, FACE_ROWS, plane)
    post_shape = (blocks, POPS + 1, edge, plane)
    params = pltpu.CompilerParams(vmem_limit_bytes=32 * 1024 * 1024)

    def to_halo(gathered):
        first = lax.ppermute(gathered[:, FIRST : FIRST + 8], "gz", first_pairs)
        second = lax.ppermute(gathered[:, SECOND : SECOND + 8], "gz", second_pairs)
        halo = pl.pallas_call(
            functools.partial(route_kernel, devices),
            out_shape=f32(*faces_shape),
            in_specs=[VMEM] * 4,
            out_specs=VMEM,
            scratch_shapes=[vmem(devices, 8, plane)] * 3,
            compiler_params=params,
            name="route",
        )(sources, gathered, first, second)
        return lax.all_to_all(halo, "blk", 0, 0, tiled=True)

    inputs = [vmem(*state.shape), vmem(*flow.shape), vmem(*design.shape)]
    post, faces, sources = pl.pallas_call(
        functools.partial(first_kernel, blocks, devices),
        out_shape=(
            vmem(*post_shape),
            f32(*faces_shape),
            jax.ShapeDtypeStruct((devices, SOURCES, 128), jnp.int32),
        ),
        in_specs=[ANY] * 4,
        out_specs=(VMEM,) * 3,
        scratch_shapes=inputs
        + [
            pltpu.SMEM(table.shape, jnp.int32),
            pltpu.SemaphoreType.DMA((blocks,)),
            pltpu.SemaphoreType.DMA((3,)),
        ],
        compiler_params=params,
        name="collide_first",
    )(table, state, flow, design)
    halo = to_halo(lax.all_to_all(faces, "blk", 0, 0, tiled=True))
    near, late, faces = pl.pallas_call(
        functools.partial(second_kernel, blocks, devices, chunks),
        out_shape=(hbm(*near_shape), hbm(*late_shape), f32(devices, FACE_ROWS + 8 * chunks, plane)),
        in_specs=[ANY, VMEM, ANY, ANY, VMEM],
        out_specs=(ANY, ANY, VMEM),
        scratch_shapes=inputs[1:]
        + [
            vmem(*state.shape),
            vmem(*state.shape),
            vmem(blocks * plane // 128, edge, 128),
            vmem(4, blocks * plane // 128 + 1, edge, 128),
            pltpu.SMEM(owner_map.shape, jnp.int32),
            pltpu.SemaphoreType.DMA((blocks,)),
            pltpu.SemaphoreType.DMA((3,)),
        ],
        compiler_params=params,
        name="stream_collide",
    )(owner_map, post, flow, design, halo)
    gathered = lax.all_to_all(faces, "blk", 0, 0, tiled=True)
    halo = to_halo(gathered)
    slab_shape, ends = (rows_cap, edge, width), (rows_cap, 2, width)
    slab, first, second = pl.pallas_call(
        functools.partial(slab_kernel, blocks, devices, chunks),
        out_shape=(f32(*slab_shape), f32(*ends), f32(*ends)),
        in_specs=[SMEM, SMEM, VMEM],
        out_specs=(VMEM,) * 3,
        scratch_shapes=[vmem(chunks * 8, edge, width)],
        compiler_params=params,
        name="slab_rows",
    )(owner_map, block_x, gathered)
    first = lax.ppermute(first, "gz", first_pairs)
    second = lax.ppermute(second, "gz", second_pairs)
    smoothed = pl.pallas_call(
        functools.partial(depth_kernel, devices, layers),
        out_shape=f32(*slab_shape),
        in_specs=[SMEM, VMEM, VMEM, VMEM],
        out_specs=VMEM,
        compiler_params=params,
        name="slab_depth",
    )(owner_map, slab, first, second)
    moved = pl.pallas_call(
        functools.partial(last_kernel, blocks),
        out_shape=hbm(*state.shape),
        in_specs=[VMEM, ANY, VMEM],
        out_specs=ANY,
        scratch_shapes=[
            vmem(*late_shape),
            vmem(*state.shape),
            pltpu.SemaphoreType.DMA((2 * blocks - blocks // 2,)),
        ],
        compiler_params=params,
        name="stream_last",
    )(near, pltpu.with_memory_space_constraint(late, pltpu.HBM), halo)
    return (moved[None], smoothed[None, None])


def solution(mesh):
    placed = (
        P("gz", "blk", None, None, None),
        P("gz", "blk", None, None, None),
        P("gz", "blk", None, None),
        P("gz", None),
        P("gz", None, None),
        P(),
    )
    return jax.shard_map(
        local,
        mesh=mesh,
        in_specs=placed,
        out_specs=(P("gz", "blk", None, None, None), P("gz", "blk", None, None, None)),
        check_vma=False,
    )
```

time: 97.8 us -> 90.6 us (0.926)
  the two profiles are of different devices: /device:TPU:1 before, /device:TPU:0 now
where the time goes in v3:
time: 90.6 us; the launch traced here: 90.2 us
  blocking collectives  55 us (61%)
  Pallas kernels  16.9 us (19%)
  waiting for transfers between devices  9.7 us (11%)
  starting transfers between devices  7.9 us (9%)
    all_to_all x1, blocking collectives, local(): gathered = lax.all_to_all(faces, 'blk', 0, 0, tiled=True)  23 us
    all_to_all x1, blocking collectives, local(): halo = to_halo(lax.all_to_all(faces, 'blk', 0, 0, tiled=True))  18 us
    all_to_all x1, blocking collectives, to_halo(): return lax.all_to_all(halo, 'blk', 0, 0, tiled=True)  14 us
    ppermute x2, waiting for transfers between devices, to_halo(): second = lax.ppermute(gathered[:, SECOND:SECOND + 8], 'gz', second_pairs)  5.57 us
    pallas_call x1, Pallas kernels, local(): pl.pallas_call(functools.partial(second_kernel, blocks, devices, chunks),...  3.69 us
    all_to_all x1, starting transfers between devices, to_halo(): return lax.all_to_all(halo, 'blk', 0, 0, tiled=True)  3.59 us
    pallas_call x1, Pallas kernels, local(): pl.pallas_call(functools.partial(first_kernel, blocks, devices), out_shap...  3.28 us
    pallas_call x1, Pallas kernels, local(): pl.pallas_call(functools.partial(slab_kernel, blocks, devices, chunks), o...  3.27 us
  transfers between devices with their start and end apart: 7, of which 4 were waited for; matrix products, arithmetic and copies ran while one was open for 0% of the time, Pallas kernels for 5%

profile of v3, /device:TPU:0, one launch (start us, length us, event | category | flops | bytes accessed | tf_op | source)
XLA Modules:
  0.0 90.2 jit_solution(12539959191859009277)
XLA Ops:
  0.6 0.0 copy-start.1
  0.6 3.3 %collide_first.1 = (f32[8,20,16,256]{3,2,1,0:T(8,128)S(1)}, f32[8,40,256]{2,1,0:T(8,128)S(1)}, s32[8,16,128]{2,1,0:T(8,128)S(1)}) custom-call(s32[6,1,64]{2,1,0:T(1,128)} %bitcast.13, f32[8,19,16,256]{3,2,1,0:T(8,128)} %bitcast.6, f32[8,3,16,256]{3,2,1,0:T(8,128)} %bitcast.8, f32[8,16,256]{2,1,0:T(8,128)} %bitcast.10), custom_call_target="tpu_custom_call" | custom-call | tf_op jit(solution)/shard_map/collide_first/pallas_call | solution.py:692
  3.9 18.0 %all_to_all.20.faces_ref = f32[8,40,256]{2,1,0:T(8,128)S(1)} all-to-all(f32[8,40,256]{2,1,0:T(8,128)S(1)} %get-tuple-element.13), channel_id=1, replica_groups=mesh['blk'=8,'gz'=4] {'blk'}, dimensions={0} | all-to-all | bytes 655360 | tf_op jit(solution)/shard_map/all_to_all | solution.py:710
  21.9 0.1 collective-permute-start.1
  22.0 1.6 %collective-permute-start = (f32[8,8,256]{2,1,0:T(8,128)S(1)}, f32[8,8,256]{2,1,0:T(8,128)S(1)}, u32[]{:S(2)}, u32[]{:S(2)}) collective-permute-start(f32[8,8,256]{2,1,0:T(8,128)S(1)} %get-tuple-element.23), channel_id=1, source_target_pairs={{0,1},{1,0},{2,3},{3,2},{4,5},{5,4},{6,7},{7,6},{8,9},{9,8},{10,11... | collective-permute-start | bytes 196616 | tf_op jit(solution)/shard_map/ppermute | solution.py:678
  23.6 2.7 %collective-permute-done.1.second_ref = f32[8,8,256]{2,1,0:T(8,128)S(1)} collective-permute-done((f32[8,8,256]{2,1,0:T(8,128)S(1)}, f32[8,8,256]{2,1,0:T(8,128)S(1)}, u32[]{:S(2)}, u32[]{:S(2)}) %collective-permute-start.1) | collective-permute-done | bytes 65568 | tf_op jit(solution)/shard_map/ppermute | solution.py:679
  26.3 0.0 collective-permute-done.first_ref
  26.3 0.8 route.2
  27.1 14.0 %all_to_all.21.halo_ref = f32[8,40,256]{2,1,0:T(8,128)S(1)} all-to-all(f32[8,40,256]{2,1,0:T(8,128)S(1)} %route.2), channel_id=1, replica_groups=mesh['blk'=8,'gz'=4] {'blk'}, dimensions={0} | all-to-all | bytes 655360 | tf_op jit(solution)/shard_map/all_to_all | solution.py:689
  41.1 0.0 copy-done.1
  41.1 3.7 %stream_collide.1 = (f32[4,19,16,256]{3,2,1,0:T(8,128)}, f32[4,19,16,256]{3,2,1,0:T(8,128)}, f32[8,96,256]{2,1,0:T(8,128)S(1)}) custom-call(s32[8]{0:T(128)S(1)} %copy-done.1, f32[8,20,16,256]{3,2,1,0:T(8,128)S(1)} %get-tuple-element.11.before_ref, f32[8,3,16,256]{3,2,1,0:T(8,128)} %bitcast.9, f32[8,16,256]{2,1,0:T(8,128)} %bitcast.11, ...), custom_call_target="tpu_custom_call" | custom-call | tf_op jit(solution)/shard_map/stream_collide/pallas_call | solution.py:711
  44.8 0.0 copy-start.2
  44.8 0.0 copy-start
  44.8 23.0 %all_to_all.22.faces_ref.rows_ref = f32[8,96,256]{2,1,0:T(8,128)S(1)} all-to-all(f32[8,96,256]{2,1,0:T(8,128)S(1)} %get-tuple-element.16), channel_id=1, replica_groups=mesh['blk'=8,'gz'=4] {'blk'}, dimensions={0} | all-to-all | bytes 1572864 | tf_op jit(solution)/shard_map/all_to_all | solution.py:729
  67.8 0.1 collective-permute-start.3
  67.9 1.3 %collective-permute-start.2 = (f32[8,8,256]{2,1,0:T(8,128)S(1)}, f32[8,8,256]{2,1,0:T(8,128)S(1)}, u32[]{:S(2)}, u32[]{:S(2)}) collective-permute-start(f32[8,8,256]{2,1,0:T(8,128)S(1)} %get-tuple-element.21), channel_id=1, source_target_pairs={{0,1},{1,0},{2,3},{3,2},{4,5},{5,4},{6,7},{7,6},{8,9},{9,8},{10,11... | collective-permute-start | bytes 196616 | tf_op jit(solution)/shard_map/ppermute | solution.py:678
  69.2 2.8 %collective-permute-done.3.second_ref = f32[8,8,256]{2,1,0:T(8,128)S(1)} collective-permute-done((f32[8,8,256]{2,1,0:T(8,128)S(1)}, f32[8,8,256]{2,1,0:T(8,128)S(1)}, u32[]{:S(2)}, u32[]{:S(2)}) %collective-permute-start.3) | collective-permute-done | bytes 65568 | tf_op jit(solution)/shard_map/ppermute | solution.py:679
  72.0 0.0 collective-permute-done.2.first_ref
  72.0 1.5 %route.3 = f32[8,40,256]{2,1,0:T(8,128)} custom-call(s32[8,16,128]{2,1,0:T(8,128)S(1)} %get-tuple-element.12.sources_ref, f32[8,96,256]{2,1,0:T(8,128)S(1)} %all_to_all.22.faces_ref.rows_ref, f32[8,8,256]{2,1,0:T(8,128)S(1)} %collective-permute-done.2.first_ref, f32[8,8,256]{2,1,0:T(8,128)S(1)} %collective-permute-done.3.second_ref), custom_call_target="tpu_custom_call" | custom-call | tf_op jit(solution)/shard_map/route/pallas_call | solution.py:680
  73.5 3.6 %all-to-all-start.3 = ((f32[8,40,256]{2,1,0:T(8,128)}), f32[8,40,256]{2,1,0:T(8,128)S(1)}, u32[]{:S(2)}, u32[]{:S(2)}) async-start(f32[8,40,256]{2,1,0:T(8,128)} %route.3), calls=%async_computation.3 | async-start | bytes 655360 | tf_op jit(solution)/shard_map/all_to_all | solution.py:689
  77.1 0.0 copy-done.2
  77.1 3.3 %slab_rows.1 = (f32[48,16,128]{2,1,0:T(8,128)S(1)}, f32[48,2,128]{2,1,0:T(2,128)S(1)}, f32[48,2,128]{2,1,0:T(2,128)S(1)}) custom-call(s32[8]{0:T(128)S(1)} %copy-done.1, s32[1,64]{1,0:T(1,128)S(1)} %copy-done.2, f32[8,96,256]{2,1,0:T(8,128)S(1)} %all_to_all.22.faces_ref.rows_ref), custom_call_target="tpu_custom_call" | custom-call | tf_op jit(solution)/shard_map/slab_rows/pallas_call | solution.py:732
  80.4 0.1 collective-permute-start.4
  80.5 1.2 %collective-permute-start.5 = (f32[48,2,128]{2,1,0:T(2,128)S(1)}, f32[48,2,128]{2,1,0:T(2,128)S(1)}, u32[]{:S(2)}, u32[]{:S(2)}) collective-permute-start(f32[48,2,128]{2,1,0:T(2,128)S(1)} %get-tuple-element.19), channel_id=1, source_target_pairs={{0,3},{1,2},{2,1},{3,0},{4,7},{5,6},{6,5},{7,4},{8,11},{9,10},{10,... | collective-permute-start | bytes 147464 | tf_op jit(solution)/shard_map/ppermute | solution.py:742
  81.7 0.0 collective-permute-done.4.first_ref
  81.7 2.4 %collective-permute-done.5.second_ref = f32[48,2,128]{2,1,0:T(2,128)S(1)} collective-permute-done((f32[48,2,128]{2,1,0:T(2,128)S(1)}, f32[48,2,128]{2,1,0:T(2,128)S(1)}, u32[]{:S(2)}, u32[]{:S(2)}) %collective-permute-start.5) | collective-permute-done | bytes 49184 | tf_op jit(solution)/shard_map/ppermute | solution.py:742
  84.1 1.6 %slab_depth.1 = f32[48,16,128]{2,1,0:T(8,128)} custom-call(s32[8]{0:T(128)S(1)} %copy-done.1, f32[48,16,128]{2,1,0:T(8,128)S(1)} %get-tuple-element.17.rows_ref, f32[48,2,128]{2,1,0:T(2,128)S(1)} %collective-permute-done.4.first_ref, f32[48,2,128]{2,1,0:T(2,128)S(1)} %collective-permute-done.5.second_ref), custom_call_target="tpu_custom_call" | custom-call | tf_op jit(solution)/shard_map/slab_depth/pallas_call | solution.py:743
  85.7 1.8 %all-to-all-done.3.halo_ref = f32[8,40,256]{2,1,0:T(8,128)S(1)} async-done(((f32[8,40,256]{2,1,0:T(8,128)}), f32[8,40,256]{2,1,0:T(8,128)S(1)}, u32[]{:S(2)}, u32[]{:S(2)}) %all-to-all-start.3) | async-done | bytes 327712 | tf_op jit(solution)/shard_map/all_to_all | solution.py:689
  87.5 0.0 copy-done
  87.5 2.7 %stream_last.1 = f32[8,19,16,256]{3,2,1,0:T(8,128)} custom-call(f32[4,19,16,256]{3,2,1,0:T(8,128)S(1)} %copy-done, f32[4,19,16,256]{3,2,1,0:T(8,128)} %get-tuple-element.15.late_hbm, f32[8,40,256]{2,1,0:T(8,128)S(1)} %all-to-all-done.3.halo_ref), custom_call_target="tpu_custom_call" | custom-call | tf_op jit(solution)/shard_map/stream_last/pallas_call | solution.py:751
  (2 shorter events, 0.0 us)
Async XLA Ops:
  0.6 40.5 %copy-start.1 = (s32[8]{0:T(128)S(1)}, s32[8]{0:T(128)}, u32[]{:S(2)}) copy-start(s32[8]{0:T(128)} %owner_ref.3) | copy-start | bytes 100
  21.9 4.4 %collective-permute-start.1 = (f32[8,8,256]{2,1,0:T(8,128)S(1)}, f32[8,8,256]{2,1,0:T(8,128)S(1)}, u32[]{:S(2)}, u32[]{:S(2)}) collective-permute-start(f32[8,8,256]{2,1,0:T(8,128)S(1)} %get-tuple-element.22), channel_id=1, source_target_pairs={{0,3},{1,2},{2,1},{3,0},{4,7},{5,6},{6,5},{7,4},{8,11},{9,10},{10,... | collective-permute-start | bytes 196616 | tf_op jit(solution)/shard_map/ppermute | solution.py:679
  22.0 4.3 %collective-permute-start = (f32[8,8,256]{2,1,0:T(8,128)S(1)}, f32[8,8,256]{2,1,0:T(8,128)S(1)}, u32[]{:S(2)}, u32[]{:S(2)}) collective-permute-start(f32[8,8,256]{2,1,0:T(8,128)S(1)} %get-tuple-element.23), channel_id=1, source_target_pairs={{0,1},{1,0},{2,3},{3,2},{4,5},{5,4},{6,7},{7,6},{8,9},{9,8},{10,11... | collective-permute-start | bytes 196616 | tf_op jit(solution)/shard_map/ppermute | solution.py:678
  44.8 32.3 %copy-start.2 = (s32[1,64]{1,0:T(1,128)S(1)}, s32[1,64]{1,0:T(1,128)}, u32[]{:S(2)}) copy-start(s32[1,64]{1,0:T(1,128)} %column_ref.1) | copy-start | bytes 772
  44.8 42.6 %copy-start = (f32[4,19,16,256]{3,2,1,0:T(8,128)S(1)}, f32[4,19,16,256]{3,2,1,0:T(8,128)}, u32[]{:S(2)}) copy-start(f32[4,19,16,256]{3,2,1,0:T(8,128)} %get-tuple-element.14.near_ref) | copy-start | bytes 3735556
  67.8 4.2 %collective-permute-start.3 = (f32[8,8,256]{2,1,0:T(8,128)S(1)}, f32[8,8,256]{2,1,0:T(8,128)S(1)}, u32[]{:S(2)}, u32[]{:S(2)}) collective-permute-start(f32[8,8,256]{2,1,0:T(8,128)S(1)} %get-tuple-element.20), channel_id=1, source_target_pairs={{0,3},{1,2},{2,1},{3,0},{4,7},{5,6},{6,5},{7,4},{8,11},{9,10},{10,... | collective-permute-start | bytes 196616 | tf_op jit(solution)/shard_map/ppermute | solution.py:679
  67.9 4.1 %collective-permute-start.2 = (f32[8,8,256]{2,1,0:T(8,128)S(1)}, f32[8,8,256]{2,1,0:T(8,128)S(1)}, u32[]{:S(2)}, u32[]{:S(2)}) collective-permute-start(f32[8,8,256]{2,1,0:T(8,128)S(1)} %get-tuple-element.21), channel_id=1, source_target_pairs={{0,1},{1,0},{2,3},{3,2},{4,5},{5,4},{6,7},{7,6},{8,9},{9,8},{10,11... | collective-permute-start | bytes 196616 | tf_op jit(solution)/shard_map/ppermute | solution.py:678
  73.5 13.9 %all-to-all-start.3 = ((f32[8,40,256]{2,1,0:T(8,128)}), f32[8,40,256]{2,1,0:T(8,128)S(1)}, u32[]{:S(2)}, u32[]{:S(2)}) async-start(f32[8,40,256]{2,1,0:T(8,128)} %route.3), calls=%async_computation.3 | async-start | bytes 655360 | tf_op jit(solution)/shard_map/all_to_all | solution.py:689
  80.4 1.3 %collective-permute-start.4 = (f32[48,2,128]{2,1,0:T(2,128)S(1)}, f32[48,2,128]{2,1,0:T(2,128)S(1)}, u32[]{:S(2)}, u32[]{:S(2)}) collective-permute-start(f32[48,2,128]{2,1,0:T(2,128)S(1)} %get-tuple-element.18), channel_id=1, source_target_pairs={{0,1},{1,0},{2,3},{3,2},{4,5},{5,4},{6,7},{7,6},{8,9},{9,8},{10,11... | collective-permute-start | bytes 147464 | tf_op jit(solution)/shard_map/ppermute | solution.py:741
  80.5 3.6 %collective-permute-start.5 = (f32[48,2,128]{2,1,0:T(2,128)S(1)}, f32[48,2,128]{2,1,0:T(2,128)S(1)}, u32[]{:S(2)}, u32[]{:S(2)}) collective-permute-start(f32[48,2,128]{2,1,0:T(2,128)S(1)} %get-tuple-element.19), channel_id=1, source_target_pairs={{0,3},{1,2},{2,1},{3,0},{4,7},{5,6},{6,5},{7,4},{8,11},{9,10},{10,... | collective-permute-start | bytes 147464 | tf_op jit(solution)/shard_map/ppermute | solution.py:742

commit v4 on v3

--- a/solution.py
+++ b/solution.py
@@ -41,10 +41,10 @@
 DRAG_RATE = 0.3
 TAP_EDGE, TAP_NEAR = 1.0 / 3.0, 2.0 / 3.0
 
-FACE_ROWS = 40
+FACE_ROWS, HALO_ROWS = 80, 72
+Y_ROWS, FIRST, SECOND = 32, 48, 64
+SOUTH = 64
 STREAM_GROUP = 5
-FIRST, SECOND = 24, 32
-SOUTH = 64
 
 
 SOURCES = 16
@@ -114,13 +114,29 @@
     return ref[p, low : low + 8, left : left + 128]
 
 
+def x_rows(low, left):
+    at = low * 2 + left // 16
+    return slice(at, at + 8)
+
+
+def end_row(tile, left, row):
+    at = tile + left // 16 + row
+    return slice(at, at + 1)
+
+
+def halo_row(upper, left, row):
+    at = FIRST + (0 if upper else 12) + (6 if left else 0) + row
+    return slice(at, at + 1)
+
+
 def pack_faces(block, blocks, swapped, post_ref, faces_ref, edge, plane):
-    def put_ends(target, row, cells, low, high):
-        faces_ref[target, FIRST + row : FIRST + row + 1, cells] = jnp.where(swapped, high, low)
-        faces_ref[target, SECOND + row : SECOND + row + 1, cells] = jnp.where(swapped, low, high)
+    def put_ends(target, row, left, cells, low, high):
+        faces_ref[target, end_row(FIRST, left, row), cells] = jnp.where(swapped, high, low)
+        faces_ref[target, end_row(SECOND, left, row), cells] = jnp.where(swapped, low, high)
 
     lane = lanes((8, 128))
     slot, group = lane % edge, lane // edge
+    every = slice(0, 128)
     for left in range(0, plane, 128):
         cells = slice(left, left + 128)
         tiles = []
@@ -130,14 +146,15 @@
                 tile = jnp.where(slot == s, shift(part(post_ref, p, low, left), s), tile)
             for s, p in enumerate(WEST_POPS, 5):
                 tile = jnp.where(slot == s, shift(part(post_ref, p, low, left), s - (edge - 1)), tile)
-            faces_ref[block, low : low + 8, cells] = tile
+            faces_ref[block, x_rows(low, left), :] = tile
             tiles.append(tile)
-        put_ends(block, 5, cells, tiles[0][0:1], tiles[-1][7:8])
+        put_ends(block, 5, left, every, tiles[0][0:1], tiles[-1][7:8])
         for i in range(5):
             put_ends(
                 block,
                 i,
-                cells,
+                left,
+                every,
                 post_ref[UPPER_POPS[i], 0:1, cells],
                 post_ref[LOWER_POPS[i], edge - 1 : edge, cells],
             )
@@ -158,12 +175,12 @@
     def put_y(target, tiles, start, pop, left, first, row):
         cells = slice(start, start + 64)
         for half in range(2):
-            at = half * 128
-            faces_ref[target, 16:24, at + start : at + start + 64] = tiles[half][:, cells]
+            at = Y_ROWS + half * 8
+            faces_ref[target, at : at + 8, cells] = tiles[half][:, cells]
             line = jnp.where(group == first, part(post_ref, pop, half * 8, left), 0.0)
             line = pltpu.roll(line, (128 - first * edge) % 128, 1, stride=edge, stride_axis=0)
-            faces_ref[target, row + 7 : row + 8, at : at + 128] = jnp.sum(line, axis=0, keepdims=True)
-        put_ends(target, 6, cells, tiles[0][0:1, cells], tiles[1][7:8, cells])
+            faces_ref[target, end_row(row, half * 128, 7), :] = jnp.sum(line, axis=0, keepdims=True)
+        put_ends(target, 6, 0, cells, tiles[0][0:1, cells], tiles[1][7:8, cells])
 
     if block > 0:
         put_y(block - 1, north, 0, 3, 0, 0, FIRST)
@@ -184,7 +201,7 @@
     if cx != 0:
         s = EAST_POPS.index(p) if cx > 0 else 5 + WEST_POPS.index(p)
         turn = (edge - 1 if cx > 0 else 0) - s - edge * cy
-        arrived = {(z, c): shift(halo_ref[z * 8 : z * 8 + 8, c * 128 : c * 128 + 128], turn) for z in depths for c in sides}
+        arrived = {(z, c): shift(halo_ref[x_rows(z * 8, c * 128), :], turn) for z in depths for c in sides}
     if cy == 0:
         if cx != 0:
             value = {at: jnp.where(at_face, arrived[at], value[at]) for at in value}
@@ -193,14 +210,13 @@
         border = lane // edge == far
         outer = 1 if cy > 0 else 0
         if p in (3, 4):
-            row = (FIRST if cy > 0 else SECOND) + 7
             lined = lax.broadcasted_iota(jnp.int32, (8, 128), 0) == lane // edge
-            faces = [jnp.where(lined, halo_ref[row : row + 1, at : at + 128], 0.0) for at in (0, 128)]
+            faces = [jnp.where(lined, halo_ref[halo_row(cy > 0, at, 5), :], 0.0) for at in (0, 128)]
             for step in (4, 2, 1):
                 faces = [face + shift(face, step * edge) for face in faces]
         else:
             start = NORTH_POPS.index(p) * edge if cy > 0 else SOUTH + SOUTH_POPS.index(p) * edge
-            faces = [shift(halo_ref[16:24, at : at + 128], far * edge - start) for at in (0, 128)]
+            faces = [shift(halo_ref[at : at + 8, :], far * edge - start) for at in (Y_ROWS, Y_ROWS + 8)]
         moved = {}
         for z in depths:
             inner = jnp.where(border, value[z, outer], value[z, 1 - outer])
@@ -212,14 +228,14 @@
             moved[z, outer] = jnp.where(border, faces[z], rim)
         value = moved
     if cz != 0:
-        row = FIRST + UPPER_POPS.index(p) if cz > 0 else SECOND + LOWER_POPS.index(p)
+        row = UPPER_POPS.index(p) if cz > 0 else LOWER_POPS.index(p)
         outer = 1 if cz > 0 else 0
         border = lax.broadcasted_iota(jnp.int32, (8, 128), 0) == (7 if cz > 0 else 0)
         moved = {}
         for c in sides:
             turned = [shift(value[z, c], -cz, 0) for z in depths]
             moved[1 - outer, c] = jnp.where(border, turned[outer], turned[1 - outer])
-            moved[outer, c] = jnp.where(border, halo_ref[row : row + 1, c * 128 : c * 128 + 128], turned[outer])
+            moved[outer, c] = jnp.where(border, halo_ref[halo_row(cz > 0, c * 128, row), :], turned[outer])
         value = moved
     return value
 
@@ -350,7 +366,6 @@
     porosity_ref,
     post_ref,
     state_ref,
-    field_ref,
     turned_ref,
     owner_ref,
     sems,
@@ -398,9 +413,8 @@
             result(b, late_hbm, half).start()
 
         for (low, left), sens in parts.items():
-            field_ref[b * (plane // 128) + left // 128, pl.ds(low, 8), :] = (
-                before_ref[b, POPS, pl.ds(low, 8), pl.ds(left, 128)] + sens
-            )
+            sens = before_ref[b, POPS, pl.ds(low, 8), pl.ds(left, 128)] + sens
+            turned_ref[0, b * (plane // 128) + left // 128, pl.ds(low, 8), :] = sens
         return carry
 
     lax.fori_loop(0, blocks, collide, 0)
@@ -408,26 +422,25 @@
     for b in range(blocks):
         pack_faces(b, blocks, swapped, post_ref.at[b], faces_ref, edge, plane)
     held = blocks * (plane // 128)
-    lane = lanes((8, 128))
-    for m in range(4):
-        for low in (0, 8):
-            turned = [shift(field_ref[c, low : low + 8, :], -2 * m * edge) for c in range(held)]
-            for c in range(held + 1):
-                ahead = turned[min(c, held - 1)]
-                if 0 < c < held and m > 0:
-                    ahead = jnp.where(lane < 128 - 2 * m * edge, turned[c - 1], ahead)
-                elif m == 0 or c == held:
-                    ahead = turned[max(c - 1, 0)]
-                turned_ref[m, c, low : low + 8, :] = ahead
+    for c in range(held):
+        for m in range(1, 4):
+            for low in (0, 8):
+                turned_ref[m, c, low : low + 8, :] = shift(turned_ref[0, c, low : low + 8, :], -2 * m * edge)
+    lane = lanes((edge, 128))
     start = jnp.int32(0)
     for j in range(devices):
-        first = lax.div(start + 6, jnp.int32(8))
-        phase = lax.div(start + 6 - 8 * first, jnp.int32(2))
+        first = lax.div(start + 6, jnp.int32(8)) - 1
+        behind = start - 2 - 8 * first
+        phase = lax.div(behind, jnp.int32(2))
+        turned = [turned_ref[phase, jnp.clip(first + i, 0, held - 1)] for i in range(chunks + 1)]
+        kept = lane < 128 - behind * edge
         for i in range(chunks):
-            at = FACE_ROWS + 8 * i
-            value = turned_ref[phase, jnp.minimum(first + i, held)]
-            faces_ref[j, at : at + 8, 0:128] = value[0:8]
-            faces_ref[j, at : at + 8, 128:256] = value[8:16]
+            value = jnp.where(kept, turned[i], turned[i + 1])
+            at = FACE_ROWS + 16 * i
+            if at + 16 <= faces_ref.shape[1]:
+                faces_ref[j, at : at + 16, :] = value
+            else:
+                faces_ref[j, at : at + 8, :] = jnp.where(lane[0:8] < 64, value[0:8], shift(value[8:16], 64))
         start = start + 2 * owner_ref[j]
     for b in range(blocks):
         (result(b, near_hbm, 0) if b < half else result(b, late_hbm, half)).wait()
@@ -495,21 +508,21 @@
                 rim = jnp.where(group == face, arrived, turned[outer])
                 out[1 - outer] = jnp.where(level == i, inner, out[1 - outer])
                 out[outer] = jnp.where(level == i, rim, out[outer])
-        return [jnp.where(level == 7, last[c], out[c]) for c in range(2)]
+        return [jnp.where(level == 5, last[c], out[c]) for c in range(2)]
 
     def prepare(e, carry):
-        first, second = [[ref[e, :, at : at + 128] for at in sides] for ref in (first_ref, second_ref)]
+        first, second = [[ref[e, at : at + 8, :] for at in (0, 8)] for ref in (first_ref, second_ref)]
         above = [jnp.where(swapped, a, b) for a, b in zip(first, second)]
         below = [jnp.where(swapped, b, a) for a, b in zip(first, second)]
         for own, pops, row, ref in ((above, UPPER_POPS, FIRST, above_ref), (below, LOWER_POPS, SECOND, below_ref)):
-            last = [faces_ref[e, row + 7 : row + 8, at : at + 128] for at in sides]
-            for at, tile in zip(sides, z_tiles(own, pops, last)):
-                ref[e, :, at : at + 128] = tile
-        for at in sides:
-            own = faces_ref[e, 16:24, at : at + 128]
+            last = [faces_ref[e, end_row(row, left, 7), :] for left in sides]
+            for at, tile in zip((0, 8), z_tiles(own, pops, last)):
+                ref[e, at : at + 8, :] = tile
+        for at in (0, 8):
+            own = faces_ref[e, Y_ROWS + at : Y_ROWS + at + 8, :]
             east = jnp.where(x == edge - 1, shift(own, edge - 1), shift(own, -1))
             west = jnp.where(x == 0, shift(own, 1 - edge), shift(own, 1))
-            y_ref[e, :, at : at + 128] = jnp.where(in_east, east, jnp.where(in_west, west, own))
+            y_ref[e, at : at + 8, :] = jnp.where(in_east, east, jnp.where(in_west, west, own))
         return carry
 
     lax.fori_loop(0, devices, prepare, 0, unroll=2)
@@ -524,15 +537,13 @@
 
     def one(d, carry):
         row = [jnp.broadcast_to(sources_ref[d, r : r + 1, :], (8, 128)) for r in range(14)]
-        spots = [(low, at) for low in (0, 8) for at in sides]
-        x_tiles = pick(row[0], lambda e: [faces_ref[e, low : low + 8, at : at + 128] for low, at in spots])
-        for (low, at), tile in zip(spots, x_tiles):
-            halo_ref[d, low : low + 8, at : at + 128] = tile
-        y_tiles = pick(row[1], lambda e: [y_ref[e, :, at : at + 128] for at in sides])
-        for at, tile in zip(sides, y_tiles):
-            halo_ref[d, 16:24, at : at + 128] = tile
-        for pops, last, base, ref, top in ((UPPER_POPS, 2, 4, above_ref, FIRST), (LOWER_POPS, 3, 9, below_ref, SECOND)):
-            index = [jnp.where(level == 7, row[last], row[base])] * 2
+        spots = range(0, Y_ROWS, 8)
+        for at, tile in zip(spots, pick(row[0], lambda e: [faces_ref[e, at : at + 8, :] for at in spots])):
+            halo_ref[d, at : at + 8, :] = tile
+        for at, tile in zip((0, 8), pick(row[1], lambda e: [y_ref[e, at : at + 8, :] for at in (0, 8)])):
+            halo_ref[d, Y_ROWS + at : Y_ROWS + at + 8, :] = tile
+        for pops, last, base, ref, upper in ((UPPER_POPS, 2, 4, above_ref, True), (LOWER_POPS, 3, 9, below_ref, False)):
+            index = [jnp.where(level == 5, row[last], row[base])] * 2
             for i, p in enumerate(pops):
                 cx, cy, _ = VELOCITIES[p]
                 if cx != 0:
@@ -542,9 +553,10 @@
                     outer, face = (1, 7) if cy > 0 else (0, 0)
                     here = (level == i) & (group == face)
                     index[outer] = jnp.where(here, row[base + (3 if cy > 0 else 4)], index[outer])
-            for at, side in zip(sides, index):
-                (tile,) = pick(side, lambda e: [ref[e, :, at : at + 128]])
-                halo_ref[d, top : top + 8, at : at + 128] = tile
+            for left, at, side in zip(sides, (0, 8), index):
+                (tile,) = pick(side, lambda e: [ref[e, at : at + 8, :]])
+                top = halo_row(upper, left, 0).start
+                halo_ref[d, top : top + 6, :] = tile[0:6]
         return carry
 
     lax.fori_loop(0, devices, one, 0, unroll=2)
@@ -561,14 +573,15 @@
     lane = lanes((edge, width))
     height = blocks * edge
 
-    def chunk(i, carry):
+    def chunk(i):
         top = start - 2 + 8 * i
         tiles = [jnp.zeros((edge, width), jnp.float32) for _ in range(8)]
-        at = pl.multiple_of(FACE_ROWS + 8 * i, 8)
-        values = [
-            jnp.concatenate([rows_ref[e, pl.ds(at, 8), 0:128], rows_ref[e, pl.ds(at, 8), 128:256]], axis=0)
-            for e in range(devices)
-        ]
+        at = FACE_ROWS + 16 * i
+        if at + 16 <= rows_ref.shape[1]:
+            values = [rows_ref[e, at : at + 16, :] for e in range(devices)]
+        else:
+            halves = [rows_ref[e, at : at + 8, :] for e in range(devices)]
+            values = [jnp.concatenate([half, shift(half, 64)], axis=0) for half in halves]
         for r in range(0, 8, 2):
             inside = (top + r >= 0) & (top + r < height)
             block_row = lax.div(jnp.clip(top + r, 0, height - 1), jnp.int32(edge))
@@ -582,9 +595,9 @@
                     tiles[k] = jnp.where(hit, part, tiles[k])
         for r in range(8):
             field_ref[i * 8 + r] = tiles[r]
-        return carry
-
-    lax.fori_loop(0, chunks, chunk, 0)
+
+    for i in range(chunks):
+        chunk(i)
 
     def row(r):
         at = r
@@ -670,19 +683,20 @@
     first_pairs = [(g, g ^ 1) for g in range(layers)]
     second_pairs = [(g, (g + 1 if g % 2 else g - 1) % layers) for g in range(layers)]
     near_shape, late_shape = [(count,) + state.shape[1:] for count in (blocks // 2, blocks - blocks // 2)]
-    faces_shape = (devices, FACE_ROWS, plane)
+    faces_shape, halo_shape = (devices, FACE_ROWS, 128), (devices, HALO_ROWS, 128)
+    row_count = 16 * chunks - (8 if 0 < (rows_cap + 4) % 8 <= 4 else 0)
     post_shape = (blocks, POPS + 1, edge, plane)
     params = pltpu.CompilerParams(vmem_limit_bytes=32 * 1024 * 1024)
 
     def to_halo(gathered):
-        first = lax.ppermute(gathered[:, FIRST : FIRST + 8], "gz", first_pairs)
-        second = lax.ppermute(gathered[:, SECOND : SECOND + 8], "gz", second_pairs)
+        first = lax.ppermute(gathered[:, FIRST : FIRST + 16], "gz", first_pairs)
+        second = lax.ppermute(gathered[:, SECOND : SECOND + 16], "gz", second_pairs)
         halo = pl.pallas_call(
             functools.partial(route_kernel, devices),
-            out_shape=f32(*faces_shape),
+            out_shape=f32(*halo_shape),
             in_specs=[VMEM] * 4,
             out_specs=VMEM,
-            scratch_shapes=[vmem(devices, 8, plane)] * 3,
+            scratch_shapes=[vmem(devices, 16, 128)] * 3,
             compiler_params=params,
             name="route",
         )(sources, gathered, first, second)
@@ -710,15 +724,14 @@
     halo = to_halo(lax.all_to_all(faces, "blk", 0, 0, tiled=True))
     near, late, faces = pl.pallas_call(
         functools.partial(second_kernel, blocks, devices, chunks),
-        out_shape=(hbm(*near_shape), hbm(*late_shape), f32(devices, FACE_ROWS + 8 * chunks, plane)),
+        out_shape=(hbm(*near_shape), hbm(*late_shape), f32(devices, FACE_ROWS + row_count, 128)),
         in_specs=[ANY, VMEM, ANY, ANY, VMEM],
         out_specs=(ANY, ANY, VMEM),
         scratch_shapes=inputs[1:]
         + [
             vmem(*state.shape),
             vmem(*state.shape),
-            vmem(blocks * plane // 128, edge, 128),
-            vmem(4, blocks * plane // 128 + 1, edge, 128),
+            vmem(4, blocks * plane // 128, edge, 128),
             pltpu.SMEM(owner_map.shape, jnp.int32),
             pltpu.SemaphoreType.DMA((blocks,)),
             pltpu.SemaphoreType.DMA((3,)),

time: 90.6 us -> 88.5 us (0.977)
  the two profiles are of different devices: /device:TPU:0 before, /device:TPU:1 now
where the time goes in v4:
time: 88.5 us; the launch traced here: 87.1 us
  blocking collectives  49.3 us (56%)
  Pallas kernels  16.6 us (19%)
  starting transfers between devices  11.9 us (13%)
  waiting for transfers between devices  8.51 us (10%)
    all_to_all x1, blocking collectives, local(): gathered = lax.all_to_all(faces, 'blk', 0, 0, tiled=True)  22.8 us
    all_to_all x1, blocking collectives, local(): halo = to_halo(lax.all_to_all(faces, 'blk', 0, 0, tiled=True))  15.1 us
    all_to_all x1, blocking collectives, to_halo(): return lax.all_to_all(halo, 'blk', 0, 0, tiled=True)  11.3 us
    ppermute x2, starting transfers between devices, to_halo(): second = lax.ppermute(gathered[:, SECOND:SECOND + 16], 'gz', second_pairs)  6.75 us
    ppermute x2, waiting for transfers between devices, to_halo(): second = lax.ppermute(gathered[:, SECOND:SECOND + 16], 'gz', second_pairs)  5.52 us
    pallas_call x1, Pallas kernels, local(): pl.pallas_call(functools.partial(second_kernel, blocks, devices, chunks),...  3.73 us
    all_to_all x1, starting transfers between devices, to_halo(): return lax.all_to_all(halo, 'blk', 0, 0, tiled=True)  3.42 us
    pallas_call x1, Pallas kernels, local(): pl.pallas_call(functools.partial(first_kernel, blocks, devices), out_shap...  3.27 us
  transfers between devices with their start and end apart: 7, of which 3 were waited for; matrix products, arithmetic and copies ran while one was open for 0% of the time, Pallas kernels for 5%

profile of v4, /device:TPU:1, one launch (start us, length us, event | category | flops | bytes accessed | tf_op | source)
XLA Modules:
  0.0 87.1 jit_solution(2251006359113945328)
XLA Ops:
  0.6 0.0 copy-start.1
  0.6 3.3 %collide_first.1 = (f32[8,20,16,256]{3,2,1,0:T(8,128)S(1)}, f32[8,80,128]{2,1,0:T(8,128)S(1)}, s32[8,16,128]{2,1,0:T(8,128)S(1)}) custom-call(s32[6,1,64]{2,1,0:T(1,128)} %bitcast.13, f32[8,19,16,256]{3,2,1,0:T(8,128)} %bitcast.7, f32[8,3,16,256]{3,2,1,0:T(8,128)} %bitcast.8, f32[8,16,256]{2,1,0:T(8,128)} %bitcast.10), custom_call_target="tpu_custom_call" | custom-call | tf_op jit(solution)/shard_map/collide_first/pallas_call | solution.py:706
  3.9 15.1 %all_to_all.20.faces_ref = f32[8,80,128]{2,1,0:T(8,128)S(1)} all-to-all(f32[8,80,128]{2,1,0:T(8,128)S(1)} %get-tuple-element.13), channel_id=1, replica_groups=mesh['blk'=8,'gz'=4] {'blk'}, dimensions={0} | all-to-all | bytes 655360 | tf_op jit(solution)/shard_map/all_to_all | solution.py:724
  19.1 4.1 %collective-permute-start.1 = (f32[8,16,128]{2,1,0:T(8,128)S(1)}, f32[8,16,128]{2,1,0:T(8,128)S(1)}, u32[]{:S(2)}, u32[]{:S(2)}) collective-permute-start(f32[8,16,128]{2,1,0:T(8,128)S(1)} %get-tuple-element.22), channel_id=1, source_target_pairs={{0,3},{1,2},{2,1},{3,0},{4,7},{5,6},{6,5},{7,4},{8,11},{9,10},{10,... | collective-permute-start | bytes 196616 | tf_op jit(solution)/shard_map/ppermute | solution.py:693
  23.1 0.0 collective-permute-start
  23.1 2.8 %collective-permute-done.1.second_ref = f32[8,16,128]{2,1,0:T(8,128)S(1)} collective-permute-done((f32[8,16,128]{2,1,0:T(8,128)S(1)}, f32[8,16,128]{2,1,0:T(8,128)S(1)}, u32[]{:S(2)}, u32[]{:S(2)}) %collective-permute-start.1) | collective-permute-done | bytes 65568 | tf_op jit(solution)/shard_map/ppermute | solution.py:693
  26.0 0.0 collective-permute-done.first_ref
  26.0 0.8 route.2
  26.8 11.3 %all_to_all.21.halo_ref = f32[8,72,128]{2,1,0:T(8,128)S(1)} all-to-all(f32[8,72,128]{2,1,0:T(8,128)S(1)} %route.2), channel_id=1, replica_groups=mesh['blk'=8,'gz'=4] {'blk'}, dimensions={0} | all-to-all | bytes 589824 | tf_op jit(solution)/shard_map/all_to_all | solution.py:703
  38.1 0.0 copy-done.1
  38.1 3.7 %stream_collide.1 = (f32[4,19,16,256]{3,2,1,0:T(8,128)}, f32[4,19,16,256]{3,2,1,0:T(8,128)}, f32[8,184,128]{2,1,0:T(8,128)S(1)}) custom-call(s32[8]{0:T(128)S(1)} %copy-done.1, f32[8,20,16,256]{3,2,1,0:T(8,128)S(1)} %get-tuple-element.11.before_ref, f32[8,3,16,256]{3,2,1,0:T(8,128)} %bitcast.9, f32[8,16,256]{2,1,0:T(8,128)} %bitcast.11, ...), custom_call_target="tpu_custom_call" | custom-call | tf_op jit(solution)/shard_map/stream_collide/pallas_call | solution.py:725
  41.9 0.0 copy-start.2
  41.9 0.0 copy-start
  41.9 22.8 %all_to_all.22.faces_ref.rows_ref = f32[8,184,128]{2,1,0:T(8,128)S(1)} all-to-all(f32[8,184,128]{2,1,0:T(8,128)S(1)} %get-tuple-element.16), channel_id=1, replica_groups=mesh['blk'=8,'gz'=4] {'blk'}, dimensions={0} | all-to-all | bytes 1507328 | tf_op jit(solution)/shard_map/all_to_all | solution.py:742
  64.7 2.7 %collective-permute-start.3 = (f32[8,16,128]{2,1,0:T(8,128)S(1)}, f32[8,16,128]{2,1,0:T(8,128)S(1)}, u32[]{:S(2)}, u32[]{:S(2)}) collective-permute-start(f32[8,16,128]{2,1,0:T(8,128)S(1)} %get-tuple-element.20), channel_id=1, source_target_pairs={{0,3},{1,2},{2,1},{3,0},{4,7},{5,6},{6,5},{7,4},{8,11},{9,10},{10,... | collective-permute-start | bytes 196616 | tf_op jit(solution)/shard_map/ppermute | solution.py:693
  67.4 0.0 collective-permute-start.2
  67.4 2.7 %collective-permute-done.3.second_ref = f32[8,16,128]{2,1,0:T(8,128)S(1)} collective-permute-done((f32[8,16,128]{2,1,0:T(8,128)S(1)}, f32[8,16,128]{2,1,0:T(8,128)S(1)}, u32[]{:S(2)}, u32[]{:S(2)}) %collective-permute-start.3) | collective-permute-done | bytes 65568 | tf_op jit(solution)/shard_map/ppermute | solution.py:693
  70.0 0.0 collective-permute-done.2.first_ref
  70.0 1.5 %route.3 = f32[8,72,128]{2,1,0:T(8,128)} custom-call(s32[8,16,128]{2,1,0:T(8,128)S(1)} %get-tuple-element.12.sources_ref, f32[8,184,128]{2,1,0:T(8,128)S(1)} %all_to_all.22.faces_ref.rows_ref, f32[8,16,128]{2,1,0:T(8,128)S(1)} %collective-permute-done.2.first_ref, f32[8,16,128]{2,1,0:T(8,128)S(1)} %collective-permute-done.3.second_ref), custom_call_target="tpu_custom_call" | custom-call | tf_op jit(solution)/shard_map/route/pallas_call | solution.py:694
  71.5 3.4 %all-to-all-start.3 = ((f32[8,72,128]{2,1,0:T(8,128)}), f32[8,72,128]{2,1,0:T(8,128)S(1)}, u32[]{:S(2)}, u32[]{:S(2)}) async-start(f32[8,72,128]{2,1,0:T(8,128)} %route.3), calls=%async_computation.3 | async-start | bytes 589824 | tf_op jit(solution)/shard_map/all_to_all | solution.py:703
  75.0 0.0 copy-done.2
  75.0 3.0 %slab_rows.1 = (f32[48,16,128]{2,1,0:T(8,128)S(1)}, f32[48,2,128]{2,1,0:T(2,128)S(1)}, f32[48,2,128]{2,1,0:T(2,128)S(1)}) custom-call(s32[8]{0:T(128)S(1)} %copy-done.1, s32[1,64]{1,0:T(1,128)S(1)} %copy-done.2, f32[8,184,128]{2,1,0:T(8,128)S(1)} %all_to_all.22.faces_ref.rows_ref), custom_call_target="tpu_custom_call" | custom-call | tf_op jit(solution)/shard_map/slab_rows/pallas_call | solution.py:745
  78.0 0.9 %collective-permute-start.4 = (f32[48,2,128]{2,1,0:T(2,128)S(1)}, f32[48,2,128]{2,1,0:T(2,128)S(1)}, u32[]{:S(2)}, u32[]{:S(2)}) collective-permute-start(f32[48,2,128]{2,1,0:T(2,128)S(1)} %get-tuple-element.18), channel_id=1, source_target_pairs={{0,1},{1,0},{2,3},{3,2},{4,5},{5,4},{6,7},{7,6},{8,9},{9,8},{10,11... | collective-permute-start | bytes 147464 | tf_op jit(solution)/shard_map/ppermute | solution.py:754
  78.9 0.8 collective-permute-start.5
  79.7 0.0 collective-permute-done.4.first_ref
  79.7 2.9 %collective-permute-done.5.second_ref = f32[48,2,128]{2,1,0:T(2,128)S(1)} collective-permute-done((f32[48,2,128]{2,1,0:T(2,128)S(1)}, f32[48,2,128]{2,1,0:T(2,128)S(1)}, u32[]{:S(2)}, u32[]{:S(2)}) %collective-permute-start.5) | collective-permute-done | bytes 49184 | tf_op jit(solution)/shard_map/ppermute | solution.py:755
  82.7 1.6 %slab_depth.1 = f32[48,16,128]{2,1,0:T(8,128)} custom-call(s32[8]{0:T(128)S(1)} %copy-done.1, f32[48,16,128]{2,1,0:T(8,128)S(1)} %get-tuple-element.17.rows_ref, f32[48,2,128]{2,1,0:T(2,128)S(1)} %collective-permute-done.4.first_ref, f32[48,2,128]{2,1,0:T(2,128)S(1)} %collective-permute-done.5.second_ref), custom_call_target="tpu_custom_call" | custom-call | tf_op jit(solution)/shard_map/slab_depth/pallas_call | solution.py:756
  84.3 0.0 all-to-all-done.3.halo_ref
  84.3 0.0 copy-done
  84.3 2.7 %stream_last.1 = f32[8,19,16,256]{3,2,1,0:T(8,128)} custom-call(f32[4,19,16,256]{3,2,1,0:T(8,128)S(1)} %copy-done, f32[4,19,16,256]{3,2,1,0:T(8,128)} %get-tuple-element.15.late_hbm, f32[8,72,128]{2,1,0:T(8,128)S(1)} %all-to-all-done.3.halo_ref), custom_call_target="tpu_custom_call" | custom-call | tf_op jit(solution)/shard_map/stream_last/pallas_call | solution.py:764
  (2 shorter events, 0.0 us)
Async XLA Ops:
  0.6 37.5 %copy-start.1 = (s32[8]{0:T(128)S(1)}, s32[8]{0:T(128)}, u32[]{:S(2)}) copy-start(s32[8]{0:T(128)} %owner_ref.3) | copy-start | bytes 100
  19.1 6.9 %collective-permute-start.1 = (f32[8,16,128]{2,1,0:T(8,128)S(1)}, f32[8,16,128]{2,1,0:T(8,128)S(1)}, u32[]{:S(2)}, u32[]{:S(2)}) collective-permute-start(f32[8,16,128]{2,1,0:T(8,128)S(1)} %get-tuple-element.22), channel_id=1, source_target_pairs={{0,3},{1,2},{2,1},{3,0},{4,7},{5,6},{6,5},{7,4},{8,11},{9,10},{10,... | collective-permute-start | bytes 196616 | tf_op jit(solution)/shard_map/ppermute | solution.py:693
  23.1 2.9 %collective-permute-start = (f32[8,16,128]{2,1,0:T(8,128)S(1)}, f32[8,16,128]{2,1,0:T(8,128)S(1)}, u32[]{:S(2)}, u32[]{:S(2)}) collective-permute-start(f32[8,16,128]{2,1,0:T(8,128)S(1)} %get-tuple-element.23), channel_id=1, source_target_pairs={{0,1},{1,0},{2,3},{3,2},{4,5},{5,4},{6,7},{7,6},{8,9},{9,8},{10,11... | collective-permute-start | bytes 196616 | tf_op jit(solution)/shard_map/ppermute | solution.py:692
  41.9 33.1 %copy-start.2 = (s32[1,64]{1,0:T(1,128)S(1)}, s32[1,64]{1,0:T(1,128)}, u32[]{:S(2)}) copy-start(s32[1,64]{1,0:T(1,128)} %column_ref.1) | copy-start | bytes 772
  41.9 42.5 %copy-start = (f32[4,19,16,256]{3,2,1,0:T(8,128)S(1)}, f32[4,19,16,256]{3,2,1,0:T(8,128)}, u32[]{:S(2)}) copy-start(f32[4,19,16,256]{3,2,1,0:T(8,128)} %get-tuple-element.14.near_ref) | copy-start | bytes 3735556
  64.7 5.3 %collective-permute-start.3 = (f32[8,16,128]{2,1,0:T(8,128)S(1)}, f32[8,16,128]{2,1,0:T(8,128)S(1)}, u32[]{:S(2)}, u32[]{:S(2)}) collective-permute-start(f32[8,16,128]{2,1,0:T(8,128)S(1)} %get-tuple-element.20), channel_id=1, source_target_pairs={{0,3},{1,2},{2,1},{3,0},{4,7},{5,6},{6,5},{7,4},{8,11},{9,10},{10,... | collective-permute-start | bytes 196616 | tf_op jit(solution)/shard_map/ppermute | solution.py:693
  67.4 2.7 %collective-permute-start.2 = (f32[8,16,128]{2,1,0:T(8,128)S(1)}, f32[8,16,128]{2,1,0:T(8,128)S(1)}, u32[]{:S(2)}, u32[]{:S(2)}) collective-permute-start(f32[8,16,128]{2,1,0:T(8,128)S(1)} %get-tuple-element.21), channel_id=1, source_target_pairs={{0,1},{1,0},{2,3},{3,2},{4,5},{5,4},{6,7},{7,6},{8,9},{9,8},{10,11... | collective-permute-start | bytes 196616 | tf_op jit(solution)/shard_map/ppermute | solution.py:692
  71.5 12.8 %all-to-all-start.3 = ((f32[8,72,128]{2,1,0:T(8,128)}), f32[8,72,128]{2,1,0:T(8,128)S(1)}, u32[]{:S(2)}, u32[]{:S(2)}) async-start(f32[8,72,128]{2,1,0:T(8,128)} %route.3), calls=%async_computation.3 | async-start | bytes 589824 | tf_op jit(solution)/shard_map/all_to_all | solution.py:703
  78.0 1.8 %collective-permute-start.4 = (f32[48,2,128]{2,1,0:T(2,128)S(1)}, f32[48,2,128]{2,1,0:T(2,128)S(1)}, u32[]{:S(2)}, u32[]{:S(2)}) collective-permute-start(f32[48,2,128]{2,1,0:T(2,128)S(1)} %get-tuple-element.18), channel_id=1, source_target_pairs={{0,1},{1,0},{2,3},{3,2},{4,5},{5,4},{6,7},{7,6},{8,9},{9,8},{10,11... | collective-permute-start | bytes 147464 | tf_op jit(solution)/shard_map/ppermute | solution.py:754
  78.9 3.8 %collective-permute-start.5 = (f32[48,2,128]{2,1,0:T(2,128)S(1)}, f32[48,2,128]{2,1,0:T(2,128)S(1)}, u32[]{:S(2)}, u32[]{:S(2)}) collective-permute-start(f32[48,2,128]{2,1,0:T(2,128)S(1)} %get-tuple-element.19), channel_id=1, source_target_pairs={{0,3},{1,2},{2,1},{3,0},{4,7},{5,6},{6,5},{7,4},{8,11},{9,10},{10,... | collective-permute-start | bytes 147464 | tf_op jit(solution)/shard_map/ppermute | solution.py:755

commit v5 on v4

--- a/solution.py
+++ b/solution.py
@@ -41,8 +41,8 @@
 DRAG_RATE = 0.3
 TAP_EDGE, TAP_NEAR = 1.0 / 3.0, 2.0 / 3.0
 
-FACE_ROWS, HALO_ROWS = 80, 72
-Y_ROWS, FIRST, SECOND = 32, 48, 64
+FACE_ROWS, HALO_ROWS = 72, 64
+Y_ROWS, FIRST, SECOND = 24, 40, 56
 SOUTH = 64
 STREAM_GROUP = 5
 
@@ -114,9 +114,16 @@
     return ref[p, low : low + 8, left : left + 128]
 
 
-def x_rows(low, left):
-    at = low * 2 + left // 16
-    return slice(at, at + 8)
+def x_spot(p, depth, side):
+    east = p in EAST_POPS
+    i = EAST_POPS.index(p) if east else WEST_POPS.index(p)
+    if (depth, side) == (1, 1):
+        return i // 3, (10 if east else 13) + i % 3
+    return depth * 2 + side, (0 if east else 5) + i
+
+
+def from_east(slot):
+    return (slot < 5) | ((slot >= 10) & (slot < 13))
 
 
 def end_row(tile, left, row):
@@ -137,18 +144,16 @@
     lane = lanes((8, 128))
     slot, group = lane % edge, lane // edge
     every = slice(0, 128)
+    tiles = [None] * 3
+    for depth, side in ((0, 0), (0, 1), (1, 0), (1, 1)):
+        for p in EAST_POPS + WEST_POPS:
+            t, s = x_spot(p, depth, side)
+            moved = shift(part(post_ref, p, depth * 8, side * 128), s - (0 if p in EAST_POPS else edge - 1))
+            tiles[t] = moved if tiles[t] is None else jnp.where(slot == s, moved, tiles[t])
+    for t, tile in enumerate(tiles):
+        faces_ref[block, t * 8 : t * 8 + 8, :] = tile
     for left in range(0, plane, 128):
         cells = slice(left, left + 128)
-        tiles = []
-        for low in range(0, edge, 8):
-            tile = part(post_ref, EAST_POPS[0], low, left)
-            for s, p in enumerate(EAST_POPS[1:], 1):
-                tile = jnp.where(slot == s, shift(part(post_ref, p, low, left), s), tile)
-            for s, p in enumerate(WEST_POPS, 5):
-                tile = jnp.where(slot == s, shift(part(post_ref, p, low, left), s - (edge - 1)), tile)
-            faces_ref[block, x_rows(low, left), :] = tile
-            tiles.append(tile)
-        put_ends(block, 5, left, every, tiles[0][0:1], tiles[-1][7:8])
         for i in range(5):
             put_ends(
                 block,
@@ -199,9 +204,12 @@
     value = {(z, c): shift(part(source_ref, p, z * 8, c * 128), -(cx + edge * cy)) for z in depths for c in sides}
     at_face = lane % edge == (edge - 1 if cx > 0 else 0)
     if cx != 0:
-        s = EAST_POPS.index(p) if cx > 0 else 5 + WEST_POPS.index(p)
-        turn = (edge - 1 if cx > 0 else 0) - s - edge * cy
-        arrived = {(z, c): shift(halo_ref[x_rows(z * 8, c * 128), :], turn) for z in depths for c in sides}
+        arrived = {}
+        for z in depths:
+            for c in sides:
+                t, s = x_spot(p, z, c)
+                turn = (edge - 1 if cx > 0 else 0) - s - edge * cy
+                arrived[z, c] = shift(halo_ref[t * 8 : t * 8 + 8, :], turn)
     if cy == 0:
         if cx != 0:
             value = {at: jnp.where(at_face, arrived[at], value[at]) for at in value}
@@ -263,7 +271,7 @@
     far_west = jnp.where(in_north, beside(north, 0), beside(south, 0))
     in_east, in_west = east_west_groups(lane, edge)
     rows = [
-        jnp.where(lane % edge < 5, east, west),
+        jnp.where(from_east(lane % edge), east, west),
         jnp.where(
             in_east & (lane % edge == edge - 1),
             far_east,
@@ -493,10 +501,8 @@
             cx, cy, _ = VELOCITIES[p]
             if cx != 0:
                 face = edge - 1 if cx > 0 else 0
-                s = EAST_POPS.index(p) if cx > 0 else 5 + WEST_POPS.index(p)
                 for c in range(2):
-                    arrived = jnp.broadcast_to(shift(own[c][5:6], face - s), (8, 128))
-                    value = jnp.where(x == face, arrived, shift(own[c], -cx))
+                    value = jnp.where(x == face, shift(own[c], cx * (edge - 1)), shift(own[c], -cx))
                     out[c] = jnp.where(level == i, value, out[c])
             if cy != 0:
                 outer = 1 if cy > 0 else 0

time: 88.5 us -> 85.6 us (0.967)
  blocking collectives: 49.3 us -> 46.8 us
    all_to_all x1, blocking collectives: 11.3 us -> 10.1 us  [to_halo(): return lax.all_to_all(halo, 'blk', 0, 0, tiled=True)]
  transfers between devices with their start and end apart: 7 -> 7, of which waited for: 3 -> 4; matrix products, arithmetic and copies ran while one was open for 0% -> 0% of each run, Pallas kernels for 5% -> 5%
where the time goes in v5:
time: 85.6 us; the launch traced here: 84.7 us
  blocking collectives  46.8 us (55%)
  Pallas kernels  16.6 us (19%)
  starting transfers between devices  11.9 us (14%)
  waiting for transfers between devices  8.69 us (10%)
    all_to_all x1, blocking collectives, local(): gathered = lax.all_to_all(faces, 'blk', 0, 0, tiled=True)  22 us
    all_to_all x1, blocking collectives, local(): halo = to_halo(lax.all_to_all(faces, 'blk', 0, 0, tiled=True))  14.7 us
    all_to_all x1, blocking collectives, to_halo(): return lax.all_to_all(halo, 'blk', 0, 0, tiled=True)  10.1 us
    ppermute x2, starting transfers between devices, to_halo(): second = lax.ppermute(gathered[:, SECOND:SECOND + 16], 'gz', second_pairs)  7.01 us
    ppermute x2, waiting for transfers between devices, to_halo(): second = lax.ppermute(gathered[:, SECOND:SECOND + 16], 'gz', second_pairs)  5.52 us
    pallas_call x1, Pallas kernels, local(): pl.pallas_call(functools.partial(second_kernel, blocks, devices, chunks),...  3.72 us
    all_to_all x1, starting transfers between devices, to_halo(): return lax.all_to_all(halo, 'blk', 0, 0, tiled=True)  3.41 us
    pallas_call x1, Pallas kernels, local(): pl.pallas_call(functools.partial(first_kernel, blocks, devices), out_shap...  3.28 us
  transfers between devices with their start and end apart: 7, of which 4 were waited for; matrix products, arithmetic and copies ran while one was open for 0% of the time, Pallas kernels for 5%

profile of v5, /device:TPU:1, one launch (start us, length us, event | category | flops | bytes accessed | tf_op | source)
XLA Modules:
  0.0 84.7 jit_solution(1634038001552293929)
XLA Ops:
  0.6 0.0 copy-start.1
  0.6 3.3 %collide_first.1 = (f32[8,20,16,256]{3,2,1,0:T(8,128)S(1)}, f32[8,72,128]{2,1,0:T(8,128)S(1)}, s32[8,16,128]{2,1,0:T(8,128)S(1)}) custom-call(s32[6,1,64]{2,1,0:T(1,128)} %bitcast.13, f32[8,19,16,256]{3,2,1,0:T(8,128)} %bitcast.7, f32[8,3,16,256]{3,2,1,0:T(8,128)} %bitcast.8, f32[8,16,256]{2,1,0:T(8,128)} %bitcast.10), custom_call_target="tpu_custom_call" | custom-call | tf_op jit(solution)/shard_map/collide_first/pallas_call | solution.py:712
  3.9 14.7 %all_to_all.20.faces_ref = f32[8,72,128]{2,1,0:T(8,128)S(1)} all-to-all(f32[8,72,128]{2,1,0:T(8,128)S(1)} %get-tuple-element.13), channel_id=1, replica_groups=mesh['blk'=8,'gz'=4] {'blk'}, dimensions={0} | all-to-all | bytes 589824 | tf_op jit(solution)/shard_map/all_to_all | solution.py:730
  18.6 3.9 %collective-permute-start.1 = (f32[8,16,128]{2,1,0:T(8,128)S(1)}, f32[8,16,128]{2,1,0:T(8,128)S(1)}, u32[]{:S(2)}, u32[]{:S(2)}) collective-permute-start(f32[8,16,128]{2,1,0:T(8,128)S(1)} %get-tuple-element.22), channel_id=1, source_target_pairs={{0,3},{1,2},{2,1},{3,0},{4,7},{5,6},{6,5},{7,4},{8,11},{9,10},{10,... | collective-permute-start | bytes 196616 | tf_op jit(solution)/shard_map/ppermute | solution.py:699
  22.6 0.0 collective-permute-start
  22.6 2.8 %collective-permute-done.1.second_ref = f32[8,16,128]{2,1,0:T(8,128)S(1)} collective-permute-done((f32[8,16,128]{2,1,0:T(8,128)S(1)}, f32[8,16,128]{2,1,0:T(8,128)S(1)}, u32[]{:S(2)}, u32[]{:S(2)}) %collective-permute-start.1) | collective-permute-done | bytes 65568 | tf_op jit(solution)/shard_map/ppermute | solution.py:699
  25.4 0.0 collective-permute-done.first_ref
  25.4 0.8 route.2
  26.2 10.1 %all_to_all.21.halo_ref = f32[8,64,128]{2,1,0:T(8,128)S(1)} all-to-all(f32[8,64,128]{2,1,0:T(8,128)S(1)} %route.2), channel_id=1, replica_groups=mesh['blk'=8,'gz'=4] {'blk'}, dimensions={0} | all-to-all | bytes 524288 | tf_op jit(solution)/shard_map/all_to_all | solution.py:709
  36.3 0.0 copy-done.1
  36.3 3.7 %stream_collide.1 = (f32[4,19,16,256]{3,2,1,0:T(8,128)}, f32[4,19,16,256]{3,2,1,0:T(8,128)}, f32[8,176,128]{2,1,0:T(8,128)S(1)}) custom-call(s32[8]{0:T(128)S(1)} %copy-done.1, f32[8,20,16,256]{3,2,1,0:T(8,128)S(1)} %get-tuple-element.11.before_ref, f32[8,3,16,256]{3,2,1,0:T(8,128)} %bitcast.9, f32[8,16,256]{2,1,0:T(8,128)} %bitcast.11, ...), custom_call_target="tpu_custom_call" | custom-call | tf_op jit(solution)/shard_map/stream_collide/pallas_call | solution.py:731
  40.1 0.0 copy-start.2
  40.1 0.0 copy-start
  40.1 22.0 %all_to_all.22.faces_ref.rows_ref = f32[8,176,128]{2,1,0:T(8,128)S(1)} all-to-all(f32[8,176,128]{2,1,0:T(8,128)S(1)} %get-tuple-element.16), channel_id=1, replica_groups=mesh['blk'=8,'gz'=4] {'blk'}, dimensions={0} | all-to-all | bytes 1441792 | tf_op jit(solution)/shard_map/all_to_all | solution.py:748
  62.1 3.1 %collective-permute-start.3 = (f32[8,16,128]{2,1,0:T(8,128)S(1)}, f32[8,16,128]{2,1,0:T(8,128)S(1)}, u32[]{:S(2)}, u32[]{:S(2)}) collective-permute-start(f32[8,16,128]{2,1,0:T(8,128)S(1)} %get-tuple-element.20), channel_id=1, source_target_pairs={{0,3},{1,2},{2,1},{3,0},{4,7},{5,6},{6,5},{7,4},{8,11},{9,10},{10,... | collective-permute-start | bytes 196616 | tf_op jit(solution)/shard_map/ppermute | solution.py:699
  65.1 0.0 collective-permute-start.2
  65.1 2.7 %collective-permute-done.3.second_ref = f32[8,16,128]{2,1,0:T(8,128)S(1)} collective-permute-done((f32[8,16,128]{2,1,0:T(8,128)S(1)}, f32[8,16,128]{2,1,0:T(8,128)S(1)}, u32[]{:S(2)}, u32[]{:S(2)}) %collective-permute-start.3) | collective-permute-done | bytes 65568 | tf_op jit(solution)/shard_map/ppermute | solution.py:699
  67.8 0.0 collective-permute-done.2.first_ref
  67.8 1.5 %route.3 = f32[8,64,128]{2,1,0:T(8,128)} custom-call(s32[8,16,128]{2,1,0:T(8,128)S(1)} %get-tuple-element.12.sources_ref, f32[8,176,128]{2,1,0:T(8,128)S(1)} %all_to_all.22.faces_ref.rows_ref, f32[8,16,128]{2,1,0:T(8,128)S(1)} %collective-permute-done.2.first_ref, f32[8,16,128]{2,1,0:T(8,128)S(1)} %collective-permute-done.3.second_ref), custom_call_target="tpu_custom_call" | custom-call | tf_op jit(solution)/shard_map/route/pallas_call | solution.py:700
  69.3 3.4 %all-to-all-start.3 = ((f32[8,64,128]{2,1,0:T(8,128)}), f32[8,64,128]{2,1,0:T(8,128)S(1)}, u32[]{:S(2)}, u32[]{:S(2)}) async-start(f32[8,64,128]{2,1,0:T(8,128)} %route.3), calls=%async_computation.3 | async-start | bytes 524288 | tf_op jit(solution)/shard_map/all_to_all | solution.py:709
  72.7 0.0 copy-done.2
  72.7 3.0 %slab_rows.1 = (f32[48,16,128]{2,1,0:T(8,128)S(1)}, f32[48,2,128]{2,1,0:T(2,128)S(1)}, f32[48,2,128]{2,1,0:T(2,128)S(1)}) custom-call(s32[8]{0:T(128)S(1)} %copy-done.1, s32[1,64]{1,0:T(1,128)S(1)} %copy-done.2, f32[8,176,128]{2,1,0:T(8,128)S(1)} %all_to_all.22.faces_ref.rows_ref), custom_call_target="tpu_custom_call" | custom-call | tf_op jit(solution)/shard_map/slab_rows/pallas_call | solution.py:751
  75.7 0.8 collective-permute-start.4
  76.5 0.7 collective-permute-start.5
  77.2 0.2 collective-permute-done.4.first_ref
  77.4 2.9 %collective-permute-done.5.second_ref = f32[48,2,128]{2,1,0:T(2,128)S(1)} collective-permute-done((f32[48,2,128]{2,1,0:T(2,128)S(1)}, f32[48,2,128]{2,1,0:T(2,128)S(1)}, u32[]{:S(2)}, u32[]{:S(2)}) %collective-permute-start.5) | collective-permute-done | bytes 49184 | tf_op jit(solution)/shard_map/ppermute | solution.py:761
  80.3 1.6 %slab_depth.1 = f32[48,16,128]{2,1,0:T(8,128)} custom-call(s32[8]{0:T(128)S(1)} %copy-done.1, f32[48,16,128]{2,1,0:T(8,128)S(1)} %get-tuple-element.17.rows_ref, f32[48,2,128]{2,1,0:T(2,128)S(1)} %collective-permute-done.4.first_ref, f32[48,2,128]{2,1,0:T(2,128)S(1)} %collective-permute-done.5.second_ref), custom_call_target="tpu_custom_call" | custom-call | tf_op jit(solution)/shard_map/slab_depth/pallas_call | solution.py:762
  82.0 0.0 all-to-all-done.3.halo_ref
  82.0 0.0 copy-done
  82.0 2.7 %stream_last.1 = f32[8,19,16,256]{3,2,1,0:T(8,128)} custom-call(f32[4,19,16,256]{3,2,1,0:T(8,128)S(1)} %copy-done, f32[4,19,16,256]{3,2,1,0:T(8,128)} %get-tuple-element.15.late_hbm, f32[8,64,128]{2,1,0:T(8,128)S(1)} %all-to-all-done.3.halo_ref), custom_call_target="tpu_custom_call" | custom-call | tf_op jit(solution)/shard_map/stream_last/pallas_call | solution.py:770
  (2 shorter events, 0.0 us)
Async XLA Ops:
  0.6 35.7 %copy-start.1 = (s32[8]{0:T(128)S(1)}, s32[8]{0:T(128)}, u32[]{:S(2)}) copy-start(s32[8]{0:T(128)} %owner_ref.3) | copy-start | bytes 100
  18.6 6.8 %collective-permute-start.1 = (f32[8,16,128]{2,1,0:T(8,128)S(1)}, f32[8,16,128]{2,1,0:T(8,128)S(1)}, u32[]{:S(2)}, u32[]{:S(2)}) collective-permute-start(f32[8,16,128]{2,1,0:T(8,128)S(1)} %get-tuple-element.22), channel_id=1, source_target_pairs={{0,3},{1,2},{2,1},{3,0},{4,7},{5,6},{6,5},{7,4},{8,11},{9,10},{10,... | collective-permute-start | bytes 196616 | tf_op jit(solution)/shard_map/ppermute | solution.py:699
  22.6 2.9 %collective-permute-start = (f32[8,16,128]{2,1,0:T(8,128)S(1)}, f32[8,16,128]{2,1,0:T(8,128)S(1)}, u32[]{:S(2)}, u32[]{:S(2)}) collective-permute-start(f32[8,16,128]{2,1,0:T(8,128)S(1)} %get-tuple-element.23), channel_id=1, source_target_pairs={{0,1},{1,0},{2,3},{3,2},{4,5},{5,4},{6,7},{7,6},{8,9},{9,8},{10,11... | collective-permute-start | bytes 196616 | tf_op jit(solution)/shard_map/ppermute | solution.py:698
  40.1 32.6 %copy-start.2 = (s32[1,64]{1,0:T(1,128)S(1)}, s32[1,64]{1,0:T(1,128)}, u32[]{:S(2)}) copy-start(s32[1,64]{1,0:T(1,128)} %column_ref.1) | copy-start | bytes 772
  40.1 41.9 %copy-start = (f32[4,19,16,256]{3,2,1,0:T(8,128)S(1)}, f32[4,19,16,256]{3,2,1,0:T(8,128)}, u32[]{:S(2)}) copy-start(f32[4,19,16,256]{3,2,1,0:T(8,128)} %get-tuple-element.14.near_ref) | copy-start | bytes 3735556
  62.1 5.7 %collective-permute-start.3 = (f32[8,16,128]{2,1,0:T(8,128)S(1)}, f32[8,16,128]{2,1,0:T(8,128)S(1)}, u32[]{:S(2)}, u32[]{:S(2)}) collective-permute-start(f32[8,16,128]{2,1,0:T(8,128)S(1)} %get-tuple-element.20), channel_id=1, source_target_pairs={{0,3},{1,2},{2,1},{3,0},{4,7},{5,6},{6,5},{7,4},{8,11},{9,10},{10,... | collective-permute-start | bytes 196616 | tf_op jit(solution)/shard_map/ppermute | solution.py:699
  65.1 2.7 %collective-permute-start.2 = (f32[8,16,128]{2,1,0:T(8,128)S(1)}, f32[8,16,128]{2,1,0:T(8,128)S(1)}, u32[]{:S(2)}, u32[]{:S(2)}) collective-permute-start(f32[8,16,128]{2,1,0:T(8,128)S(1)} %get-tuple-element.21), channel_id=1, source_target_pairs={{0,1},{1,0},{2,3},{3,2},{4,5},{5,4},{6,7},{7,6},{8,9},{9,8},{10,11... | collective-permute-start | bytes 196616 | tf_op jit(solution)/shard_map/ppermute | solution.py:698
  69.3 12.7 %all-to-all-start.3 = ((f32[8,64,128]{2,1,0:T(8,128)}), f32[8,64,128]{2,1,0:T(8,128)S(1)}, u32[]{:S(2)}, u32[]{:S(2)}) async-start(f32[8,64,128]{2,1,0:T(8,128)} %route.3), calls=%async_computation.3 | async-start | bytes 524288 | tf_op jit(solution)/shard_map/all_to_all | solution.py:709
  75.7 1.7 %collective-permute-start.4 = (f32[48,2,128]{2,1,0:T(2,128)S(1)}, f32[48,2,128]{2,1,0:T(2,128)S(1)}, u32[]{:S(2)}, u32[]{:S(2)}) collective-permute-start(f32[48,2,128]{2,1,0:T(2,128)S(1)} %get-tuple-element.18), channel_id=1, source_target_pairs={{0,1},{1,0},{2,3},{3,2},{4,5},{5,4},{6,7},{7,6},{8,9},{9,8},{10,11... | collective-permute-start | bytes 147464 | tf_op jit(solution)/shard_map/ppermute | solution.py:760
  76.5 3.8 %collective-permute-start.5 = (f32[48,2,128]{2,1,0:T(2,128)S(1)}, f32[48,2,128]{2,1,0:T(2,128)S(1)}, u32[]{:S(2)}, u32[]{:S(2)}) collective-permute-start(f32[48,2,128]{2,1,0:T(2,128)S(1)} %get-tuple-element.19), channel_id=1, source_target_pairs={{0,3},{1,2},{2,1},{3,0},{4,7},{5,6},{6,5},{7,4},{8,11},{9,10},{10,... | collective-permute-start | bytes 147464 | tf_op jit(solution)/shard_map/ppermute | solution.py:761

commit v6 on v5

--- a/solution.py
+++ b/solution.py
@@ -41,9 +41,14 @@
 DRAG_RATE = 0.3
 TAP_EDGE, TAP_NEAR = 1.0 / 3.0, 2.0 / 3.0
 
-FACE_ROWS, HALO_ROWS = 72, 64
-Y_ROWS, FIRST, SECOND = 24, 40, 56
+FACE_ROWS = 64
+Y_ROWS, FIRST, SECOND = 24, 40, 52
 SOUTH = 64
+EAST_SLOTS = [0, 1, 2, 3, 4]
+WEST_SLOTS = [5, 8, 9, 10, 11]
+EAST_FREE = [(0, 12), (0, 6), (1, 12), (1, 6), (2, 12)]
+WEST_FREE = [(0, 13), (0, 14), (1, 13), (1, 14), (2, 13)]
+Y_SPOTS = {3: [(0, 7), (1, 7)], 4: [(2, 6), (2, 7)]}
 STREAM_GROUP = 5
 
 
@@ -118,16 +123,40 @@
     east = p in EAST_POPS
     i = EAST_POPS.index(p) if east else WEST_POPS.index(p)
     if (depth, side) == (1, 1):
-        return i // 3, (10 if east else 13) + i % 3
-    return depth * 2 + side, (0 if east else 5) + i
-
-
-def from_east(slot):
-    return (slot < 5) | ((slot >= 10) & (slot < 13))
+        return EAST_FREE[i] if east else WEST_FREE[i]
+    return depth * 2 + side, EAST_SLOTS[i] if east else WEST_SLOTS[i]
+
+
+def slot_source(slot, tile, east, west, y_face):
+    spots = [(2, s) for s in EAST_SLOTS] + EAST_FREE
+    y_slots = [s + half for pair in Y_SPOTS.values() for t, s in pair if t == tile for half in (0, 8)]
+    source = west
+    for t, s in spots:
+        if t in (tile, 2) and (t == tile or s in EAST_SLOTS):
+            source = jnp.where(slot == s, east, source)
+    for s in y_slots:
+        source = jnp.where(slot == s, y_face, source)
+    return source
+
+
+def spread(values, bases, lane):
+    places = [(lane - base) % 128 for base in bases]
+    for bit in (2, 1, 0):
+        moved = [shift(value, 15 << bit) for value in values]
+        values = [jnp.where(p & (16 << bit) != 0, m, v) for p, m, v in zip(places, moved, values)]
+    return values
+
+
+def gathered_lanes(values, bases, lane):
+    places = [(lane - base) % 128 for base in bases]
+    for bit in (0, 1, 2):
+        moved = [shift(value, -(15 << bit)) for value in values]
+        values = [jnp.where(p & (1 << bit) != 0, m, v) for p, m, v in zip(places, moved, values)]
+    return values
 
 
 def end_row(tile, left, row):
-    at = tile + left // 16 + row
+    at = tile + (6 if left else 0) + row
     return slice(at, at + 1)
 
 
@@ -136,7 +165,7 @@
     return slice(at, at + 1)
 
 
-def pack_faces(block, blocks, swapped, post_ref, faces_ref, edge, plane):
+def pack_faces(block, blocks, swapped, post_ref, lines_ref, faces_ref, edge, plane):
     def put_ends(target, row, left, cells, low, high):
         faces_ref[target, end_row(FIRST, left, row), cells] = jnp.where(swapped, high, low)
         faces_ref[target, end_row(SECOND, left, row), cells] = jnp.where(swapped, low, high)
@@ -150,6 +179,11 @@
             t, s = x_spot(p, depth, side)
             moved = shift(part(post_ref, p, depth * 8, side * 128), s - (0 if p in EAST_POPS else edge - 1))
             tiles[t] = moved if tiles[t] is None else jnp.where(slot == s, moved, tiles[t])
+    for p, beyond in ((3, block + 1), (4, block - 1)):
+        if 0 <= beyond < blocks:
+            for depth, (t, s) in enumerate(Y_SPOTS[p]):
+                at = (p - 3) * 16 + depth * 8
+                tiles[t] = jnp.where((slot == s) | (slot == s + 8), lines_ref[beyond, at : at + 8, :], tiles[t])
     for t, tile in enumerate(tiles):
         faces_ref[block, t * 8 : t * 8 + 8, :] = tile
     for left in range(0, plane, 128):
@@ -177,27 +211,47 @@
     north = y_tiles(NORTH_POPS, 0, 0)
     south = y_tiles(SOUTH_POPS, plane - 128, 4)
 
-    def put_y(target, tiles, start, pop, left, first, row):
+    def put_y(target, tiles, start):
         cells = slice(start, start + 64)
         for half in range(2):
             at = Y_ROWS + half * 8
             faces_ref[target, at : at + 8, cells] = tiles[half][:, cells]
-            line = jnp.where(group == first, part(post_ref, pop, half * 8, left), 0.0)
-            line = pltpu.roll(line, (128 - first * edge) % 128, 1, stride=edge, stride_axis=0)
-            faces_ref[target, end_row(row, half * 128, 7), :] = jnp.sum(line, axis=0, keepdims=True)
-        put_ends(target, 6, 0, cells, tiles[0][0:1, cells], tiles[1][7:8, cells])
+        put_ends(target, 5, 0, cells, tiles[0][0:1, cells], tiles[1][7:8, cells])
 
     if block > 0:
-        put_y(block - 1, north, 0, 3, 0, 0, FIRST)
+        put_y(block - 1, north, 0)
     if block < blocks - 1:
-        put_y(block + 1, south, SOUTH, 4, plane - 128, 7, SECOND)
+        put_y(block + 1, south, SOUTH)
+
+
+def y_lines(blocks, posts_ref, lines_ref, plane):
+    lane = lanes((8, 128))
+    spots = [(b, p, depth) for b in range(blocks) for p in (3, 4) for depth in (0, 1)]
+    bases = [0 if p == 3 else 112 for _, p, _ in spots]
+    lines = [part(posts_ref.at[b], p, depth * 8, 0 if p == 3 else plane - 128) for b, p, depth in spots]
+    for (b, p, depth), line, base in zip(spots, spread(lines, bases, lane), bases):
+        at = (p - 3) * 16 + depth * 8
+        lines_ref[b, at : at + 8, :] = shift(line, Y_SPOTS[p][depth][1] - base)
+
+
+def y_halos(blocks, halo_ref, lines_ref):
+    lane = lanes((8, 128))
+    spots = [(b, p, depth) for b in range(blocks) for p in (3, 4) for depth in (0, 1)]
+    bases = [Y_SPOTS[p][depth][1] for _, p, depth in spots]
+    lines = []
+    for b, p, depth in spots:
+        t = Y_SPOTS[p][depth][0]
+        lines.append(halo_ref[b, t * 8 : t * 8 + 8, :])
+    for (b, p, depth), line, base in zip(spots, gathered_lanes(lines, bases, lane), bases):
+        at = (p - 3) * 16 + depth * 8
+        lines_ref[b, at : at + 8, :] = shift(line, (112 if p == 3 else 0) - base)
 
 
 def first_partner_above():
     return lax.rem(lax.axis_index("gz").astype(jnp.int32), jnp.int32(2)) == 0
 
 
-def stream_pop(p, source_ref, halo_ref, edge):
+def stream_pop(p, source_ref, halo_ref, y_faces, edge):
     cx, cy, cz = VELOCITIES[p]
     lane = lanes((8, 128))
     sides, depths = (0, 1), (0, 1)
@@ -218,10 +272,7 @@
         border = lane // edge == far
         outer = 1 if cy > 0 else 0
         if p in (3, 4):
-            lined = lax.broadcasted_iota(jnp.int32, (8, 128), 0) == lane // edge
-            faces = [jnp.where(lined, halo_ref[halo_row(cy > 0, at, 5), :], 0.0) for at in (0, 128)]
-            for step in (4, 2, 1):
-                faces = [face + shift(face, step * edge) for face in faces]
+            faces = y_faces[p]
         else:
             start = NORTH_POPS.index(p) * edge if cy > 0 else SOUTH + SOUTH_POPS.index(p) * edge
             faces = [shift(halo_ref[at : at + 8, :], far * edge - start) for at in (Y_ROWS, Y_ROWS + 8)]
@@ -248,10 +299,12 @@
     return value
 
 
-def stream_block(source_ref, halo_ref, out_ref, edge):
+def stream_block(source_ref, halo_ref, lines_ref, out_ref, edge):
+    y_faces = {3: [lines_ref[0:8, :], lines_ref[8:16, :]], 4: [lines_ref[16:24, :], lines_ref[24:32, :]]}
+    order = [p for p in range(POPS) if p not in y_faces] + list(y_faces)
     for start in range(0, POPS, STREAM_GROUP):
-        pops = range(start, min(start + STREAM_GROUP, POPS))
-        values = [stream_pop(p, source_ref, halo_ref, edge) for p in pops]
+        pops = order[start : start + STREAM_GROUP]
+        values = [stream_pop(p, source_ref, halo_ref, y_faces, edge) for p in pops]
         for p, value in zip(pops, values):
             for (z, c), tile in value.items():
                 out_ref[p, z * 8 : z * 8 + 8, c * 128 : c * 128 + 128] = tile
@@ -271,14 +324,13 @@
     far_west = jnp.where(in_north, beside(north, 0), beside(south, 0))
     in_east, in_west = east_west_groups(lane, edge)
     rows = [
-        jnp.where(from_east(lane % edge), east, west),
+        slot_source(lane % edge, 0, east, west, north),
+        slot_source(lane % edge, 2, east, west, south),
         jnp.where(
             in_east & (lane % edge == edge - 1),
             far_east,
             jnp.where(in_west & (lane % edge == 0), far_west, near),
         ),
-        north,
-        south,
     ]
     for face, own in ((5, above), (4, below)):
         rows += [own, beside(east, face), beside(west, face), beside(north, face), beside(south, face)]
@@ -305,6 +357,7 @@
     state_ref,
     velocity_ref,
     porosity_ref,
+    lines_ref,
     table_ref,
     sems,
     sem,
@@ -347,8 +400,9 @@
         return carry
 
     lax.fori_loop(0, blocks, one, 0)
+    y_lines(blocks, post_ref, lines_ref, plane)
     for b in range(blocks):
-        pack_faces(b, blocks, swapped, post_ref.at[b], faces_ref, edge, plane)
+        pack_faces(b, blocks, swapped, post_ref.at[b], lines_ref, faces_ref, edge, plane)
 
 
 def slab_start(owner_ref, slab, devices):
@@ -374,6 +428,7 @@
     porosity_ref,
     post_ref,
     state_ref,
+    lines_ref,
     turned_ref,
     owner_ref,
     sems,
@@ -395,9 +450,10 @@
         return pltpu.make_async_copy(post_ref.at[b], out_hbm.at[b - first], sems.at[b])
 
     def stream(b, carry):
-        stream_block(before_ref.at[b], halo_ref.at[b], state_ref.at[b], edge)
+        stream_block(before_ref.at[b], halo_ref.at[b], lines_ref.at[b], state_ref.at[b], edge)
         return carry
 
+    y_halos(blocks, halo_ref, lines_ref)
     lax.fori_loop(0, blocks, stream, 0)
     for other in others:
         other.wait()
@@ -426,9 +482,10 @@
         return carry
 
     lax.fori_loop(0, blocks, collide, 0)
+    y_lines(blocks, post_ref, lines_ref, plane)
 
     for b in range(blocks):
-        pack_faces(b, blocks, swapped, post_ref.at[b], faces_ref, edge, plane)
+        pack_faces(b, blocks, swapped, post_ref.at[b], lines_ref, faces_ref, edge, plane)
     held = blocks * (plane // 128)
     for c in range(held):
         for m in range(1, 4):
@@ -454,7 +511,7 @@
         (result(b, near_hbm, 0) if b < half else result(b, late_hbm, half)).wait()
 
 
-def last_kernel(blocks, near_ref, late_hbm, halo_ref, out_hbm, late_ref, out_ref, sems):
+def last_kernel(blocks, near_ref, late_hbm, halo_ref, out_hbm, late_ref, out_ref, lines_ref, sems):
     edge = late_ref.shape[2]
     half = blocks // 2
 
@@ -468,7 +525,7 @@
         late(b).start()
 
     def one(b, before_ref):
-        stream_block(before_ref, halo_ref.at[b], out_ref.at[b], edge)
+        stream_block(before_ref, halo_ref.at[b], lines_ref.at[b], out_ref.at[b], edge)
         result(b).start()
 
     def near_one(b, carry):
@@ -480,6 +537,7 @@
         one(b, late_ref.at[b - half])
         return carry
 
+    y_halos(blocks, halo_ref, lines_ref)
     lax.fori_loop(0, half, near_one, 0)
     lax.fori_loop(half, blocks, late_one, 0)
     for b in range(blocks):
@@ -495,7 +553,7 @@
     in_east, in_west = east_west_groups(lane, edge)
     sides = (0, 128)
 
-    def z_tiles(own, pops, last):
+    def z_tiles(own, pops):
         out = list(own)
         for i, p in enumerate(pops):
             cx, cy, _ = VELOCITIES[p]
@@ -509,20 +567,20 @@
                 face = 7 if cy > 0 else 0
                 start = NORTH_POPS.index(p) * edge if cy > 0 else SOUTH + SOUTH_POPS.index(p) * edge
                 turned = [shift(side, -cy * edge) for side in own]
-                arrived = jnp.broadcast_to(shift(own[0][6:7], face * edge - start), (8, 128))
+                arrived = jnp.broadcast_to(shift(own[0][5:6], face * edge - start), (8, 128))
                 inner = jnp.where(group == face, turned[outer], turned[1 - outer])
                 rim = jnp.where(group == face, arrived, turned[outer])
                 out[1 - outer] = jnp.where(level == i, inner, out[1 - outer])
                 out[outer] = jnp.where(level == i, rim, out[outer])
-        return [jnp.where(level == 5, last[c], out[c]) for c in range(2)]
+        return out
 
     def prepare(e, carry):
-        first, second = [[ref[e, at : at + 8, :] for at in (0, 8)] for ref in (first_ref, second_ref)]
+        first = [first_ref[e, at : at + 8, :] for at in (0, 6)]
+        second = [second_ref[e, 4:12, :], shift(second_ref[e, 8:16, :], -2, 0)]
         above = [jnp.where(swapped, a, b) for a, b in zip(first, second)]
         below = [jnp.where(swapped, b, a) for a, b in zip(first, second)]
-        for own, pops, row, ref in ((above, UPPER_POPS, FIRST, above_ref), (below, LOWER_POPS, SECOND, below_ref)):
-            last = [faces_ref[e, end_row(row, left, 7), :] for left in sides]
-            for at, tile in zip((0, 8), z_tiles(own, pops, last)):
+        for own, pops, ref in ((above, UPPER_POPS, above_ref), (below, LOWER_POPS, below_ref)):
+            for at, tile in zip((0, 8), z_tiles(own, pops)):
                 ref[e, at : at + 8, :] = tile
         for at in (0, 8):
             own = faces_ref[e, Y_ROWS + at : Y_ROWS + at + 8, :]
@@ -542,14 +600,14 @@
         return total
 
     def one(d, carry):
-        row = [jnp.broadcast_to(sources_ref[d, r : r + 1, :], (8, 128)) for r in range(14)]
-        spots = range(0, Y_ROWS, 8)
-        for at, tile in zip(spots, pick(row[0], lambda e: [faces_ref[e, at : at + 8, :] for at in spots])):
-            halo_ref[d, at : at + 8, :] = tile
-        for at, tile in zip((0, 8), pick(row[1], lambda e: [y_ref[e, at : at + 8, :] for at in (0, 8)])):
+        row = [jnp.broadcast_to(sources_ref[d, r : r + 1, :], (8, 128)) for r in range(13)]
+        for index, spots in ((row[0], (0, 8)), (row[1], (16,))):
+            for at, tile in zip(spots, pick(index, lambda e: [faces_ref[e, at : at + 8, :] for at in spots])):
+                halo_ref[d, at : at + 8, :] = tile
+        for at, tile in zip((0, 8), pick(row[2], lambda e: [y_ref[e, at : at + 8, :] for at in (0, 8)])):
             halo_ref[d, Y_ROWS + at : Y_ROWS + at + 8, :] = tile
-        for pops, last, base, ref, upper in ((UPPER_POPS, 2, 4, above_ref, True), (LOWER_POPS, 3, 9, below_ref, False)):
-            index = [jnp.where(level == 5, row[last], row[base])] * 2
+        for pops, base, ref, upper in ((UPPER_POPS, 3, above_ref, True), (LOWER_POPS, 8, below_ref, False)):
+            index = [row[base]] * 2
             for i, p in enumerate(pops):
                 cx, cy, _ = VELOCITIES[p]
                 if cx != 0:
@@ -689,17 +747,17 @@
     first_pairs = [(g, g ^ 1) for g in range(layers)]
     second_pairs = [(g, (g + 1 if g % 2 else g - 1) % layers) for g in range(layers)]
     near_shape, late_shape = [(count,) + state.shape[1:] for count in (blocks // 2, blocks - blocks // 2)]
-    faces_shape, halo_shape = (devices, FACE_ROWS, 128), (devices, HALO_ROWS, 128)
+    faces_shape = (devices, FACE_ROWS, 128)
     row_count = 16 * chunks - (8 if 0 < (rows_cap + 4) % 8 <= 4 else 0)
     post_shape = (blocks, POPS + 1, edge, plane)
     params = pltpu.CompilerParams(vmem_limit_bytes=32 * 1024 * 1024)
 
     def to_halo(gathered):
         first = lax.ppermute(gathered[:, FIRST : FIRST + 16], "gz", first_pairs)
-        second = lax.ppermute(gathered[:, SECOND : SECOND + 16], "gz", second_pairs)
+        second = lax.ppermute(gathered[:, SECOND - 4 : SECOND + 12], "gz", second_pairs)
         halo = pl.pallas_call(
             functools.partial(route_kernel, devices),
-            out_shape=f32(*halo_shape),
+            out_shape=f32(*faces_shape),
             in_specs=[VMEM] * 4,
             out_specs=VMEM,
             scratch_shapes=[vmem(devices, 16, 128)] * 3,
@@ -720,6 +778,7 @@
         out_specs=(VMEM,) * 3,
         scratch_shapes=inputs
         + [
+            vmem(blocks, 32, 128),
             pltpu.SMEM(table.shape, jnp.int32),
             pltpu.SemaphoreType.DMA((blocks,)),
             pltpu.SemaphoreType.DMA((3,)),
@@ -737,6 +796,7 @@
         + [
             vmem(*state.shape),
             vmem(*state.shape),
+            vmem(blocks, 32, 128),
             vmem(4, blocks * plane // 128, edge, 128),
             pltpu.SMEM(owner_map.shape, jnp.int32),
             pltpu.SemaphoreType.DMA((blocks,)),
@@ -775,6 +835,7 @@
         scratch_shapes=[
             vmem(*late_shape),
             vmem(*state.shape),
+            vmem(blocks, 32, 128),
             pltpu.SemaphoreType.DMA((2 * blocks - blocks // 2,)),
         ],
         compiler_params=params,

time: 85.6 us -> 83.9 us (0.980)
  blocking collectives: 46.8 us -> 45.7 us
    all_to_all x1, blocking collectives: 14.7 us -> 13.5 us  [local(): halo = to_halo(lax.all_to_all(faces, 'blk', 0, 0, tiled=True))]
  transfers between devices with their start and end apart: 7 -> 7, of which waited for: 4 -> 4; matrix products, arithmetic and copies ran while one was open for 0% -> 0% of each run, Pallas kernels for 5% -> 6%
where the time goes in v6:
time: 83.9 us; the launch traced here: 83.3 us
  blocking collectives  45.7 us (54%)
  Pallas kernels  16.8 us (20%)
  starting transfers between devices  11.7 us (14%)
  waiting for transfers between devices  8.29 us (10%)
    all_to_all x1, blocking collectives, local(): gathered = lax.all_to_all(faces, 'blk', 0, 0, tiled=True)  21.4 us
    all_to_all x1, blocking collectives, local(): halo = to_halo(lax.all_to_all(faces, 'blk', 0, 0, tiled=True))  13.5 us
    all_to_all x1, blocking collectives, to_halo(): return lax.all_to_all(halo, 'blk', 0, 0, tiled=True)  10.8 us
    ppermute x2, starting transfers between devices, to_halo(): lax.ppermute(gathered[:, SECOND - 4:SECOND + 12], 'gz', second_pairs)  6.49 us
    ppermute x2, waiting for transfers between devices, to_halo(): lax.ppermute(gathered[:, SECOND - 4:SECOND + 12], 'gz', second_pairs)  5.27 us
    pallas_call x1, Pallas kernels, local(): pl.pallas_call(functools.partial(second_kernel, blocks, devices, chunks),...  3.85 us
    pallas_call x1, Pallas kernels, local(): pl.pallas_call(functools.partial(first_kernel, blocks, devices), out_shap...  3.42 us
    all_to_all x1, starting transfers between devices, to_halo(): return lax.all_to_all(halo, 'blk', 0, 0, tiled=True)  3.41 us
  transfers between devices with their start and end apart: 7, of which 4 were waited for; matrix products, arithmetic and copies ran while one was open for 0% of the time, Pallas kernels for 6%

profile of v6, /device:TPU:1, one launch (start us, length us, event | category | flops | bytes accessed | tf_op | source)
XLA Modules:
  0.0 83.3 jit_solution(9134400616211252484)
XLA Ops:
  0.6 0.0 copy-start.1
  0.6 3.4 %collide_first.1 = (f32[8,20,16,256]{3,2,1,0:T(8,128)S(1)}, f32[8,64,128]{2,1,0:T(8,128)S(1)}, s32[8,16,128]{2,1,0:T(8,128)S(1)}) custom-call(s32[6,1,64]{2,1,0:T(1,128)} %bitcast.13, f32[8,19,16,256]{3,2,1,0:T(8,128)} %bitcast.7, f32[8,3,16,256]{3,2,1,0:T(8,128)} %bitcast.8, f32[8,16,256]{2,1,0:T(8,128)} %bitcast.10), custom_call_target="tpu_custom_call" | custom-call | tf_op jit(solution)/shard_map/collide_first/pallas_call | solution.py:770
  4.1 13.5 %all_to_all.20.faces_ref = f32[8,64,128]{2,1,0:T(8,128)S(1)} all-to-all(f32[8,64,128]{2,1,0:T(8,128)S(1)} %get-tuple-element.13), channel_id=1, replica_groups=mesh['blk'=8,'gz'=4] {'blk'}, dimensions={0} | all-to-all | bytes 524288 | tf_op jit(solution)/shard_map/all_to_all | solution.py:789
  17.6 3.7 %collective-permute-start.1 = (f32[8,16,128]{2,1,0:T(8,128)S(1)}, f32[8,16,128]{2,1,0:T(8,128)S(1)}, u32[]{:S(2)}, u32[]{:S(2)}) collective-permute-start(f32[8,16,128]{2,1,0:T(8,128)S(1)} %get-tuple-element.22), channel_id=1, source_target_pairs={{0,3},{1,2},{2,1},{3,0},{4,7},{5,6},{6,5},{7,4},{8,11},{9,10},{10,... | collective-permute-start | bytes 196616 | tf_op jit(solution)/shard_map/ppermute | solution.py:757
  21.3 0.0 collective-permute-start
  21.3 2.8 %collective-permute-done.1.second_ref = f32[8,16,128]{2,1,0:T(8,128)S(1)} collective-permute-done((f32[8,16,128]{2,1,0:T(8,128)S(1)}, f32[8,16,128]{2,1,0:T(8,128)S(1)}, u32[]{:S(2)}, u32[]{:S(2)}) %collective-permute-start.1) | collective-permute-done | bytes 65568 | tf_op jit(solution)/shard_map/ppermute | solution.py:757
  24.1 0.0 collective-permute-done.first_ref
  24.1 0.8 route.2
  24.9 10.8 %all_to_all.21.halo_ref = f32[8,64,128]{2,1,0:T(8,128)S(1)} all-to-all(f32[8,64,128]{2,1,0:T(8,128)S(1)} %route.2), channel_id=1, replica_groups=mesh['blk'=8,'gz'=4] {'blk'}, dimensions={0} | all-to-all | bytes 524288 | tf_op jit(solution)/shard_map/all_to_all | solution.py:767
  35.7 0.0 copy-done.1
  35.7 3.9 %stream_collide.1 = (f32[4,19,16,256]{3,2,1,0:T(8,128)}, f32[4,19,16,256]{3,2,1,0:T(8,128)}, f32[8,168,128]{2,1,0:T(8,128)S(1)}) custom-call(s32[8]{0:T(128)S(1)} %copy-done.1, f32[8,20,16,256]{3,2,1,0:T(8,128)S(1)} %get-tuple-element.11.before_ref, f32[8,3,16,256]{3,2,1,0:T(8,128)} %bitcast.9, f32[8,16,256]{2,1,0:T(8,128)} %bitcast.11, ...), custom_call_target="tpu_custom_call" | custom-call | tf_op jit(solution)/shard_map/stream_collide/pallas_call | solution.py:790
  39.6 0.0 copy-start.2
  39.6 0.0 copy-start
  39.6 21.4 %all_to_all.22.faces_ref.rows_ref = f32[8,168,128]{2,1,0:T(8,128)S(1)} all-to-all(f32[8,168,128]{2,1,0:T(8,128)S(1)} %get-tuple-element.16), channel_id=1, replica_groups=mesh['blk'=8,'gz'=4] {'blk'}, dimensions={0} | all-to-all | bytes 1376256 | tf_op jit(solution)/shard_map/all_to_all | solution.py:808
  61.0 2.8 %collective-permute-start.3 = (f32[8,16,128]{2,1,0:T(8,128)S(1)}, f32[8,16,128]{2,1,0:T(8,128)S(1)}, u32[]{:S(2)}, u32[]{:S(2)}) collective-permute-start(f32[8,16,128]{2,1,0:T(8,128)S(1)} %get-tuple-element.20), channel_id=1, source_target_pairs={{0,3},{1,2},{2,1},{3,0},{4,7},{5,6},{6,5},{7,4},{8,11},{9,10},{10,... | collective-permute-start | bytes 196616 | tf_op jit(solution)/shard_map/ppermute | solution.py:757
  63.8 0.0 collective-permute-start.2
  63.8 2.4 %collective-permute-done.3.second_ref = f32[8,16,128]{2,1,0:T(8,128)S(1)} collective-permute-done((f32[8,16,128]{2,1,0:T(8,128)S(1)}, f32[8,16,128]{2,1,0:T(8,128)S(1)}, u32[]{:S(2)}, u32[]{:S(2)}) %collective-permute-start.3) | collective-permute-done | bytes 65568 | tf_op jit(solution)/shard_map/ppermute | solution.py:757
  66.2 0.0 collective-permute-done.2.first_ref
  66.2 1.5 %route.3 = f32[8,64,128]{2,1,0:T(8,128)} custom-call(s32[8,16,128]{2,1,0:T(8,128)S(1)} %get-tuple-element.12.sources_ref, f32[8,168,128]{2,1,0:T(8,128)S(1)} %all_to_all.22.faces_ref.rows_ref, f32[8,16,128]{2,1,0:T(8,128)S(1)} %collective-permute-done.2.first_ref, f32[8,16,128]{2,1,0:T(8,128)S(1)} %collective-permute-done.3.second_ref), custom_call_target="tpu_custom_call" | custom-call | tf_op jit(solution)/shard_map/route/pallas_call | solution.py:758
  67.7 3.4 %all-to-all-start.3 = ((f32[8,64,128]{2,1,0:T(8,128)}), f32[8,64,128]{2,1,0:T(8,128)S(1)}, u32[]{:S(2)}, u32[]{:S(2)}) async-start(f32[8,64,128]{2,1,0:T(8,128)} %route.3), calls=%async_computation.3 | async-start | bytes 524288 | tf_op jit(solution)/shard_map/all_to_all | solution.py:767
  71.1 0.0 copy-done.2
  71.1 3.0 %slab_rows.1 = (f32[48,16,128]{2,1,0:T(8,128)S(1)}, f32[48,2,128]{2,1,0:T(2,128)S(1)}, f32[48,2,128]{2,1,0:T(2,128)S(1)}) custom-call(s32[8]{0:T(128)S(1)} %copy-done.1, s32[1,64]{1,0:T(1,128)S(1)} %copy-done.2, f32[8,168,128]{2,1,0:T(8,128)S(1)} %all_to_all.22.faces_ref.rows_ref), custom_call_target="tpu_custom_call" | custom-call | tf_op jit(solution)/shard_map/slab_rows/pallas_call | solution.py:811
  74.1 1.0 %collective-permute-start.4 = (f32[48,2,128]{2,1,0:T(2,128)S(1)}, f32[48,2,128]{2,1,0:T(2,128)S(1)}, u32[]{:S(2)}, u32[]{:S(2)}) collective-permute-start(f32[48,2,128]{2,1,0:T(2,128)S(1)} %get-tuple-element.18), channel_id=1, source_target_pairs={{0,1},{1,0},{2,3},{3,2},{4,5},{5,4},{6,7},{7,6},{8,9},{9,8},{10,11... | collective-permute-start | bytes 147464 | tf_op jit(solution)/shard_map/ppermute | solution.py:820
  75.1 0.8 collective-permute-start.5
  75.9 0.1 collective-permute-done.4.first_ref
  76.0 2.9 %collective-permute-done.5.second_ref = f32[48,2,128]{2,1,0:T(2,128)S(1)} collective-permute-done((f32[48,2,128]{2,1,0:T(2,128)S(1)}, f32[48,2,128]{2,1,0:T(2,128)S(1)}, u32[]{:S(2)}, u32[]{:S(2)}) %collective-permute-start.5) | collective-permute-done | bytes 49184 | tf_op jit(solution)/shard_map/ppermute | solution.py:821
  78.9 1.6 %slab_depth.1 = f32[48,16,128]{2,1,0:T(8,128)} custom-call(s32[8]{0:T(128)S(1)} %copy-done.1, f32[48,16,128]{2,1,0:T(8,128)S(1)} %get-tuple-element.17.rows_ref, f32[48,2,128]{2,1,0:T(2,128)S(1)} %collective-permute-done.4.first_ref, f32[48,2,128]{2,1,0:T(2,128)S(1)} %collective-permute-done.5.second_ref), custom_call_target="tpu_custom_call" | custom-call | tf_op jit(solution)/shard_map/slab_depth/pallas_call | solution.py:822
  80.6 0.0 all-to-all-done.3.halo_ref
  80.6 0.0 copy-done
  80.6 2.7 %stream_last.1 = f32[8,19,16,256]{3,2,1,0:T(8,128)} custom-call(f32[4,19,16,256]{3,2,1,0:T(8,128)S(1)} %copy-done, f32[4,19,16,256]{3,2,1,0:T(8,128)} %get-tuple-element.15.late_hbm, f32[8,64,128]{2,1,0:T(8,128)S(1)} %all-to-all-done.3.halo_ref), custom_call_target="tpu_custom_call" | custom-call | tf_op jit(solution)/shard_map/stream_last/pallas_call | solution.py:830
  (2 shorter events, 0.0 us)
Async XLA Ops:
  0.6 35.1 %copy-start.1 = (s32[8]{0:T(128)S(1)}, s32[8]{0:T(128)}, u32[]{:S(2)}) copy-start(s32[8]{0:T(128)} %owner_ref.3) | copy-start | bytes 100
  17.6 6.5 %collective-permute-start.1 = (f32[8,16,128]{2,1,0:T(8,128)S(1)}, f32[8,16,128]{2,1,0:T(8,128)S(1)}, u32[]{:S(2)}, u32[]{:S(2)}) collective-permute-start(f32[8,16,128]{2,1,0:T(8,128)S(1)} %get-tuple-element.22), channel_id=1, source_target_pairs={{0,3},{1,2},{2,1},{3,0},{4,7},{5,6},{6,5},{7,4},{8,11},{9,10},{10,... | collective-permute-start | bytes 196616 | tf_op jit(solution)/shard_map/ppermute | solution.py:757
  21.3 2.9 %collective-permute-start = (f32[8,16,128]{2,1,0:T(8,128)S(1)}, f32[8,16,128]{2,1,0:T(8,128)S(1)}, u32[]{:S(2)}, u32[]{:S(2)}) collective-permute-start(f32[8,16,128]{2,1,0:T(8,128)S(1)} %get-tuple-element.23), channel_id=1, source_target_pairs={{0,1},{1,0},{2,3},{3,2},{4,5},{5,4},{6,7},{7,6},{8,9},{9,8},{10,11... | collective-permute-start | bytes 196616 | tf_op jit(solution)/shard_map/ppermute | solution.py:756
  39.6 31.5 %copy-start.2 = (s32[1,64]{1,0:T(1,128)S(1)}, s32[1,64]{1,0:T(1,128)}, u32[]{:S(2)}) copy-start(s32[1,64]{1,0:T(1,128)} %column_ref.1) | copy-start | bytes 772
  39.6 41.0 %copy-start = (f32[4,19,16,256]{3,2,1,0:T(8,128)S(1)}, f32[4,19,16,256]{3,2,1,0:T(8,128)}, u32[]{:S(2)}) copy-start(f32[4,19,16,256]{3,2,1,0:T(8,128)} %get-tuple-element.14.near_ref) | copy-start | bytes 3735556
  61.0 5.2 %collective-permute-start.3 = (f32[8,16,128]{2,1,0:T(8,128)S(1)}, f32[8,16,128]{2,1,0:T(8,128)S(1)}, u32[]{:S(2)}, u32[]{:S(2)}) collective-permute-start(f32[8,16,128]{2,1,0:T(8,128)S(1)} %get-tuple-element.20), channel_id=1, source_target_pairs={{0,3},{1,2},{2,1},{3,0},{4,7},{5,6},{6,5},{7,4},{8,11},{9,10},{10,... | collective-permute-start | bytes 196616 | tf_op jit(solution)/shard_map/ppermute | solution.py:757
  63.8 2.4 %collective-permute-start.2 = (f32[8,16,128]{2,1,0:T(8,128)S(1)}, f32[8,16,128]{2,1,0:T(8,128)S(1)}, u32[]{:S(2)}, u32[]{:S(2)}) collective-permute-start(f32[8,16,128]{2,1,0:T(8,128)S(1)} %get-tuple-element.21), channel_id=1, source_target_pairs={{0,1},{1,0},{2,3},{3,2},{4,5},{5,4},{6,7},{7,6},{8,9},{9,8},{10,11... | collective-permute-start | bytes 196616 | tf_op jit(solution)/shard_map/ppermute | solution.py:756
  67.7 12.9 %all-to-all-start.3 = ((f32[8,64,128]{2,1,0:T(8,128)}), f32[8,64,128]{2,1,0:T(8,128)S(1)}, u32[]{:S(2)}, u32[]{:S(2)}) async-start(f32[8,64,128]{2,1,0:T(8,128)} %route.3), calls=%async_computation.3 | async-start | bytes 524288 | tf_op jit(solution)/shard_map/all_to_all | solution.py:767
  74.1 1.9 %collective-permute-start.4 = (f32[48,2,128]{2,1,0:T(2,128)S(1)}, f32[48,2,128]{2,1,0:T(2,128)S(1)}, u32[]{:S(2)}, u32[]{:S(2)}) collective-permute-start(f32[48,2,128]{2,1,0:T(2,128)S(1)} %get-tuple-element.18), channel_id=1, source_target_pairs={{0,1},{1,0},{2,3},{3,2},{4,5},{5,4},{6,7},{7,6},{8,9},{9,8},{10,11... | collective-permute-start | bytes 147464 | tf_op jit(solution)/shard_map/ppermute | solution.py:820
  75.1 3.8 %collective-permute-start.5 = (f32[48,2,128]{2,1,0:T(2,128)S(1)}, f32[48,2,128]{2,1,0:T(2,128)S(1)}, u32[]{:S(2)}, u32[]{:S(2)}) collective-permute-start(f32[48,2,128]{2,1,0:T(2,128)S(1)} %get-tuple-element.19), channel_id=1, source_target_pairs={{0,3},{1,2},{2,1},{3,0},{4,7},{5,6},{6,5},{7,4},{8,11},{9,10},{10,... | collective-permute-start | bytes 147464 | tf_op jit(solution)/shard_map/ppermute | solution.py:821

commit v7 on v6

--- a/solution.py
+++ b/solution.py
@@ -32,7 +32,7 @@
 ]
 POPS = 19
 EAST_POPS = [1, 7, 9, 11, 13]
-WEST_POPS = [2, 8, 10, 12, 14]
+WEST_POPS = [2, 10, 8, 12, 14]
 NORTH_POPS = [7, 10, 15, 17]
 SOUTH_POPS = [8, 9, 16, 18]
 UPPER_POPS = [5, 11, 14, 15, 18]
@@ -44,12 +44,11 @@
 FACE_ROWS = 64
 Y_ROWS, FIRST, SECOND = 24, 40, 52
 SOUTH = 64
-EAST_SLOTS = [0, 1, 2, 3, 4]
-WEST_SLOTS = [5, 8, 9, 10, 11]
-EAST_FREE = [(0, 12), (0, 6), (1, 12), (1, 6), (2, 12)]
-WEST_FREE = [(0, 13), (0, 14), (1, 13), (1, 14), (2, 13)]
-Y_SPOTS = {3: [(0, 7), (1, 7)], 4: [(2, 6), (2, 7)]}
-STREAM_GROUP = 5
+OWN_PAIRS = [0, 1, 2, 4, 5]
+FREE_PAIRS = [(0, 6), (1, 3), (1, 6), (1, 7), (2, 6)]
+Y_SPOTS = {3: [(0, 6), (0, 7)], 4: [(2, 6), (2, 7)]}
+STREAM_ORDER = [1, 2, 7, 10, 9, 8, 11, 12, 13, 14, 0, 5, 6, 15, 16, 17, 18, 3, 4]
+STREAM_GROUP = 4
 
 
 SOURCES = 16
@@ -119,24 +118,14 @@
     return ref[p, low : low + 8, left : left + 128]
 
 
-def x_spot(p, depth, side):
-    east = p in EAST_POPS
-    i = EAST_POPS.index(p) if east else WEST_POPS.index(p)
-    if (depth, side) == (1, 1):
-        return EAST_FREE[i] if east else WEST_FREE[i]
-    return depth * 2 + side, EAST_SLOTS[i] if east else WEST_SLOTS[i]
-
-
-def slot_source(slot, tile, east, west, y_face):
-    spots = [(2, s) for s in EAST_SLOTS] + EAST_FREE
-    y_slots = [s + half for pair in Y_SPOTS.values() for t, s in pair if t == tile for half in (0, 8)]
-    source = west
-    for t, s in spots:
-        if t in (tile, 2) and (t == tile or s in EAST_SLOTS):
-            source = jnp.where(slot == s, east, source)
-    for s in y_slots:
-        source = jnp.where(slot == s, y_face, source)
-    return source
+def x_pair(p, depth, side):
+    i = EAST_POPS.index(p) if p in EAST_POPS else WEST_POPS.index(p)
+    return FREE_PAIRS[i] if (depth, side) == (1, 1) else (depth * 2 + side, OWN_PAIRS[i])
+
+
+def slot_source(slot, east, west, y_face):
+    source = jnp.where(slot % 2 == 0, east, west)
+    return source if y_face is None else jnp.where(slot % 8 >= 6, y_face, source)
 
 
 def spread(values, bases, lane):
@@ -176,8 +165,10 @@
     tiles = [None] * 3
     for depth, side in ((0, 0), (0, 1), (1, 0), (1, 1)):
         for p in EAST_POPS + WEST_POPS:
-            t, s = x_spot(p, depth, side)
-            moved = shift(part(post_ref, p, depth * 8, side * 128), s - (0 if p in EAST_POPS else edge - 1))
+            t, pair = x_pair(p, depth, side)
+            east = p in EAST_POPS
+            s = 2 * pair + (0 if east else 1)
+            moved = shift(part(post_ref, p, depth * 8, side * 128), s - (0 if east else 2 * edge - 1))
             tiles[t] = moved if tiles[t] is None else jnp.where(slot == s, moved, tiles[t])
     for p, beyond in ((3, block + 1), (4, block - 1)):
         if 0 <= beyond < blocks:
@@ -251,7 +242,7 @@
     return lax.rem(lax.axis_index("gz").astype(jnp.int32), jnp.int32(2)) == 0
 
 
-def stream_pop(p, source_ref, halo_ref, y_faces, edge):
+def stream_pop(p, source_ref, halo_ref, y_faces, x_faces, edge):
     cx, cy, cz = VELOCITIES[p]
     lane = lanes((8, 128))
     sides, depths = (0, 1), (0, 1)
@@ -261,9 +252,11 @@
         arrived = {}
         for z in depths:
             for c in sides:
-                t, s = x_spot(p, z, c)
-                turn = (edge - 1 if cx > 0 else 0) - s - edge * cy
-                arrived[z, c] = shift(halo_ref[t * 8 : t * 8 + 8, :], turn)
+                spot = x_pair(p, z, c)
+                if spot not in x_faces:
+                    t, pair = spot
+                    x_faces[spot] = shift(halo_ref[t * 8 : t * 8 + 8, :], edge - 1 - 2 * pair - edge * cy)
+                arrived[z, c] = x_faces[spot]
     if cy == 0:
         if cx != 0:
             value = {at: jnp.where(at_face, arrived[at], value[at]) for at in value}
@@ -301,10 +294,10 @@
 
 def stream_block(source_ref, halo_ref, lines_ref, out_ref, edge):
     y_faces = {3: [lines_ref[0:8, :], lines_ref[8:16, :]], 4: [lines_ref[16:24, :], lines_ref[24:32, :]]}
-    order = [p for p in range(POPS) if p not in y_faces] + list(y_faces)
+    x_faces = {}
     for start in range(0, POPS, STREAM_GROUP):
-        pops = order[start : start + STREAM_GROUP]
-        values = [stream_pop(p, source_ref, halo_ref, y_faces, edge) for p in pops]
+        pops = STREAM_ORDER[start : start + STREAM_GROUP]
+        values = [stream_pop(p, source_ref, halo_ref, y_faces, x_faces, edge) for p in pops]
         for p, value in zip(pops, values):
             for (z, c), tile in value.items():
                 out_ref[p, z * 8 : z * 8 + 8, c * 128 : c * 128 + 128] = tile
@@ -324,8 +317,9 @@
     far_west = jnp.where(in_north, beside(north, 0), beside(south, 0))
     in_east, in_west = east_west_groups(lane, edge)
     rows = [
-        slot_source(lane % edge, 0, east, west, north),
-        slot_source(lane % edge, 2, east, west, south),
+        slot_source(lane % edge, east, west, north),
+        slot_source(lane % edge, east, west, None),
+        slot_source(lane % edge, east, west, south),
         jnp.where(
             in_east & (lane % edge == edge - 1),
             far_east,
@@ -361,6 +355,7 @@
     table_ref,
     sems,
     sem,
+    flow_sems,
 ):
     edge, plane = porosity_ref.shape[1:]
     swapped = first_partner_above()
@@ -369,22 +364,27 @@
     def copy(b):
         return pltpu.make_async_copy(state_hbm.at[b], state_ref.at[b], sems.at[b])
 
-    others = [
-        pltpu.make_async_copy(table_hbm, table_ref, sem.at[0]),
-        pltpu.make_async_copy(velocity_hbm, velocity_ref, sem.at[1]),
-        pltpu.make_async_copy(porosity_hbm, porosity_ref, sem.at[2]),
-    ]
-    copy(0).start()
-    for other in others:
-        other.start()
-    for b in range(1, blocks):
+    lookup = pltpu.make_async_copy(table_hbm, table_ref, sem.at[0])
+
+    def flow(b):
+        return (
+            pltpu.make_async_copy(velocity_hbm.at[b], velocity_ref.at[b], flow_sems.at[0, b]),
+            pltpu.make_async_copy(porosity_hbm.at[b], porosity_ref.at[b], flow_sems.at[1, b]),
+        )
+
+    for b in range(blocks):
         copy(b).start()
-    for other in others:
-        other.wait()
+        for other in flow(b):
+            other.start()
+        if b == 0:
+            lookup.start()
+    lookup.wait()
     per = -(-devices // blocks)
 
     def one(b, carry):
         copy(b).wait()
+        for other in flow(b):
+            other.wait()
         parts = collide_block(
             lambda p, zs, cells: state_ref[b, p, zs, cells],
             velocity_ref.at[b],
@@ -600,13 +600,12 @@
         return total
 
     def one(d, carry):
-        row = [jnp.broadcast_to(sources_ref[d, r : r + 1, :], (8, 128)) for r in range(13)]
-        for index, spots in ((row[0], (0, 8)), (row[1], (16,))):
-            for at, tile in zip(spots, pick(index, lambda e: [faces_ref[e, at : at + 8, :] for at in spots])):
-                halo_ref[d, at : at + 8, :] = tile
-        for at, tile in zip((0, 8), pick(row[2], lambda e: [y_ref[e, at : at + 8, :] for at in (0, 8)])):
+        row = [jnp.broadcast_to(sources_ref[d, r : r + 1, :], (8, 128)) for r in range(14)]
+        for at, index in zip((0, 8, 16), row):
+            (halo_ref[d, at : at + 8, :],) = pick(index, lambda e: [faces_ref[e, at : at + 8, :]])
+        for at, tile in zip((0, 8), pick(row[3], lambda e: [y_ref[e, at : at + 8, :] for at in (0, 8)])):
             halo_ref[d, Y_ROWS + at : Y_ROWS + at + 8, :] = tile
-        for pops, base, ref, upper in ((UPPER_POPS, 3, above_ref, True), (LOWER_POPS, 8, below_ref, False)):
+        for pops, base, ref, upper in ((UPPER_POPS, 4, above_ref, True), (LOWER_POPS, 9, below_ref, False)):
             index = [row[base]] * 2
             for i, p in enumerate(pops):
                 cx, cy, _ = VELOCITIES[p]
@@ -781,7 +780,8 @@
             vmem(blocks, 32, 128),
             pltpu.SMEM(table.shape, jnp.int32),
             pltpu.SemaphoreType.DMA((blocks,)),
-            pltpu.SemaphoreType.DMA((3,)),
+            pltpu.SemaphoreType.DMA((1,)),
+            pltpu.SemaphoreType.DMA((2, blocks)),
         ],
         compiler_params=params,
         name="collide_first",

time: 83.9 us -> 83.2 us (level)
  no operation moved by 1% of the time
where the time goes in v7:
time: 83.2 us; the launch traced here: 82.6 us
  blocking collectives  45.7 us (55%)
  Pallas kernels  16.1 us (19%)
  starting transfers between devices  11.7 us (14%)
  waiting for transfers between devices  8.29 us (10%)
    all_to_all x1, blocking collectives, local(): gathered = lax.all_to_all(faces, 'blk', 0, 0, tiled=True)  21.4 us
    all_to_all x1, blocking collectives, local(): halo = to_halo(lax.all_to_all(faces, 'blk', 0, 0, tiled=True))  13.5 us
    all_to_all x1, blocking collectives, to_halo(): return lax.all_to_all(halo, 'blk', 0, 0, tiled=True)  10.8 us
    ppermute x2, starting transfers between devices, to_halo(): lax.ppermute(gathered[:, SECOND - 4:SECOND + 12], 'gz', second_pairs)  6.49 us
    ppermute x2, waiting for transfers between devices, to_halo(): lax.ppermute(gathered[:, SECOND - 4:SECOND + 12], 'gz', second_pairs)  5.27 us
    pallas_call x1, Pallas kernels, local(): pl.pallas_call(functools.partial(second_kernel, blocks, devices, chunks),...  3.68 us
    all_to_all x1, starting transfers between devices, to_halo(): return lax.all_to_all(halo, 'blk', 0, 0, tiled=True)  3.41 us
    pallas_call x1, Pallas kernels, local(): pl.pallas_call(functools.partial(first_kernel, blocks, devices), out_shap...  3.02 us
  transfers between devices with their start and end apart: 7, of which 4 were waited for; matrix products, arithmetic and copies ran while one was open for 0% of the time, Pallas kernels for 6%

profile of v7, /device:TPU:1, one launch (start us, length us, event | category | flops | bytes accessed | tf_op | source)
XLA Modules:
  0.0 82.6 jit_solution(15509911625799109782)
XLA Ops:
  0.6 0.0 copy-start.1
  0.6 3.0 %collide_first.1 = (f32[8,20,16,256]{3,2,1,0:T(8,128)S(1)}, f32[8,64,128]{2,1,0:T(8,128)S(1)}, s32[8,16,128]{2,1,0:T(8,128)S(1)}) custom-call(s32[6,1,64]{2,1,0:T(1,128)} %bitcast.13, f32[8,19,16,256]{3,2,1,0:T(8,128)} %bitcast.7, f32[8,3,16,256]{3,2,1,0:T(8,128)} %bitcast.8, f32[8,16,256]{2,1,0:T(8,128)} %bitcast.10), custom_call_target="tpu_custom_call" | custom-call | tf_op jit(solution)/shard_map/collide_first/pallas_call | solution.py:769
  3.7 13.5 %all_to_all.20.faces_ref = f32[8,64,128]{2,1,0:T(8,128)S(1)} all-to-all(f32[8,64,128]{2,1,0:T(8,128)S(1)} %get-tuple-element.13), channel_id=1, replica_groups=mesh['blk'=8,'gz'=4] {'blk'}, dimensions={0} | all-to-all | bytes 524288 | tf_op jit(solution)/shard_map/all_to_all | solution.py:789
  17.2 3.7 %collective-permute-start.1 = (f32[8,16,128]{2,1,0:T(8,128)S(1)}, f32[8,16,128]{2,1,0:T(8,128)S(1)}, u32[]{:S(2)}, u32[]{:S(2)}) collective-permute-start(f32[8,16,128]{2,1,0:T(8,128)S(1)} %get-tuple-element.22), channel_id=1, source_target_pairs={{0,3},{1,2},{2,1},{3,0},{4,7},{5,6},{6,5},{7,4},{8,11},{9,10},{10,... | collective-permute-start | bytes 196616 | tf_op jit(solution)/shard_map/ppermute | solution.py:756
  20.9 0.0 collective-permute-start
  20.9 2.8 %collective-permute-done.1.second_ref = f32[8,16,128]{2,1,0:T(8,128)S(1)} collective-permute-done((f32[8,16,128]{2,1,0:T(8,128)S(1)}, f32[8,16,128]{2,1,0:T(8,128)S(1)}, u32[]{:S(2)}, u32[]{:S(2)}) %collective-permute-start.1) | collective-permute-done | bytes 65568 | tf_op jit(solution)/shard_map/ppermute | solution.py:756
  23.8 0.0 collective-permute-done.first_ref
  23.8 0.8 route.2
  24.5 10.8 %all_to_all.21.halo_ref = f32[8,64,128]{2,1,0:T(8,128)S(1)} all-to-all(f32[8,64,128]{2,1,0:T(8,128)S(1)} %route.2), channel_id=1, replica_groups=mesh['blk'=8,'gz'=4] {'blk'}, dimensions={0} | all-to-all | bytes 524288 | tf_op jit(solution)/shard_map/all_to_all | solution.py:766
  35.3 0.0 copy-done.1
  35.3 3.7 %stream_collide.1 = (f32[4,19,16,256]{3,2,1,0:T(8,128)}, f32[4,19,16,256]{3,2,1,0:T(8,128)}, f32[8,168,128]{2,1,0:T(8,128)S(1)}) custom-call(s32[8]{0:T(128)S(1)} %copy-done.1, f32[8,20,16,256]{3,2,1,0:T(8,128)S(1)} %get-tuple-element.11.before_ref, f32[8,3,16,256]{3,2,1,0:T(8,128)} %bitcast.9, f32[8,16,256]{2,1,0:T(8,128)} %bitcast.11, ...), custom_call_target="tpu_custom_call" | custom-call | tf_op jit(solution)/shard_map/stream_collide/pallas_call | solution.py:790
  39.0 0.0 copy-start.2
  39.0 0.0 copy-start
  39.0 21.4 %all_to_all.22.faces_ref.rows_ref = f32[8,168,128]{2,1,0:T(8,128)S(1)} all-to-all(f32[8,168,128]{2,1,0:T(8,128)S(1)} %get-tuple-element.16), channel_id=1, replica_groups=mesh['blk'=8,'gz'=4] {'blk'}, dimensions={0} | all-to-all | bytes 1376256 | tf_op jit(solution)/shard_map/all_to_all | solution.py:808
  60.4 2.8 %collective-permute-start.3 = (f32[8,16,128]{2,1,0:T(8,128)S(1)}, f32[8,16,128]{2,1,0:T(8,128)S(1)}, u32[]{:S(2)}, u32[]{:S(2)}) collective-permute-start(f32[8,16,128]{2,1,0:T(8,128)S(1)} %get-tuple-element.20), channel_id=1, source_target_pairs={{0,3},{1,2},{2,1},{3,0},{4,7},{5,6},{6,5},{7,4},{8,11},{9,10},{10,... | collective-permute-start | bytes 196616 | tf_op jit(solution)/shard_map/ppermute | solution.py:756
  63.2 0.0 collective-permute-start.2
  63.2 2.4 %collective-permute-done.3.second_ref = f32[8,16,128]{2,1,0:T(8,128)S(1)} collective-permute-done((f32[8,16,128]{2,1,0:T(8,128)S(1)}, f32[8,16,128]{2,1,0:T(8,128)S(1)}, u32[]{:S(2)}, u32[]{:S(2)}) %collective-permute-start.3) | collective-permute-done | bytes 65568 | tf_op jit(solution)/shard_map/ppermute | solution.py:756
  65.7 0.0 collective-permute-done.2.first_ref
  65.7 1.5 %route.3 = f32[8,64,128]{2,1,0:T(8,128)} custom-call(s32[8,16,128]{2,1,0:T(8,128)S(1)} %get-tuple-element.12.sources_ref, f32[8,168,128]{2,1,0:T(8,128)S(1)} %all_to_all.22.faces_ref.rows_ref, f32[8,16,128]{2,1,0:T(8,128)S(1)} %collective-permute-done.2.first_ref, f32[8,16,128]{2,1,0:T(8,128)S(1)} %collective-permute-done.3.second_ref), custom_call_target="tpu_custom_call" | custom-call | tf_op jit(solution)/shard_map/route/pallas_call | solution.py:757
  67.1 3.4 %all-to-all-start.3 = ((f32[8,64,128]{2,1,0:T(8,128)}), f32[8,64,128]{2,1,0:T(8,128)S(1)}, u32[]{:S(2)}, u32[]{:S(2)}) async-start(f32[8,64,128]{2,1,0:T(8,128)} %route.3), calls=%async_computation.3 | async-start | bytes 524288 | tf_op jit(solution)/shard_map/all_to_all | solution.py:766
  70.5 0.0 copy-done.2
  70.6 3.0 %slab_rows.1 = (f32[48,16,128]{2,1,0:T(8,128)S(1)}, f32[48,2,128]{2,1,0:T(2,128)S(1)}, f32[48,2,128]{2,1,0:T(2,128)S(1)}) custom-call(s32[8]{0:T(128)S(1)} %copy-done.1, s32[1,64]{1,0:T(1,128)S(1)} %copy-done.2, f32[8,168,128]{2,1,0:T(8,128)S(1)} %all_to_all.22.faces_ref.rows_ref), custom_call_target="tpu_custom_call" | custom-call | tf_op jit(solution)/shard_map/slab_rows/pallas_call | solution.py:811
  73.6 1.0 %collective-permute-start.4 = (f32[48,2,128]{2,1,0:T(2,128)S(1)}, f32[48,2,128]{2,1,0:T(2,128)S(1)}, u32[]{:S(2)}, u32[]{:S(2)}) collective-permute-start(f32[48,2,128]{2,1,0:T(2,128)S(1)} %get-tuple-element.18), channel_id=1, source_target_pairs={{0,1},{1,0},{2,3},{3,2},{4,5},{5,4},{6,7},{7,6},{8,9},{9,8},{10,11... | collective-permute-start | bytes 147464 | tf_op jit(solution)/shard_map/ppermute | solution.py:820
  74.6 0.8 collective-permute-start.5
  75.4 0.1 collective-permute-done.4.first_ref
  75.5 2.9 %collective-permute-done.5.second_ref = f32[48,2,128]{2,1,0:T(2,128)S(1)} collective-permute-done((f32[48,2,128]{2,1,0:T(2,128)S(1)}, f32[48,2,128]{2,1,0:T(2,128)S(1)}, u32[]{:S(2)}, u32[]{:S(2)}) %collective-permute-start.5) | collective-permute-done | bytes 49184 | tf_op jit(solution)/shard_map/ppermute | solution.py:821
  78.4 1.6 %slab_depth.1 = f32[48,16,128]{2,1,0:T(8,128)} custom-call(s32[8]{0:T(128)S(1)} %copy-done.1, f32[48,16,128]{2,1,0:T(8,128)S(1)} %get-tuple-element.17.rows_ref, f32[48,2,128]{2,1,0:T(2,128)S(1)} %collective-permute-done.4.first_ref, f32[48,2,128]{2,1,0:T(2,128)S(1)} %collective-permute-done.5.second_ref), custom_call_target="tpu_custom_call" | custom-call | tf_op jit(solution)/shard_map/slab_depth/pallas_call | solution.py:822
  80.0 0.0 all-to-all-done.3.halo_ref
  80.0 0.0 copy-done
  80.0 2.5 %stream_last.1 = f32[8,19,16,256]{3,2,1,0:T(8,128)} custom-call(f32[4,19,16,256]{3,2,1,0:T(8,128)S(1)} %copy-done, f32[4,19,16,256]{3,2,1,0:T(8,128)} %get-tuple-element.15.late_hbm, f32[8,64,128]{2,1,0:T(8,128)S(1)} %all-to-all-done.3.halo_ref), custom_call_target="tpu_custom_call" | custom-call | tf_op jit(solution)/shard_map/stream_last/pallas_call | solution.py:830
  (2 shorter events, 0.0 us)
Async XLA Ops:
  0.6 34.7 %copy-start.1 = (s32[8]{0:T(128)S(1)}, s32[8]{0:T(128)}, u32[]{:S(2)}) copy-start(s32[8]{0:T(128)} %owner_ref.3) | copy-start | bytes 100
  17.2 6.5 %collective-permute-start.1 = (f32[8,16,128]{2,1,0:T(8,128)S(1)}, f32[8,16,128]{2,1,0:T(8,128)S(1)}, u32[]{:S(2)}, u32[]{:S(2)}) collective-permute-start(f32[8,16,128]{2,1,0:T(8,128)S(1)} %get-tuple-element.22), channel_id=1, source_target_pairs={{0,3},{1,2},{2,1},{3,0},{4,7},{5,6},{6,5},{7,4},{8,11},{9,10},{10,... | collective-permute-start | bytes 196616 | tf_op jit(solution)/shard_map/ppermute | solution.py:756
  20.9 2.9 %collective-permute-start = (f32[8,16,128]{2,1,0:T(8,128)S(1)}, f32[8,16,128]{2,1,0:T(8,128)S(1)}, u32[]{:S(2)}, u32[]{:S(2)}) collective-permute-start(f32[8,16,128]{2,1,0:T(8,128)S(1)} %get-tuple-element.23), channel_id=1, source_target_pairs={{0,1},{1,0},{2,3},{3,2},{4,5},{5,4},{6,7},{7,6},{8,9},{9,8},{10,11... | collective-permute-start | bytes 196616 | tf_op jit(solution)/shard_map/ppermute | solution.py:755
  39.0 31.5 %copy-start.2 = (s32[1,64]{1,0:T(1,128)S(1)}, s32[1,64]{1,0:T(1,128)}, u32[]{:S(2)}) copy-start(s32[1,64]{1,0:T(1,128)} %column_ref.1) | copy-start | bytes 772
  39.0 41.0 %copy-start = (f32[4,19,16,256]{3,2,1,0:T(8,128)S(1)}, f32[4,19,16,256]{3,2,1,0:T(8,128)}, u32[]{:S(2)}) copy-start(f32[4,19,16,256]{3,2,1,0:T(8,128)} %get-tuple-element.14.near_ref) | copy-start | bytes 3735556
  60.4 5.2 %collective-permute-start.3 = (f32[8,16,128]{2,1,0:T(8,128)S(1)}, f32[8,16,128]{2,1,0:T(8,128)S(1)}, u32[]{:S(2)}, u32[]{:S(2)}) collective-permute-start(f32[8,16,128]{2,1,0:T(8,128)S(1)} %get-tuple-element.20), channel_id=1, source_target_pairs={{0,3},{1,2},{2,1},{3,0},{4,7},{5,6},{6,5},{7,4},{8,11},{9,10},{10,... | collective-permute-start | bytes 196616 | tf_op jit(solution)/shard_map/ppermute | solution.py:756
  63.2 2.4 %collective-permute-start.2 = (f32[8,16,128]{2,1,0:T(8,128)S(1)}, f32[8,16,128]{2,1,0:T(8,128)S(1)}, u32[]{:S(2)}, u32[]{:S(2)}) collective-permute-start(f32[8,16,128]{2,1,0:T(8,128)S(1)} %get-tuple-element.21), channel_id=1, source_target_pairs={{0,1},{1,0},{2,3},{3,2},{4,5},{5,4},{6,7},{7,6},{8,9},{9,8},{10,11... | collective-permute-start | bytes 196616 | tf_op jit(solution)/shard_map/ppermute | solution.py:755
  67.1 12.9 %all-to-all-start.3 = ((f32[8,64,128]{2,1,0:T(8,128)}), f32[8,64,128]{2,1,0:T(8,128)S(1)}, u32[]{:S(2)}, u32[]{:S(2)}) async-start(f32[8,64,128]{2,1,0:T(8,128)} %route.3), calls=%async_computation.3 | async-start | bytes 524288 | tf_op jit(solution)/shard_map/all_to_all | solution.py:766
  73.6 1.9 %collective-permute-start.4 = (f32[48,2,128]{2,1,0:T(2,128)S(1)}, f32[48,2,128]{2,1,0:T(2,128)S(1)}, u32[]{:S(2)}, u32[]{:S(2)}) collective-permute-start(f32[48,2,128]{2,1,0:T(2,128)S(1)} %get-tuple-element.18), channel_id=1, source_target_pairs={{0,1},{1,0},{2,3},{3,2},{4,5},{5,4},{6,7},{7,6},{8,9},{9,8},{10,11... | collective-permute-start | bytes 147464 | tf_op jit(solution)/shard_map/ppermute | solution.py:820
  74.6 3.8 %collective-permute-start.5 = (f32[48,2,128]{2,1,0:T(2,128)S(1)}, f32[48,2,128]{2,1,0:T(2,128)S(1)}, u32[]{:S(2)}, u32[]{:S(2)}) collective-permute-start(f32[48,2,128]{2,1,0:T(2,128)S(1)} %get-tuple-element.19), channel_id=1, source_target_pairs={{0,3},{1,2},{2,1},{3,0},{4,7},{5,6},{6,5},{7,4},{8,11},{9,10},{10,... | collective-permute-start | bytes 147464 | tf_op jit(solution)/shard_map/ppermute | solution.py:821

commit v8 on v7

--- a/solution.py
+++ b/solution.py
@@ -589,7 +589,7 @@
             y_ref[e, at : at + 8, :] = jnp.where(in_east, east, jnp.where(in_west, west, own))
         return carry
 
-    lax.fori_loop(0, devices, prepare, 0, unroll=2)
+    lax.fori_loop(0, devices, prepare, 0, unroll=8)
 
     def pick(index, tiles_of):
         total = None
@@ -622,7 +622,7 @@
                 halo_ref[d, top : top + 6, :] = tile[0:6]
         return carry
 
-    lax.fori_loop(0, devices, one, 0, unroll=2)
+    lax.fori_loop(0, devices, one, 0, unroll=8)
 
 
 def slab_kernel(

time: 83.2 us -> 82.6 us (level)
  no operation moved by 1% of the time
where the time goes in v8:
time: 82.6 us; the launch traced here: 81.9 us
  blocking collectives  45.7 us (55%)
  Pallas kernels  15.5 us (19%)
  starting transfers between devices  11.7 us (14%)
  waiting for transfers between devices  8.29 us (10%)
    all_to_all x1, blocking collectives, local(): gathered = lax.all_to_all(faces, 'blk', 0, 0, tiled=True)  21.4 us
    all_to_all x1, blocking collectives, local(): halo = to_halo(lax.all_to_all(faces, 'blk', 0, 0, tiled=True))  13.5 us
    all_to_all x1, blocking collectives, to_halo(): return lax.all_to_all(halo, 'blk', 0, 0, tiled=True)  10.8 us
    ppermute x2, starting transfers between devices, to_halo(): lax.ppermute(gathered[:, SECOND - 4:SECOND + 12], 'gz', second_pairs)  6.49 us
    ppermute x2, waiting for transfers between devices, to_halo(): lax.ppermute(gathered[:, SECOND - 4:SECOND + 12], 'gz', second_pairs)  5.27 us
    pallas_call x1, Pallas kernels, local(): pl.pallas_call(functools.partial(second_kernel, blocks, devices, chunks),...  3.68 us
    all_to_all x1, starting transfers between devices, to_halo(): return lax.all_to_all(halo, 'blk', 0, 0, tiled=True)  3.41 us
    pallas_call x1, Pallas kernels, local(): pl.pallas_call(functools.partial(first_kernel, blocks, devices), out_shap...  3.02 us
  transfers between devices with their start and end apart: 7, of which 4 were waited for; matrix products, arithmetic and copies ran while one was open for 0% of the time, Pallas kernels for 6%

profile of v8, /device:TPU:1, one launch (start us, length us, event | category | flops | bytes accessed | tf_op | source)
XLA Modules:
  0.0 81.9 jit_solution(7645851434962415636)
XLA Ops:
  0.6 0.0 copy-start.1
  0.6 3.0 %collide_first.1 = (f32[8,20,16,256]{3,2,1,0:T(8,128)S(1)}, f32[8,64,128]{2,1,0:T(8,128)S(1)}, s32[8,16,128]{2,1,0:T(8,128)S(1)}) custom-call(s32[6,1,64]{2,1,0:T(1,128)} %bitcast.13, f32[8,19,16,256]{3,2,1,0:T(8,128)} %bitcast.7, f32[8,3,16,256]{3,2,1,0:T(8,128)} %bitcast.8, f32[8,16,256]{2,1,0:T(8,128)} %bitcast.10), custom_call_target="tpu_custom_call" | custom-call | tf_op jit(solution)/shard_map/collide_first/pallas_call | solution.py:769
  3.7 13.5 %all_to_all.20.faces_ref = f32[8,64,128]{2,1,0:T(8,128)S(1)} all-to-all(f32[8,64,128]{2,1,0:T(8,128)S(1)} %get-tuple-element.13), channel_id=1, replica_groups=mesh['blk'=8,'gz'=4] {'blk'}, dimensions={0} | all-to-all | bytes 524288 | tf_op jit(solution)/shard_map/all_to_all | solution.py:789
  17.2 3.7 %collective-permute-start.1 = (f32[8,16,128]{2,1,0:T(8,128)S(1)}, f32[8,16,128]{2,1,0:T(8,128)S(1)}, u32[]{:S(2)}, u32[]{:S(2)}) collective-permute-start(f32[8,16,128]{2,1,0:T(8,128)S(1)} %get-tuple-element.22), channel_id=1, source_target_pairs={{0,3},{1,2},{2,1},{3,0},{4,7},{5,6},{6,5},{7,4},{8,11},{9,10},{10,... | collective-permute-start | bytes 196616 | tf_op jit(solution)/shard_map/ppermute | solution.py:756
  20.9 0.0 collective-permute-start
  20.9 2.8 %collective-permute-done.1.second_ref = f32[8,16,128]{2,1,0:T(8,128)S(1)} collective-permute-done((f32[8,16,128]{2,1,0:T(8,128)S(1)}, f32[8,16,128]{2,1,0:T(8,128)S(1)}, u32[]{:S(2)}, u32[]{:S(2)}) %collective-permute-start.1) | collective-permute-done | bytes 65568 | tf_op jit(solution)/shard_map/ppermute | solution.py:756
  23.8 0.0 collective-permute-done.first_ref
  23.8 0.5 route.2
  24.2 10.8 %all_to_all.21.halo_ref = f32[8,64,128]{2,1,0:T(8,128)S(1)} all-to-all(f32[8,64,128]{2,1,0:T(8,128)S(1)} %route.2), channel_id=1, replica_groups=mesh['blk'=8,'gz'=4] {'blk'}, dimensions={0} | all-to-all | bytes 524288 | tf_op jit(solution)/shard_map/all_to_all | solution.py:766
  35.0 0.0 copy-done.1
  35.0 3.7 %stream_collide.1 = (f32[4,19,16,256]{3,2,1,0:T(8,128)}, f32[4,19,16,256]{3,2,1,0:T(8,128)}, f32[8,168,128]{2,1,0:T(8,128)S(1)}) custom-call(s32[8]{0:T(128)S(1)} %copy-done.1, f32[8,20,16,256]{3,2,1,0:T(8,128)S(1)} %get-tuple-element.11.before_ref, f32[8,3,16,256]{3,2,1,0:T(8,128)} %bitcast.9, f32[8,16,256]{2,1,0:T(8,128)} %bitcast.11, ...), custom_call_target="tpu_custom_call" | custom-call | tf_op jit(solution)/shard_map/stream_collide/pallas_call | solution.py:790
  38.7 0.0 copy-start.2
  38.7 0.0 copy-start
  38.7 21.4 %all_to_all.22.faces_ref.rows_ref = f32[8,168,128]{2,1,0:T(8,128)S(1)} all-to-all(f32[8,168,128]{2,1,0:T(8,128)S(1)} %get-tuple-element.16), channel_id=1, replica_groups=mesh['blk'=8,'gz'=4] {'blk'}, dimensions={0} | all-to-all | bytes 1376256 | tf_op jit(solution)/shard_map/all_to_all | solution.py:808
  60.1 2.8 %collective-permute-start.3 = (f32[8,16,128]{2,1,0:T(8,128)S(1)}, f32[8,16,128]{2,1,0:T(8,128)S(1)}, u32[]{:S(2)}, u32[]{:S(2)}) collective-permute-start(f32[8,16,128]{2,1,0:T(8,128)S(1)} %get-tuple-element.20), channel_id=1, source_target_pairs={{0,3},{1,2},{2,1},{3,0},{4,7},{5,6},{6,5},{7,4},{8,11},{9,10},{10,... | collective-permute-start | bytes 196616 | tf_op jit(solution)/shard_map/ppermute | solution.py:756
  62.9 0.0 collective-permute-start.2
  62.9 2.4 %collective-permute-done.3.second_ref = f32[8,16,128]{2,1,0:T(8,128)S(1)} collective-permute-done((f32[8,16,128]{2,1,0:T(8,128)S(1)}, f32[8,16,128]{2,1,0:T(8,128)S(1)}, u32[]{:S(2)}, u32[]{:S(2)}) %collective-permute-start.3) | collective-permute-done | bytes 65568 | tf_op jit(solution)/shard_map/ppermute | solution.py:756
  65.3 0.0 collective-permute-done.2.first_ref
  65.3 1.2 %route.3 = f32[8,64,128]{2,1,0:T(8,128)} custom-call(s32[8,16,128]{2,1,0:T(8,128)S(1)} %get-tuple-element.12.sources_ref, f32[8,168,128]{2,1,0:T(8,128)S(1)} %all_to_all.22.faces_ref.rows_ref, f32[8,16,128]{2,1,0:T(8,128)S(1)} %collective-permute-done.2.first_ref, f32[8,16,128]{2,1,0:T(8,128)S(1)} %collective-permute-done.3.second_ref), custom_call_target="tpu_custom_call" | custom-call | tf_op jit(solution)/shard_map/route/pallas_call | solution.py:757
  66.5 3.4 %all-to-all-start.3 = ((f32[8,64,128]{2,1,0:T(8,128)}), f32[8,64,128]{2,1,0:T(8,128)S(1)}, u32[]{:S(2)}, u32[]{:S(2)}) async-start(f32[8,64,128]{2,1,0:T(8,128)} %route.3), calls=%async_computation.3 | async-start | bytes 524288 | tf_op jit(solution)/shard_map/all_to_all | solution.py:766
  69.9 0.0 copy-done.2
  69.9 3.0 %slab_rows.1 = (f32[48,16,128]{2,1,0:T(8,128)S(1)}, f32[48,2,128]{2,1,0:T(2,128)S(1)}, f32[48,2,128]{2,1,0:T(2,128)S(1)}) custom-call(s32[8]{0:T(128)S(1)} %copy-done.1, s32[1,64]{1,0:T(1,128)S(1)} %copy-done.2, f32[8,168,128]{2,1,0:T(8,128)S(1)} %all_to_all.22.faces_ref.rows_ref), custom_call_target="tpu_custom_call" | custom-call | tf_op jit(solution)/shard_map/slab_rows/pallas_call | solution.py:811
  72.9 1.0 %collective-permute-start.4 = (f32[48,2,128]{2,1,0:T(2,128)S(1)}, f32[48,2,128]{2,1,0:T(2,128)S(1)}, u32[]{:S(2)}, u32[]{:S(2)}) collective-permute-start(f32[48,2,128]{2,1,0:T(2,128)S(1)} %get-tuple-element.18), channel_id=1, source_target_pairs={{0,1},{1,0},{2,3},{3,2},{4,5},{5,4},{6,7},{7,6},{8,9},{9,8},{10,11... | collective-permute-start | bytes 147464 | tf_op jit(solution)/shard_map/ppermute | solution.py:820
  74.0 0.8 collective-permute-start.5
  74.8 0.1 collective-permute-done.4.first_ref
  74.8 2.9 %collective-permute-done.5.second_ref = f32[48,2,128]{2,1,0:T(2,128)S(1)} collective-permute-done((f32[48,2,128]{2,1,0:T(2,128)S(1)}, f32[48,2,128]{2,1,0:T(2,128)S(1)}, u32[]{:S(2)}, u32[]{:S(2)}) %collective-permute-start.5) | collective-permute-done | bytes 49184 | tf_op jit(solution)/shard_map/ppermute | solution.py:821
  77.8 1.6 %slab_depth.1 = f32[48,16,128]{2,1,0:T(8,128)} custom-call(s32[8]{0:T(128)S(1)} %copy-done.1, f32[48,16,128]{2,1,0:T(8,128)S(1)} %get-tuple-element.17.rows_ref, f32[48,2,128]{2,1,0:T(2,128)S(1)} %collective-permute-done.4.first_ref, f32[48,2,128]{2,1,0:T(2,128)S(1)} %collective-permute-done.5.second_ref), custom_call_target="tpu_custom_call" | custom-call | tf_op jit(solution)/shard_map/slab_depth/pallas_call | solution.py:822
  79.4 0.0 all-to-all-done.3.halo_ref
  79.4 0.0 copy-done
  79.4 2.5 %stream_last.1 = f32[8,19,16,256]{3,2,1,0:T(8,128)} custom-call(f32[4,19,16,256]{3,2,1,0:T(8,128)S(1)} %copy-done, f32[4,19,16,256]{3,2,1,0:T(8,128)} %get-tuple-element.15.late_hbm, f32[8,64,128]{2,1,0:T(8,128)S(1)} %all-to-all-done.3.halo_ref), custom_call_target="tpu_custom_call" | custom-call | tf_op jit(solution)/shard_map/stream_last/pallas_call | solution.py:830
  (2 shorter events, 0.0 us)
Async XLA Ops:
  0.6 34.4 %copy-start.1 = (s32[8]{0:T(128)S(1)}, s32[8]{0:T(128)}, u32[]{:S(2)}) copy-start(s32[8]{0:T(128)} %owner_ref.3) | copy-start | bytes 100
  17.2 6.5 %collective-permute-start.1 = (f32[8,16,128]{2,1,0:T(8,128)S(1)}, f32[8,16,128]{2,1,0:T(8,128)S(1)}, u32[]{:S(2)}, u32[]{:S(2)}) collective-permute-start(f32[8,16,128]{2,1,0:T(8,128)S(1)} %get-tuple-element.22), channel_id=1, source_target_pairs={{0,3},{1,2},{2,1},{3,0},{4,7},{5,6},{6,5},{7,4},{8,11},{9,10},{10,... | collective-permute-start | bytes 196616 | tf_op jit(solution)/shard_map/ppermute | solution.py:756
  20.9 2.9 %collective-permute-start = (f32[8,16,128]{2,1,0:T(8,128)S(1)}, f32[8,16,128]{2,1,0:T(8,128)S(1)}, u32[]{:S(2)}, u32[]{:S(2)}) collective-permute-start(f32[8,16,128]{2,1,0:T(8,128)S(1)} %get-tuple-element.23), channel_id=1, source_target_pairs={{0,1},{1,0},{2,3},{3,2},{4,5},{5,4},{6,7},{7,6},{8,9},{9,8},{10,11... | collective-permute-start | bytes 196616 | tf_op jit(solution)/shard_map/ppermute | solution.py:755
  38.7 31.2 %copy-start.2 = (s32[1,64]{1,0:T(1,128)S(1)}, s32[1,64]{1,0:T(1,128)}, u32[]{:S(2)}) copy-start(s32[1,64]{1,0:T(1,128)} %column_ref.1) | copy-start | bytes 772
  38.7 40.7 %copy-start = (f32[4,19,16,256]{3,2,1,0:T(8,128)S(1)}, f32[4,19,16,256]{3,2,1,0:T(8,128)}, u32[]{:S(2)}) copy-start(f32[4,19,16,256]{3,2,1,0:T(8,128)} %get-tuple-element.14.near_ref) | copy-start | bytes 3735556
  60.1 5.2 %collective-permute-start.3 = (f32[8,16,128]{2,1,0:T(8,128)S(1)}, f32[8,16,128]{2,1,0:T(8,128)S(1)}, u32[]{:S(2)}, u32[]{:S(2)}) collective-permute-start(f32[8,16,128]{2,1,0:T(8,128)S(1)} %get-tuple-element.20), channel_id=1, source_target_pairs={{0,3},{1,2},{2,1},{3,0},{4,7},{5,6},{6,5},{7,4},{8,11},{9,10},{10,... | collective-permute-start | bytes 196616 | tf_op jit(solution)/shard_map/ppermute | solution.py:756
  62.9 2.4 %collective-permute-start.2 = (f32[8,16,128]{2,1,0:T(8,128)S(1)}, f32[8,16,128]{2,1,0:T(8,128)S(1)}, u32[]{:S(2)}, u32[]{:S(2)}) collective-permute-start(f32[8,16,128]{2,1,0:T(8,128)S(1)} %get-tuple-element.21), channel_id=1, source_target_pairs={{0,1},{1,0},{2,3},{3,2},{4,5},{5,4},{6,7},{7,6},{8,9},{9,8},{10,11... | collective-permute-start | bytes 196616 | tf_op jit(solution)/shard_map/ppermute | solution.py:755
  66.5 12.9 %all-to-all-start.3 = ((f32[8,64,128]{2,1,0:T(8,128)}), f32[8,64,128]{2,1,0:T(8,128)S(1)}, u32[]{:S(2)}, u32[]{:S(2)}) async-start(f32[8,64,128]{2,1,0:T(8,128)} %route.3), calls=%async_computation.3 | async-start | bytes 524288 | tf_op jit(solution)/shard_map/all_to_all | solution.py:766
  72.9 1.9 %collective-permute-start.4 = (f32[48,2,128]{2,1,0:T(2,128)S(1)}, f32[48,2,128]{2,1,0:T(2,128)S(1)}, u32[]{:S(2)}, u32[]{:S(2)}) collective-permute-start(f32[48,2,128]{2,1,0:T(2,128)S(1)} %get-tuple-element.18), channel_id=1, source_target_pairs={{0,1},{1,0},{2,3},{3,2},{4,5},{5,4},{6,7},{7,6},{8,9},{9,8},{10,11... | collective-permute-start | bytes 147464 | tf_op jit(solution)/shard_map/ppermute | solution.py:820
  74.0 3.8 %collective-permute-start.5 = (f32[48,2,128]{2,1,0:T(2,128)S(1)}, f32[48,2,128]{2,1,0:T(2,128)S(1)}, u32[]{:S(2)}, u32[]{:S(2)}) collective-permute-start(f32[48,2,128]{2,1,0:T(2,128)S(1)} %get-tuple-element.19), channel_id=1, source_target_pairs={{0,3},{1,2},{2,1},{3,0},{4,7},{5,6},{6,5},{7,4},{8,11},{9,10},{10,... | collective-permute-start | bytes 147464 | tf_op jit(solution)/shard_map/ppermute | solution.py:821

commit v9 on v8

--- a/solution.py
+++ b/solution.py
@@ -292,12 +292,98 @@
     return value
 
 
-def stream_block(source_ref, halo_ref, lines_ref, out_ref, edge):
+def shift_inside(p, source_ref, edge):
+    cx, cy, cz = VELOCITIES[p]
+    value = {(z, c): shift(part(source_ref, p, z * 8, c * 128), -(cx + edge * cy)) for z in (0, 1) for c in (0, 1)}
+    if cy != 0:
+        outer, far = (1, 7) if cy > 0 else (0, 0)
+        border = lanes((8, 128)) // edge == far
+        for z in (0, 1):
+            value[z, 1 - outer] = jnp.where(border, value[z, outer], value[z, 1 - outer])
+    return shift_depth(value, cz)
+
+
+def shift_depth(value, cz):
+    if cz == 0:
+        return value
+    outer = 1 if cz > 0 else 0
+    border = lax.broadcasted_iota(jnp.int32, (8, 128), 0) == (7 if cz > 0 else 0)
+    turned = {at: shift(tile, -cz, 0) for at, tile in value.items()}
+    return {
+        (z, c): tile if z == outer else jnp.where(border, turned[outer, c], tile) for (z, c), tile in turned.items()
+    }
+
+
+def insert_halo(p, source_ref, halo_ref, y_faces, x_faces, edge):
+    cx, cy, cz = VELOCITIES[p]
+    lane = lanes((8, 128))
+    sides, depths = (0, 1), (0, 1)
+    value = {(z, c): part(source_ref, p, z * 8, c * 128) for z in depths for c in sides}
+    if cx != 0:
+        at_face = lane % edge == (edge - 1 if cx > 0 else 0)
+        arrived = {}
+        for z in depths:
+            for c in sides:
+                spot = x_pair(p, z, c)
+                if spot not in x_faces:
+                    t, pair = spot
+                    x_faces[spot] = shift(halo_ref[t * 8 : t * 8 + 8, :], edge - 1 - 2 * pair - edge * cy)
+                arrived[z, c] = x_faces[spot]
+    if cy != 0:
+        outer, far = (1, 7) if cy > 0 else (0, 0)
+        border = lane // edge == far
+        if cx != 0:
+            for z in depths:
+                arrived[z, 1 - outer] = jnp.where(border, arrived[z, outer], arrived[z, 1 - outer])
+    if cx != 0:
+        arrived = shift_depth(arrived, cz)
+        value = {at: jnp.where(at_face, arrived[at], tile) for at, tile in value.items()}
+    if cy != 0:
+        if p in y_faces:
+            faces = y_faces[p]
+        else:
+            start = NORTH_POPS.index(p) * edge if cy > 0 else SOUTH + SOUTH_POPS.index(p) * edge
+            faces = [shift(halo_ref[at : at + 8, :], far * edge - start) for at in (Y_ROWS, Y_ROWS + 8)]
+        faces = shift_depth({(z, 0): face for z, face in enumerate(faces)}, cz)
+        for z in depths:
+            value[z, outer] = jnp.where(border, faces[z, 0], value[z, outer])
+    if cz != 0:
+        row = UPPER_POPS.index(p) if cz > 0 else LOWER_POPS.index(p)
+        last = 1 if cz > 0 else 0
+        end = lax.broadcasted_iota(jnp.int32, (8, 128), 0) == (7 if cz > 0 else 0)
+        for c in sides:
+            value[last, c] = jnp.where(end, halo_ref[halo_row(cz > 0, c * 128, row), :], value[last, c])
+    return value
+
+
+def put_tiles(ref, p, value):
+    for (z, c), tile in value.items():
+        ref[p, z * 8 : z * 8 + 8, c * 128 : c * 128 + 128] = tile
+
+
+def ahead_kernel(blocks, before_ref, gathered_ref, after_ref):
+    edge = before_ref.shape[2]
+
+    def one(b, carry):
+        source_ref, out_ref = before_ref.at[b], after_ref.at[b]
+        out_ref[POPS] = source_ref[POPS]
+        for start in range(0, POPS, STREAM_GROUP):
+            pops = STREAM_ORDER[start : start + STREAM_GROUP]
+            values = [shift_inside(p, source_ref, edge) for p in pops]
+            for p, value in zip(pops, values):
+                put_tiles(out_ref, p, value)
+        return carry
+
+    lax.fori_loop(0, blocks, one, 0)
+
+
+def stream_block(source_ref, halo_ref, lines_ref, out_ref, edge, one_pop=None):
+    one_pop = one_pop or stream_pop
     y_faces = {3: [lines_ref[0:8, :], lines_ref[8:16, :]], 4: [lines_ref[16:24, :], lines_ref[24:32, :]]}
     x_faces = {}
     for start in range(0, POPS, STREAM_GROUP):
         pops = STREAM_ORDER[start : start + STREAM_GROUP]
-        values = [stream_pop(p, source_ref, halo_ref, y_faces, x_faces, edge) for p in pops]
+        values = [one_pop(p, source_ref, halo_ref, y_faces, x_faces, edge) for p in pops]
         for p, value in zip(pops, values):
             for (z, c), tile in value.items():
                 out_ref[p, z * 8 : z * 8 + 8, c * 128 : c * 128 + 128] = tile
@@ -450,7 +536,7 @@
         return pltpu.make_async_copy(post_ref.at[b], out_hbm.at[b - first], sems.at[b])
 
     def stream(b, carry):
-        stream_block(before_ref.at[b], halo_ref.at[b], lines_ref.at[b], state_ref.at[b], edge)
+        stream_block(before_ref.at[b], halo_ref.at[b], lines_ref.at[b], state_ref.at[b], edge, insert_halo)
         return carry
 
     y_halos(blocks, halo_ref, lines_ref)
@@ -544,7 +630,8 @@
         result(b).wait()
 
 
-def route_kernel(devices, sources_ref, faces_ref, first_ref, second_ref, halo_ref, y_ref, above_ref, below_ref):
+def route_kernel(devices, sources_ref, faces_ref, first_ref, second_ref, *refs):
+    halo_ref, y_ref, above_ref, below_ref = refs[-4:]
     edge = 16
     swapped = first_partner_above()
     lane = lanes((8, 128))
@@ -751,18 +838,18 @@
     post_shape = (blocks, POPS + 1, edge, plane)
     params = pltpu.CompilerParams(vmem_limit_bytes=32 * 1024 * 1024)
 
-    def to_halo(gathered):
+    def to_halo(gathered, *others):
         first = lax.ppermute(gathered[:, FIRST : FIRST + 16], "gz", first_pairs)
         second = lax.ppermute(gathered[:, SECOND - 4 : SECOND + 12], "gz", second_pairs)
         halo = pl.pallas_call(
             functools.partial(route_kernel, devices),
             out_shape=f32(*faces_shape),
-            in_specs=[VMEM] * 4,
+            in_specs=[VMEM] * 4 + [ANY] * len(others),
             out_specs=VMEM,
             scratch_shapes=[vmem(devices, 16, 128)] * 3,
             compiler_params=params,
             name="route",
-        )(sources, gathered, first, second)
+        )(sources, gathered, first, second, *others)
         return lax.all_to_all(halo, "blk", 0, 0, tiled=True)
 
     inputs = [vmem(*state.shape), vmem(*flow.shape), vmem(*design.shape)]
@@ -786,7 +873,16 @@
         compiler_params=params,
         name="collide_first",
     )(table, state, flow, design)
-    halo = to_halo(lax.all_to_all(faces, "blk", 0, 0, tiled=True))
+    gathered = lax.all_to_all(faces, "blk", 0, 0, tiled=True)
+    post = pl.pallas_call(
+        functools.partial(ahead_kernel, blocks),
+        out_shape=vmem(*post_shape),
+        in_specs=[VMEM, ANY],
+        out_specs=VMEM,
+        compiler_params=params,
+        name="shift_inside",
+    )(post, gathered)
+    halo = to_halo(gathered, post)
     near, late, faces = pl.pallas_call(
         functools.partial(second_kernel, blocks, devices, chunks),
         out_shape=(hbm(*near_shape), hbm(*late_shape), f32(devices, FACE_ROWS + row_count, 128)),

time: 82.6 us -> 82 us (level)
  waiting for transfers between devices: 8.29 us -> 7.19 us
    all_to_all x1 -> x0, blocking collectives: 13.5 us -> none  [local(): halo = to_halo(lax.all_to_all(faces, 'blk', 0, 0, tiled=True))]
    all_to_all x1 -> x2, blocking collectives: 21.4 us -> 34.9 us  [local(): gathered = lax.all_to_all(faces, 'blk', 0, 0, tiled=True)]
    ppermute x2, waiting for transfers between devices: 5.27 us -> 4.17 us  [to_halo(): lax.ppermute(gathered[:, SECOND - 4:SECOND + 12], 'gz', second_pairs)]
    pallas_call x0 -> x1, Pallas kernels: none -> 1.08 us  [local(): pl.pallas_call(functools.partial(ahead_kernel, blocks), out_shape=vmem(*p...]
  transfers between devices with their start and end apart: 7 -> 7, of which waited for: 4 -> 4; matrix products, arithmetic and copies ran while one was open for 0% -> 0% of each run, Pallas kernels for 6% -> 7%
where the time goes in v9:
time: 82 us; the launch traced here: 81.4 us
  blocking collectives  45.7 us (56%)
  Pallas kernels  16 us (20%)
  starting transfers between devices  11.7 us (14%)
  waiting for transfers between devices  7.19 us (9%)
    all_to_all x2, blocking collectives, local(): gathered = lax.all_to_all(faces, 'blk', 0, 0, tiled=True)  34.9 us
    all_to_all x1, blocking collectives, to_halo(): return lax.all_to_all(halo, 'blk', 0, 0, tiled=True)  10.8 us
    ppermute x2, starting transfers between devices, to_halo(): lax.ppermute(gathered[:, SECOND - 4:SECOND + 12], 'gz', second_pairs)  6.49 us
    ppermute x2, waiting for transfers between devices, to_halo(): lax.ppermute(gathered[:, SECOND - 4:SECOND + 12], 'gz', second_pairs)  4.17 us
    all_to_all x1, starting transfers between devices, to_halo(): return lax.all_to_all(halo, 'blk', 0, 0, tiled=True)  3.41 us
    pallas_call x1, Pallas kernels, local(): pl.pallas_call(functools.partial(second_kernel, blocks, devices, chunks),...  3.14 us
    pallas_call x1, Pallas kernels, local(): pl.pallas_call(functools.partial(first_kernel, blocks, devices), out_shap...  3.02 us
    pallas_call x1, Pallas kernels, local(): pl.pallas_call(functools.partial(slab_kernel, blocks, devices, chunks), o...  3 us
  transfers between devices with their start and end apart: 7, of which 4 were waited for; matrix products, arithmetic and copies ran while one was open for 0% of the time, Pallas kernels for 7%

profile of v9, /device:TPU:1, one launch (start us, length us, event | category | flops | bytes accessed | tf_op | source)
XLA Modules:
  0.0 81.4 jit_solution(9597139088494974620)
XLA Ops:
  0.6 3.0 %collide_first.1 = (f32[8,20,16,256]{3,2,1,0:T(8,128)S(1)}, f32[8,64,128]{2,1,0:T(8,128)S(1)}, s32[8,16,128]{2,1,0:T(8,128)S(1)}) custom-call(s32[6,1,64]{2,1,0:T(1,128)} %bitcast.13, f32[8,19,16,256]{3,2,1,0:T(8,128)} %bitcast.7, f32[8,3,16,256]{3,2,1,0:T(8,128)} %bitcast.8, f32[8,16,256]{2,1,0:T(8,128)} %bitcast.10), custom_call_target="tpu_custom_call" | custom-call | tf_op jit(solution)/shard_map/collide_first/pallas_call | solution.py:856
  3.7 13.5 %all_to_all.20.gathered_ref.faces_ref = f32[8,64,128]{2,1,0:T(8,128)S(1)} all-to-all(f32[8,64,128]{2,1,0:T(8,128)S(1)} %get-tuple-element.12), channel_id=1, replica_groups=mesh['blk'=8,'gz'=4] {'blk'}, dimensions={0} | all-to-all | bytes 524288 | tf_op jit(solution)/shard_map/all_to_all | solution.py:876
  17.2 3.7 %collective-permute-start.1 = (f32[8,16,128]{2,1,0:T(8,128)S(1)}, f32[8,16,128]{2,1,0:T(8,128)S(1)}, u32[]{:S(2)}, u32[]{:S(2)}) collective-permute-start(f32[8,16,128]{2,1,0:T(8,128)S(1)} %get-tuple-element.22), channel_id=1, source_target_pairs={{0,3},{1,2},{2,1},{3,0},{4,7},{5,6},{6,5},{7,4},{8,11},{9,10},{10,... | collective-permute-start | bytes 196616 | tf_op jit(solution)/shard_map/ppermute | solution.py:843
  20.9 0.0 collective-permute-start
  20.9 1.1 %shift_inside.1.refs_0_.before_ref = f32[8,20,16,256]{3,2,1,0:T(8,128)S(1)} custom-call(f32[8,20,16,256]{3,2,1,0:T(8,128)S(1)} %get-tuple-element.11.before_ref, f32[8,64,128]{2,1,0:T(8,128)S(1)} %all_to_all.20.gathered_ref.faces_ref), custom_call_target="tpu_custom_call" | custom-call | tf_op jit(solution)/shard_map/shift_inside/pallas_call | solution.py:877
  22.0 0.0 copy-start.1
  22.0 1.7 %collective-permute-done.1.second_ref = f32[8,16,128]{2,1,0:T(8,128)S(1)} collective-permute-done((f32[8,16,128]{2,1,0:T(8,128)S(1)}, f32[8,16,128]{2,1,0:T(8,128)S(1)}, u32[]{:S(2)}, u32[]{:S(2)}) %collective-permute-start.1) | collective-permute-done | bytes 65568 | tf_op jit(solution)/shard_map/ppermute | solution.py:843
  23.7 0.0 collective-permute-done.first_ref
  23.7 0.5 route.2
  24.2 10.8 %all_to_all.21.halo_ref = f32[8,64,128]{2,1,0:T(8,128)S(1)} all-to-all(f32[8,64,128]{2,1,0:T(8,128)S(1)} %route.2), channel_id=1, replica_groups=mesh['blk'=8,'gz'=4] {'blk'}, dimensions={0} | all-to-all | bytes 524288 | tf_op jit(solution)/shard_map/all_to_all | solution.py:853
  35.0 0.0 copy-done.1
  35.0 3.1 %stream_collide.1 = (f32[4,19,16,256]{3,2,1,0:T(8,128)}, f32[4,19,16,256]{3,2,1,0:T(8,128)}, f32[8,168,128]{2,1,0:T(8,128)S(1)}) custom-call(s32[8]{0:T(128)S(1)} %copy-done.1, f32[8,20,16,256]{3,2,1,0:T(8,128)S(1)} %shift_inside.1.refs_0_.before_ref, f32[8,3,16,256]{3,2,1,0:T(8,128)} %bitcast.9, f32[8,16,256]{2,1,0:T(8,128)} %bitcast.11, ...), custom_call_target="tpu_custom_call" | custom-call | tf_op jit(solution)/shard_map/stream_collide/pallas_call | solution.py:886
  38.2 0.0 copy-start.2
  38.2 0.0 copy-start
  38.2 21.4 %all_to_all.22.faces_ref.rows_ref = f32[8,168,128]{2,1,0:T(8,128)S(1)} all-to-all(f32[8,168,128]{2,1,0:T(8,128)S(1)} %get-tuple-element.16), channel_id=1, replica_groups=mesh['blk'=8,'gz'=4] {'blk'}, dimensions={0} | all-to-all | bytes 1376256 | tf_op jit(solution)/shard_map/all_to_all | solution.py:904
  59.5 2.8 %collective-permute-start.3 = (f32[8,16,128]{2,1,0:T(8,128)S(1)}, f32[8,16,128]{2,1,0:T(8,128)S(1)}, u32[]{:S(2)}, u32[]{:S(2)}) collective-permute-start(f32[8,16,128]{2,1,0:T(8,128)S(1)} %get-tuple-element.20), channel_id=1, source_target_pairs={{0,3},{1,2},{2,1},{3,0},{4,7},{5,6},{6,5},{7,4},{8,11},{9,10},{10,... | collective-permute-start | bytes 196616 | tf_op jit(solution)/shard_map/ppermute | solution.py:843
  62.4 0.0 collective-permute-start.2
  62.4 2.4 %collective-permute-done.3.second_ref = f32[8,16,128]{2,1,0:T(8,128)S(1)} collective-permute-done((f32[8,16,128]{2,1,0:T(8,128)S(1)}, f32[8,16,128]{2,1,0:T(8,128)S(1)}, u32[]{:S(2)}, u32[]{:S(2)}) %collective-permute-start.3) | collective-permute-done | bytes 65568 | tf_op jit(solution)/shard_map/ppermute | solution.py:843
  64.8 0.0 collective-permute-done.2.first_ref
  64.8 1.2 %route.3 = f32[8,64,128]{2,1,0:T(8,128)} custom-call(s32[8,16,128]{2,1,0:T(8,128)S(1)} %get-tuple-element.13.sources_ref, f32[8,168,128]{2,1,0:T(8,128)S(1)} %all_to_all.22.faces_ref.rows_ref, f32[8,16,128]{2,1,0:T(8,128)S(1)} %collective-permute-done.2.first_ref, f32[8,16,128]{2,1,0:T(8,128)S(1)} %collective-permute-done.3.second_ref), custom_call_target="tpu_custom_call" | custom-call | tf_op jit(solution)/shard_map/route/pallas_call | solution.py:844
  66.0 3.4 %all-to-all-start.3 = ((f32[8,64,128]{2,1,0:T(8,128)}), f32[8,64,128]{2,1,0:T(8,128)S(1)}, u32[]{:S(2)}, u32[]{:S(2)}) async-start(f32[8,64,128]{2,1,0:T(8,128)} %route.3), calls=%async_computation.3 | async-start | bytes 524288 | tf_op jit(solution)/shard_map/all_to_all | solution.py:853
  69.4 0.0 copy-done.2
  69.4 3.0 %slab_rows.1 = (f32[48,16,128]{2,1,0:T(8,128)S(1)}, f32[48,2,128]{2,1,0:T(2,128)S(1)}, f32[48,2,128]{2,1,0:T(2,128)S(1)}) custom-call(s32[8]{0:T(128)S(1)} %copy-done.1, s32[1,64]{1,0:T(1,128)S(1)} %copy-done.2, f32[8,168,128]{2,1,0:T(8,128)S(1)} %all_to_all.22.faces_ref.rows_ref), custom_call_target="tpu_custom_call" | custom-call | tf_op jit(solution)/shard_map/slab_rows/pallas_call | solution.py:907
  72.4 1.0 %collective-permute-start.4 = (f32[48,2,128]{2,1,0:T(2,128)S(1)}, f32[48,2,128]{2,1,0:T(2,128)S(1)}, u32[]{:S(2)}, u32[]{:S(2)}) collective-permute-start(f32[48,2,128]{2,1,0:T(2,128)S(1)} %get-tuple-element.18), channel_id=1, source_target_pairs={{0,1},{1,0},{2,3},{3,2},{4,5},{5,4},{6,7},{7,6},{8,9},{9,8},{10,11... | collective-permute-start | bytes 147464 | tf_op jit(solution)/shard_map/ppermute | solution.py:916
  73.4 0.8 collective-permute-start.5
  74.2 0.1 collective-permute-done.4.first_ref
  74.3 2.9 %collective-permute-done.5.second_ref = f32[48,2,128]{2,1,0:T(2,128)S(1)} collective-permute-done((f32[48,2,128]{2,1,0:T(2,128)S(1)}, f32[48,2,128]{2,1,0:T(2,128)S(1)}, u32[]{:S(2)}, u32[]{:S(2)}) %collective-permute-start.5) | collective-permute-done | bytes 49184 | tf_op jit(solution)/shard_map/ppermute | solution.py:917
  77.2 1.6 %slab_depth.1 = f32[48,16,128]{2,1,0:T(8,128)} custom-call(s32[8]{0:T(128)S(1)} %copy-done.1, f32[48,16,128]{2,1,0:T(8,128)S(1)} %get-tuple-element.17.rows_ref, f32[48,2,128]{2,1,0:T(2,128)S(1)} %collective-permute-done.4.first_ref, f32[48,2,128]{2,1,0:T(2,128)S(1)} %collective-permute-done.5.second_ref), custom_call_target="tpu_custom_call" | custom-call | tf_op jit(solution)/shard_map/slab_depth/pallas_call | solution.py:918
  78.9 0.0 all-to-all-done.3.halo_ref
  78.9 0.0 copy-done
  78.9 2.5 %stream_last.1 = f32[8,19,16,256]{3,2,1,0:T(8,128)} custom-call(f32[4,19,16,256]{3,2,1,0:T(8,128)S(1)} %copy-done, f32[4,19,16,256]{3,2,1,0:T(8,128)} %get-tuple-element.15.late_hbm, f32[8,64,128]{2,1,0:T(8,128)S(1)} %all-to-all-done.3.halo_ref), custom_call_target="tpu_custom_call" | custom-call | tf_op jit(solution)/shard_map/stream_last/pallas_call | solution.py:926
  (2 shorter events, 0.0 us)
Async XLA Ops:
  17.2 6.5 %collective-permute-start.1 = (f32[8,16,128]{2,1,0:T(8,128)S(1)}, f32[8,16,128]{2,1,0:T(8,128)S(1)}, u32[]{:S(2)}, u32[]{:S(2)}) collective-permute-start(f32[8,16,128]{2,1,0:T(8,128)S(1)} %get-tuple-element.22), channel_id=1, source_target_pairs={{0,3},{1,2},{2,1},{3,0},{4,7},{5,6},{6,5},{7,4},{8,11},{9,10},{10,... | collective-permute-start | bytes 196616 | tf_op jit(solution)/shard_map/ppermute | solution.py:843
  20.9 2.9 %collective-permute-start = (f32[8,16,128]{2,1,0:T(8,128)S(1)}, f32[8,16,128]{2,1,0:T(8,128)S(1)}, u32[]{:S(2)}, u32[]{:S(2)}) collective-permute-start(f32[8,16,128]{2,1,0:T(8,128)S(1)} %get-tuple-element.23), channel_id=1, source_target_pairs={{0,1},{1,0},{2,3},{3,2},{4,5},{5,4},{6,7},{7,6},{8,9},{9,8},{10,11... | collective-permute-start | bytes 196616 | tf_op jit(solution)/shard_map/ppermute | solution.py:842
  22.0 13.0 %copy-start.1 = (s32[8]{0:T(128)S(1)}, s32[8]{0:T(128)}, u32[]{:S(2)}) copy-start(s32[8]{0:T(128)} %owner_ref.3) | copy-start | bytes 100
  38.2 31.2 %copy-start.2 = (s32[1,64]{1,0:T(1,128)S(1)}, s32[1,64]{1,0:T(1,128)}, u32[]{:S(2)}) copy-start(s32[1,64]{1,0:T(1,128)} %column_ref.1) | copy-start | bytes 772
  38.2 40.7 %copy-start = (f32[4,19,16,256]{3,2,1,0:T(8,128)S(1)}, f32[4,19,16,256]{3,2,1,0:T(8,128)}, u32[]{:S(2)}) copy-start(f32[4,19,16,256]{3,2,1,0:T(8,128)} %get-tuple-element.14.near_ref) | copy-start | bytes 3735556
  59.5 5.2 %collective-permute-start.3 = (f32[8,16,128]{2,1,0:T(8,128)S(1)}, f32[8,16,128]{2,1,0:T(8,128)S(1)}, u32[]{:S(2)}, u32[]{:S(2)}) collective-permute-start(f32[8,16,128]{2,1,0:T(8,128)S(1)} %get-tuple-element.20), channel_id=1, source_target_pairs={{0,3},{1,2},{2,1},{3,0},{4,7},{5,6},{6,5},{7,4},{8,11},{9,10},{10,... | collective-permute-start | bytes 196616 | tf_op jit(solution)/shard_map/ppermute | solution.py:843
  62.4 2.4 %collective-permute-start.2 = (f32[8,16,128]{2,1,0:T(8,128)S(1)}, f32[8,16,128]{2,1,0:T(8,128)S(1)}, u32[]{:S(2)}, u32[]{:S(2)}) collective-permute-start(f32[8,16,128]{2,1,0:T(8,128)S(1)} %get-tuple-element.21), channel_id=1, source_target_pairs={{0,1},{1,0},{2,3},{3,2},{4,5},{5,4},{6,7},{7,6},{8,9},{9,8},{10,11... | collective-permute-start | bytes 196616 | tf_op jit(solution)/shard_map/ppermute | solution.py:842
  66.0 12.9 %all-to-all-start.3 = ((f32[8,64,128]{2,1,0:T(8,128)}), f32[8,64,128]{2,1,0:T(8,128)S(1)}, u32[]{:S(2)}, u32[]{:S(2)}) async-start(f32[8,64,128]{2,1,0:T(8,128)} %route.3), calls=%async_computation.3 | async-start | bytes 524288 | tf_op jit(solution)/shard_map/all_to_all | solution.py:853
  72.4 1.9 %collective-permute-start.4 = (f32[48,2,128]{2,1,0:T(2,128)S(1)}, f32[48,2,128]{2,1,0:T(2,128)S(1)}, u32[]{:S(2)}, u32[]{:S(2)}) collective-permute-start(f32[48,2,128]{2,1,0:T(2,128)S(1)} %get-tuple-element.18), channel_id=1, source_target_pairs={{0,1},{1,0},{2,3},{3,2},{4,5},{5,4},{6,7},{7,6},{8,9},{9,8},{10,11... | collective-permute-start | bytes 147464 | tf_op jit(solution)/shard_map/ppermute | solution.py:916
  73.4 3.8 %collective-permute-start.5 = (f32[48,2,128]{2,1,0:T(2,128)S(1)}, f32[48,2,128]{2,1,0:T(2,128)S(1)}, u32[]{:S(2)}, u32[]{:S(2)}) collective-permute-start(f32[48,2,128]{2,1,0:T(2,128)S(1)} %get-tuple-element.19), channel_id=1, source_target_pairs={{0,3},{1,2},{2,1},{3,0},{4,7},{5,6},{6,5},{7,4},{8,11},{9,10},{10,... | collective-permute-start | bytes 147464 | tf_op jit(solution)/shard_map/ppermute | solution.py:917

commit v10 on v9

--- a/solution.py
+++ b/solution.py
@@ -366,7 +366,8 @@
 
     def one(b, carry):
         source_ref, out_ref = before_ref.at[b], after_ref.at[b]
-        out_ref[POPS] = source_ref[POPS]
+        if before_ref.shape[1] > POPS:
+            out_ref[POPS] = source_ref[POPS]
         for start in range(0, POPS, STREAM_GROUP):
             pops = STREAM_ORDER[start : start + STREAM_GROUP]
             values = [shift_inside(p, source_ref, edge) for p in pops]
@@ -610,17 +611,17 @@
     for b in range(half, blocks):
         late(b).start()
 
-    def one(b, before_ref):
-        stream_block(before_ref, halo_ref.at[b], lines_ref.at[b], out_ref.at[b], edge)
+    def one(b, before_ref, one_pop):
+        stream_block(before_ref, halo_ref.at[b], lines_ref.at[b], out_ref.at[b], edge, one_pop)
         result(b).start()
 
     def near_one(b, carry):
-        one(b, near_ref.at[b])
+        one(b, near_ref.at[b], insert_halo)
         return carry
 
     def late_one(b, carry):
         late(b).wait()
-        one(b, late_ref.at[b - half])
+        one(b, late_ref.at[b - half], stream_pop)
         return carry
 
     y_halos(blocks, halo_ref, lines_ref)
@@ -852,6 +853,16 @@
         )(sources, gathered, first, second, *others)
         return lax.all_to_all(halo, "blk", 0, 0, tiled=True)
 
+    def ahead(before, gathered):
+        return pl.pallas_call(
+            functools.partial(ahead_kernel, before.shape[0]),
+            out_shape=vmem(*before.shape),
+            in_specs=[VMEM, ANY],
+            out_specs=VMEM,
+            compiler_params=params,
+            name="shift_inside",
+        )(before, gathered)
+
     inputs = [vmem(*state.shape), vmem(*flow.shape), vmem(*design.shape)]
     post, faces, sources = pl.pallas_call(
         functools.partial(first_kernel, blocks, devices),
@@ -874,14 +885,7 @@
         name="collide_first",
     )(table, state, flow, design)
     gathered = lax.all_to_all(faces, "blk", 0, 0, tiled=True)
-    post = pl.pallas_call(
-        functools.partial(ahead_kernel, blocks),
-        out_shape=vmem(*post_shape),
-        in_specs=[VMEM, ANY],
-        out_specs=VMEM,
-        compiler_params=params,
-        name="shift_inside",
-    )(post, gathered)
+    post = ahead(post, gathered)
     halo = to_halo(gathered, post)
     near, late, faces = pl.pallas_call(
         functools.partial(second_kernel, blocks, devices, chunks),
@@ -902,7 +906,8 @@
         name="stream_collide",
     )(owner_map, post, flow, design, halo)
     gathered = lax.all_to_all(faces, "blk", 0, 0, tiled=True)
-    halo = to_halo(gathered)
+    near = ahead(near, gathered)
+    halo = to_halo(gathered, near)
     slab_shape, ends = (rows_cap, edge, width), (rows_cap, 2, width)
     slab, first, second = pl.pallas_call(
         functools.partial(slab_kernel, blocks, devices, chunks),

time: 82 us -> 82 us (level)
  transfers between devices with their start and end apart: 7 -> 7, of which waited for: 4 -> 4; matrix products, arithmetic and copies ran while one was open for 0% -> 0% of each run, Pallas kernels for 7% -> 8%
where the time goes in v10:
time: 82 us; the launch traced here: 81.4 us
  blocking collectives  45.7 us (56%)
  Pallas kernels  16.5 us (20%)
  starting transfers between devices  11.7 us (14%)
  waiting for transfers between devices  6.64 us (8%)
    all_to_all x2, blocking collectives, local(): gathered = lax.all_to_all(faces, 'blk', 0, 0, tiled=True)  34.9 us
    all_to_all x1, blocking collectives, to_halo(): return lax.all_to_all(halo, 'blk', 0, 0, tiled=True)  10.8 us
    ppermute x2, starting transfers between devices, to_halo(): lax.ppermute(gathered[:, SECOND - 4:SECOND + 12], 'gz', second_pairs)  6.49 us
    ppermute x2, waiting for transfers between devices, to_halo(): lax.ppermute(gathered[:, SECOND - 4:SECOND + 12], 'gz', second_pairs)  3.62 us
    all_to_all x1, starting transfers between devices, to_halo(): return lax.all_to_all(halo, 'blk', 0, 0, tiled=True)  3.41 us
    pallas_call x1, Pallas kernels, local(): pl.pallas_call(functools.partial(second_kernel, blocks, devices, chunks),...  3.14 us
    pallas_call x1, Pallas kernels, local(): pl.pallas_call(functools.partial(first_kernel, blocks, devices), out_shap...  3.02 us
    pallas_call x1, Pallas kernels, local(): pl.pallas_call(functools.partial(slab_kernel, blocks, devices, chunks), o...  3 us
  transfers between devices with their start and end apart: 7, of which 4 were waited for; matrix products, arithmetic and copies ran while one was open for 0% of the time, Pallas kernels for 8%

profile of v10, /device:TPU:1, one launch (start us, length us, event | category | flops | bytes accessed | tf_op | source)
XLA Modules:
  0.0 81.4 jit_solution(2208021447081613660)
XLA Ops:
  0.6 3.0 %collide_first.1 = (f32[8,20,16,256]{3,2,1,0:T(8,128)S(1)}, f32[8,64,128]{2,1,0:T(8,128)S(1)}, s32[8,16,128]{2,1,0:T(8,128)S(1)}) custom-call(s32[6,1,64]{2,1,0:T(1,128)} %bitcast.13, f32[8,19,16,256]{3,2,1,0:T(8,128)} %bitcast.7, f32[8,3,16,256]{3,2,1,0:T(8,128)} %bitcast.8, f32[8,16,256]{2,1,0:T(8,128)} %bitcast.10), custom_call_target="tpu_custom_call" | custom-call | tf_op jit(solution)/shard_map/collide_first/pallas_call | solution.py:867
  3.7 13.5 %all_to_all.20.gathered_ref.faces_ref = f32[8,64,128]{2,1,0:T(8,128)S(1)} all-to-all(f32[8,64,128]{2,1,0:T(8,128)S(1)} %get-tuple-element.12), channel_id=1, replica_groups=mesh['blk'=8,'gz'=4] {'blk'}, dimensions={0} | all-to-all | bytes 524288 | tf_op jit(solution)/shard_map/all_to_all | solution.py:887
  17.2 3.7 %collective-permute-start.1 = (f32[8,16,128]{2,1,0:T(8,128)S(1)}, f32[8,16,128]{2,1,0:T(8,128)S(1)}, u32[]{:S(2)}, u32[]{:S(2)}) collective-permute-start(f32[8,16,128]{2,1,0:T(8,128)S(1)} %get-tuple-element.22), channel_id=1, source_target_pairs={{0,3},{1,2},{2,1},{3,0},{4,7},{5,6},{6,5},{7,4},{8,11},{9,10},{10,... | collective-permute-start | bytes 196616 | tf_op jit(solution)/shard_map/ppermute | solution.py:844
  20.9 0.0 collective-permute-start
  20.9 1.1 %shift_inside.2.refs_0_.before_ref = f32[8,20,16,256]{3,2,1,0:T(8,128)S(1)} custom-call(f32[8,20,16,256]{3,2,1,0:T(8,128)S(1)} %get-tuple-element.11.before_ref, f32[8,64,128]{2,1,0:T(8,128)S(1)} %all_to_all.20.gathered_ref.faces_ref), custom_call_target="tpu_custom_call" | custom-call | tf_op jit(solution)/shard_map/shift_inside/pallas_call | solution.py:857
  22.0 0.0 copy-start.1
  22.0 1.7 %collective-permute-done.1.second_ref = f32[8,16,128]{2,1,0:T(8,128)S(1)} collective-permute-done((f32[8,16,128]{2,1,0:T(8,128)S(1)}, f32[8,16,128]{2,1,0:T(8,128)S(1)}, u32[]{:S(2)}, u32[]{:S(2)}) %collective-permute-start.1) | collective-permute-done | bytes 65568 | tf_op jit(solution)/shard_map/ppermute | solution.py:844
  23.7 0.0 collective-permute-done.first_ref
  23.7 0.5 route.2
  24.2 10.8 %all_to_all.21.halo_ref = f32[8,64,128]{2,1,0:T(8,128)S(1)} all-to-all(f32[8,64,128]{2,1,0:T(8,128)S(1)} %route.2), channel_id=1, replica_groups=mesh['blk'=8,'gz'=4] {'blk'}, dimensions={0} | all-to-all | bytes 524288 | tf_op jit(solution)/shard_map/all_to_all | solution.py:854
  35.0 0.0 copy-done.1
  35.0 3.1 %stream_collide.1 = (f32[4,19,16,256]{3,2,1,0:T(8,128)}, f32[4,19,16,256]{3,2,1,0:T(8,128)}, f32[8,168,128]{2,1,0:T(8,128)S(1)}) custom-call(s32[8]{0:T(128)S(1)} %copy-done.1, f32[8,20,16,256]{3,2,1,0:T(8,128)S(1)} %shift_inside.2.refs_0_.before_ref, f32[8,3,16,256]{3,2,1,0:T(8,128)} %bitcast.9, f32[8,16,256]{2,1,0:T(8,128)} %bitcast.11, ...), custom_call_target="tpu_custom_call" | custom-call | tf_op jit(solution)/shard_map/stream_collide/pallas_call | solution.py:890
  38.2 0.0 copy-start
  38.2 21.4 %all_to_all.22.gathered_ref.faces_ref.rows_ref = f32[8,168,128]{2,1,0:T(8,128)S(1)} all-to-all(f32[8,168,128]{2,1,0:T(8,128)S(1)} %get-tuple-element.15), channel_id=1, replica_groups=mesh['blk'=8,'gz'=4] {'blk'}, dimensions={0} | all-to-all | bytes 1376256 | tf_op jit(solution)/shard_map/all_to_all | solution.py:908
  59.5 2.8 %collective-permute-start.3 = (f32[8,16,128]{2,1,0:T(8,128)S(1)}, f32[8,16,128]{2,1,0:T(8,128)S(1)}, u32[]{:S(2)}, u32[]{:S(2)}) collective-permute-start(f32[8,16,128]{2,1,0:T(8,128)S(1)} %get-tuple-element.20), channel_id=1, source_target_pairs={{0,3},{1,2},{2,1},{3,0},{4,7},{5,6},{6,5},{7,4},{8,11},{9,10},{10,... | collective-permute-start | bytes 196616 | tf_op jit(solution)/shard_map/ppermute | solution.py:844
  62.4 0.0 collective-permute-start.2
  62.4 0.0 copy-done
  62.4 0.0 copy-start.2
  62.4 0.5 shift_inside.3.refs_0_.near_ref
  62.9 1.9 %collective-permute-done.3.second_ref = f32[8,16,128]{2,1,0:T(8,128)S(1)} collective-permute-done((f32[8,16,128]{2,1,0:T(8,128)S(1)}, f32[8,16,128]{2,1,0:T(8,128)S(1)}, u32[]{:S(2)}, u32[]{:S(2)}) %collective-permute-start.3) | collective-permute-done | bytes 65568 | tf_op jit(solution)/shard_map/ppermute | solution.py:844
  64.8 0.0 collective-permute-done.2.first_ref
  64.8 1.2 %route.3 = f32[8,64,128]{2,1,0:T(8,128)} custom-call(s32[8,16,128]{2,1,0:T(8,128)S(1)} %get-tuple-element.13.sources_ref, f32[8,168,128]{2,1,0:T(8,128)S(1)} %all_to_all.22.gathered_ref.faces_ref.rows_ref, f32[8,16,128]{2,1,0:T(8,128)S(1)} %collective-permute-done.2.first_ref, f32[8,16,128]{2,1,0:T(8,128)S(1)} %collective-permute-done.3.second_ref, ...), custom_call_target="tpu_custom_call" | custom-call | tf_op jit(solution)/shard_map/route/pallas_call | solution.py:845
  66.0 3.4 %all-to-all-start.3 = ((f32[8,64,128]{2,1,0:T(8,128)}), f32[8,64,128]{2,1,0:T(8,128)S(1)}, u32[]{:S(2)}, u32[]{:S(2)}) async-start(f32[8,64,128]{2,1,0:T(8,128)} %route.3), calls=%async_computation.3 | async-start | bytes 524288 | tf_op jit(solution)/shard_map/all_to_all | solution.py:854
  69.4 0.0 copy-done.2
  69.4 3.0 %slab_rows.1 = (f32[48,16,128]{2,1,0:T(8,128)S(1)}, f32[48,2,128]{2,1,0:T(2,128)S(1)}, f32[48,2,128]{2,1,0:T(2,128)S(1)}) custom-call(s32[8]{0:T(128)S(1)} %copy-done.1, s32[1,64]{1,0:T(1,128)S(1)} %copy-done.2, f32[8,168,128]{2,1,0:T(8,128)S(1)} %all_to_all.22.gathered_ref.faces_ref.rows_ref), custom_call_target="tpu_custom_call" | custom-call | tf_op jit(solution)/shard_map/slab_rows/pallas_call | solution.py:912
  72.4 1.0 %collective-permute-start.4 = (f32[48,2,128]{2,1,0:T(2,128)S(1)}, f32[48,2,128]{2,1,0:T(2,128)S(1)}, u32[]{:S(2)}, u32[]{:S(2)}) collective-permute-start(f32[48,2,128]{2,1,0:T(2,128)S(1)} %get-tuple-element.18), channel_id=1, source_target_pairs={{0,1},{1,0},{2,3},{3,2},{4,5},{5,4},{6,7},{7,6},{8,9},{9,8},{10,11... | collective-permute-start | bytes 147464 | tf_op jit(solution)/shard_map/ppermute | solution.py:921
  73.4 0.8 collective-permute-start.5
  74.2 0.1 collective-permute-done.4.first_ref
  74.3 2.9 %collective-permute-done.5.second_ref = f32[48,2,128]{2,1,0:T(2,128)S(1)} collective-permute-done((f32[48,2,128]{2,1,0:T(2,128)S(1)}, f32[48,2,128]{2,1,0:T(2,128)S(1)}, u32[]{:S(2)}, u32[]{:S(2)}) %collective-permute-start.5) | collective-permute-done | bytes 49184 | tf_op jit(solution)/shard_map/ppermute | solution.py:922
  77.2 1.6 %slab_depth.1 = f32[48,16,128]{2,1,0:T(8,128)} custom-call(s32[8]{0:T(128)S(1)} %copy-done.1, f32[48,16,128]{2,1,0:T(8,128)S(1)} %get-tuple-element.17.rows_ref, f32[48,2,128]{2,1,0:T(2,128)S(1)} %collective-permute-done.4.first_ref, f32[48,2,128]{2,1,0:T(2,128)S(1)} %collective-permute-done.5.second_ref), custom_call_target="tpu_custom_call" | custom-call | tf_op jit(solution)/shard_map/slab_depth/pallas_call | solution.py:923
  78.9 0.0 all-to-all-done.3.halo_ref
  78.9 2.5 %stream_last.1 = f32[8,19,16,256]{3,2,1,0:T(8,128)} custom-call(f32[4,19,16,256]{3,2,1,0:T(8,128)S(1)} %shift_inside.3.refs_0_.near_ref, f32[4,19,16,256]{3,2,1,0:T(8,128)} %get-tuple-element.16.late_hbm, f32[8,64,128]{2,1,0:T(8,128)S(1)} %all-to-all-done.3.halo_ref), custom_call_target="tpu_custom_call" | custom-call | tf_op jit(solution)/shard_map/stream_last/pallas_call | solution.py:931
  (2 shorter events, 0.0 us)
Async XLA Ops:
  17.2 6.5 %collective-permute-start.1 = (f32[8,16,128]{2,1,0:T(8,128)S(1)}, f32[8,16,128]{2,1,0:T(8,128)S(1)}, u32[]{:S(2)}, u32[]{:S(2)}) collective-permute-start(f32[8,16,128]{2,1,0:T(8,128)S(1)} %get-tuple-element.22), channel_id=1, source_target_pairs={{0,3},{1,2},{2,1},{3,0},{4,7},{5,6},{6,5},{7,4},{8,11},{9,10},{10,... | collective-permute-start | bytes 196616 | tf_op jit(solution)/shard_map/ppermute | solution.py:844
  20.9 2.9 %collective-permute-start = (f32[8,16,128]{2,1,0:T(8,128)S(1)}, f32[8,16,128]{2,1,0:T(8,128)S(1)}, u32[]{:S(2)}, u32[]{:S(2)}) collective-permute-start(f32[8,16,128]{2,1,0:T(8,128)S(1)} %get-tuple-element.23), channel_id=1, source_target_pairs={{0,1},{1,0},{2,3},{3,2},{4,5},{5,4},{6,7},{7,6},{8,9},{9,8},{10,11... | collective-permute-start | bytes 196616 | tf_op jit(solution)/shard_map/ppermute | solution.py:843
  22.0 13.0 %copy-start.1 = (s32[8]{0:T(128)S(1)}, s32[8]{0:T(128)}, u32[]{:S(2)}) copy-start(s32[8]{0:T(128)} %owner_ref.3) | copy-start | bytes 100
  38.2 24.2 %copy-start = (f32[4,19,16,256]{3,2,1,0:T(8,128)S(1)}, f32[4,19,16,256]{3,2,1,0:T(8,128)}, u32[]{:S(2)}) copy-start(f32[4,19,16,256]{3,2,1,0:T(8,128)} %get-tuple-element.14.before_ref) | copy-start | bytes 3735556
  59.5 5.2 %collective-permute-start.3 = (f32[8,16,128]{2,1,0:T(8,128)S(1)}, f32[8,16,128]{2,1,0:T(8,128)S(1)}, u32[]{:S(2)}, u32[]{:S(2)}) collective-permute-start(f32[8,16,128]{2,1,0:T(8,128)S(1)} %get-tuple-element.20), channel_id=1, source_target_pairs={{0,3},{1,2},{2,1},{3,0},{4,7},{5,6},{6,5},{7,4},{8,11},{9,10},{10,... | collective-permute-start | bytes 196616 | tf_op jit(solution)/shard_map/ppermute | solution.py:844
  62.4 2.4 %collective-permute-start.2 = (f32[8,16,128]{2,1,0:T(8,128)S(1)}, f32[8,16,128]{2,1,0:T(8,128)S(1)}, u32[]{:S(2)}, u32[]{:S(2)}) collective-permute-start(f32[8,16,128]{2,1,0:T(8,128)S(1)} %get-tuple-element.21), channel_id=1, source_target_pairs={{0,1},{1,0},{2,3},{3,2},{4,5},{5,4},{6,7},{7,6},{8,9},{9,8},{10,11... | collective-permute-start | bytes 196616 | tf_op jit(solution)/shard_map/ppermute | solution.py:843
  62.4 7.0 %copy-start.2 = (s32[1,64]{1,0:T(1,128)S(1)}, s32[1,64]{1,0:T(1,128)}, u32[]{:S(2)}) copy-start(s32[1,64]{1,0:T(1,128)} %column_ref.1) | copy-start | bytes 772
  66.0 12.9 %all-to-all-start.3 = ((f32[8,64,128]{2,1,0:T(8,128)}), f32[8,64,128]{2,1,0:T(8,128)S(1)}, u32[]{:S(2)}, u32[]{:S(2)}) async-start(f32[8,64,128]{2,1,0:T(8,128)} %route.3), calls=%async_computation.3 | async-start | bytes 524288 | tf_op jit(solution)/shard_map/all_to_all | solution.py:854
  72.4 1.9 %collective-permute-start.4 = (f32[48,2,128]{2,1,0:T(2,128)S(1)}, f32[48,2,128]{2,1,0:T(2,128)S(1)}, u32[]{:S(2)}, u32[]{:S(2)}) collective-permute-start(f32[48,2,128]{2,1,0:T(2,128)S(1)} %get-tuple-element.18), channel_id=1, source_target_pairs={{0,1},{1,0},{2,3},{3,2},{4,5},{5,4},{6,7},{7,6},{8,9},{9,8},{10,11... | collective-permute-start | bytes 147464 | tf_op jit(solution)/shard_map/ppermute | solution.py:921
  73.4 3.8 %collective-permute-start.5 = (f32[48,2,128]{2,1,0:T(2,128)S(1)}, f32[48,2,128]{2,1,0:T(2,128)S(1)}, u32[]{:S(2)}, u32[]{:S(2)}) collective-permute-start(f32[48,2,128]{2,1,0:T(2,128)S(1)} %get-tuple-element.19), channel_id=1, source_target_pairs={{0,3},{1,2},{2,1},{3,0},{4,7},{5,6},{6,5},{7,4},{8,11},{9,10},{10,... | collective-permute-start | bytes 147464 | tf_op jit(solution)/shard_map/ppermute | solution.py:922
